TPU v7x, 32 devices: a whole 2x2x4 slice. The times are simulated.
32 devices in a mesh: blk: 8 (over z, y), rows: 4 (over x, core).
Axes of the slice: x: 2, y: 2, z: 4, core: 2. Of those that a mesh axis runs over, the one named last changes fastest.
Arguments:
- start_block: float32 [64, 16384], P(None, ('rows', 'blk')), may hold values from -110 to 110, as said below
- tile_vals: float32 [2048, 128, 128], P(('rows', 'blk')), may hold values from 0 to 1, as said below
- tile_rows: int32 [2048], P(('rows', 'blk')), may hold values from 0 to 127, as said below
- tile_cols: int32 [2048], P(('rows', 'blk')), may hold values from 0 to 127, as said below
- tile_count: int32 [4, 8], P('rows', 'blk'), may hold values from 4 to 64, as said below
Outputs:
- spectral_basis: float32 [64, 16384], P(None, ('rows', 'blk'))
Inputs may be any that keep to these rules, and one draw needn't show every extreme that they name: `start_block`: entries are finite. `tile_vals`: most entries are zero. In a slot s < 4 of a device every entry with |a - c| = 1 is positive. `tile_rows`: slot s < 4 of the device with blk index b in row group g has block row g * 32 + b * 4 + s; every other slot of row group g has a block row of that group. `tile_cols`: slot s < 4 of a device has block column equal to its block row. A slot of row group g has a block column in [g * 32 - 8, (g + 1) * 32 + 8) within the grid; both ends of that range occur on every device. `tile_count`: some device has 64 live slots and some device 4.
All inputs are finite; a program needn't handle non-finite values.
Results may differ from a plain program's by a relative error of at most 0.00012.
Values sent between devices are 32-bit elements; how exact they have to be, the bound alone decides.
No kernel may reach another device: no remote copies, remote signals or barrier semaphores. Data moves between devices by JAX's collectives and lax.ppermute only.
A program may use at most 64 MiB of HBM per device.

v0:
```python
import jax
import jax.numpy as jnp
from jax import lax
from jax.sharding import PartitionSpec as P

STEPS = 3


shift_term = -0.25
half_width = 0.75


def padded(cells, sides, width):
    for axis, dim in sides:
        count = lax.axis_size(axis)
        ends = count - 1
        head = lax.slice_in_dim(cells, 0, width, axis=dim)
        tail = lax.slice_in_dim(cells, cells.shape[dim] - width, cells.shape[dim], axis=dim)
        cells = jnp.concatenate(
            [
                lax.ppermute(tail, axis, [(i, (i + 1) % count) for i in range(ends)]),
                cells,
                lax.ppermute(head, axis, [((i + 1) % count, i) for i in range(ends)]),
            ],
            axis=dim,
        )
    return cells


def on_device(start_block, tile_vals, tile_rows, tile_cols, tile_count):
    local_rows = start_block.shape[1]
    slot_total = tile_vals.shape[0]
    tile_size = tile_vals.shape[1]
    blk_count = lax.axis_size("blk")
    group_rows = local_rows * blk_count
    group_blocks = group_rows // tile_size
    reach_blocks = group_blocks // 4
    reach_rows = reach_blocks * tile_size
    rows_total = group_rows * lax.axis_size("rows")
    group_index = lax.axis_index("rows")
    base_block = group_index * group_blocks - reach_blocks
    row_local = tile_rows - group_index * group_blocks
    col_local = tile_cols - base_block
    live_count = tile_count.reshape(())
    live_mask = (lax.iota(jnp.int32, slot_total) < live_count).astype(jnp.float32)
    owners = (row_local[None, :] == lax.iota(jnp.int32, group_blocks)[:, None]).astype(
        jnp.float32
    ) * live_mask[None, :]
    row_sums = jnp.sum(tile_vals, axis=2)
    degree_part = jnp.dot(owners, row_sums, precision=lax.Precision.HIGHEST).reshape(group_rows)
    degree = lax.psum_scatter(degree_part, "blk", scatter_dimension=0, tiled=True)
    inv_root = 1.0 / jnp.sqrt(degree)
    vec_width = start_block.shape[0]

    def tile_products(blocks, values, columns, owner_cols):
        picked = jnp.take(blocks, columns, axis=1)
        products = jnp.einsum("ktb,tab->kta", picked, values, precision=lax.Precision.HIGHEST)
        return jnp.einsum("kta,gt->kga", products, owner_cols, precision=lax.Precision.HIGHEST)

    def apply_operator(vectors):
        scaled = vectors * inv_root[None, :]
        gathered = lax.all_gather(scaled, "blk", axis=1, tiled=True)
        extended = padded(gathered, (("rows", 1),), reach_rows)
        blocks = extended.reshape(vec_width, -1, tile_size)
        partial_value = tile_products(blocks, tile_vals, col_local, owners)
        partial_value = partial_value.reshape(vec_width, group_rows)
        summed = lax.psum(partial_value, "blk")
        own_rows = lax.dynamic_slice_in_dim(
            summed, lax.axis_index("blk") * local_rows, local_rows, 1
        )
        applied = own_rows * inv_root[None, :]
        return (shift_term * vectors - applied) / half_width

    previous = start_block
    current = apply_operator(start_block)
    for index in range(STEPS - 1):
        following = 2.0 * apply_operator(current) - previous
        previous = current
        current = following
    gram_part = jnp.dot(current, current.T, precision=lax.Precision.HIGHEST) / rows_total
    gram_sum = lax.psum(gram_part, ("blk", "rows"))
    factor = jnp.linalg.cholesky(gram_sum)
    return lax.linalg.triangular_solve(factor, current, left_side=True, lower=True)


def solution(mesh):
    in_specs = (
        P(None, ("rows", "blk")),
        P(("rows", "blk"), None, None),
        P(("rows", "blk")),
        P(("rows", "blk")),
        P("rows", "blk"),
    )
    out_specs = P(None, ("rows", "blk"))
    return jax.shard_map(
        on_device, mesh=mesh, in_specs=in_specs, out_specs=out_specs, check_vma=False
    )
```

profile of v0, /device:TPU:0, one launch (start us, length us, event | category | flops | bytes accessed | tf_op | source)
XLA Modules:
  0.0 551.7 jit_solution(6185827732698354630)
XLA Ops:
  7.9 3.4 reduce_sum.9
  11.4 38.9 %all-reduce = f32[4096]{0:T(1024)S(1)} all-reduce(f32[4096]{0:T(1024)S(1)} %convolution_bitcast_fusion), channel_id=2, replica_groups=mesh['blk'=8,'rows'=4] {'blk'}, use_global_device_ids=true, to_apply=%region_1.0.clone | all-reduce | flops 4096 | bytes 32768
  52.3 37.6 %all-gather.4.cloned.1.call-done = f32[64,4096]{1,0:T(8,128)} async-done(((f32[64,512]{1,0:T(8,128)}), f32[64,4096]{1,0:T(8,128)}) %all-gather.4.cloned.1.call-update) | async-done | bytes 1048592 | tf_op jit(solution)/shard_map/all_gather | solution.py:62
  93.6 3.8 collective-permute-done.1
  98.8 2.0 gather_fusion
  100.8 10.1 %fusion.15 = f32[64,64,128]{2,0,1:T(8,128)S(1)} fusion(f32[64,128,128]{2,1,0:T(8,128)} %param.8, f32[64,64,128]{2,1,0:T(8,128)} %gather_fusion, pred[64]{0:T(512)(128)(4,1)S(1)} %get-tuple-element.6), kind=kOutput, calls=%fused_computation.18 | convolution fusion | flops 805830656 | bytes 8388672 | tf_op jit(solution)/shard_map/ktb,tab->kta/dot_general | solution.py:57
  110.9 2.3 fusion.10
  114.9 80.5 %all-reduce.5.cloned.1.call-done = f32[64,4096]{1,0:T(8,128)} async-done(((f32[64,4096]{1,0:T(8,128)}), f32[64,4096]{1,0:T(8,128)}) %all-reduce.5.cloned.1.call-update) | async-done | bytes 1048592 | tf_op jit(solution)/shard_map/psum | solution.py:67
  197.1 40.6 %all-gather.6.cloned.1.call-done = f32[64,4096]{1,0:T(8,128)} async-done(((f32[64,512]{1,0:T(8,128)}), f32[64,4096]{1,0:T(8,128)}) %all-gather.6.cloned.1.call-update) | async-done | bytes 1048592 | tf_op jit(solution)/shard_map/all_gather | solution.py:62
  241.5 3.6 collective-permute-done.3
  246.6 2.0 gather_fusion.1
  248.6 10.1 %fusion.18 = f32[64,64,128]{2,0,1:T(8,128)S(1)} fusion(f32[64,128,128]{2,1,0:T(8,128)} %param.8, f32[64,64,128]{2,1,0:T(8,128)} %gather_fusion.1, pred[64]{0:T(512)(128)(4,1)S(1)} %get-tuple-element.6), kind=kOutput, calls=%fused_computation.19 | convolution fusion | flops 805830656 | bytes 8388672 | tf_op jit(solution)/shard_map/ktb,tab->kta/dot_general | solution.py:57
  258.7 2.3 fusion.8
  262.7 80.3 %all-reduce.7.cloned.1.call-done = f32[64,4096]{1,0:T(8,128)} async-done(((f32[64,4096]{1,0:T(8,128)}), f32[64,4096]{1,0:T(8,128)}) %all-reduce.7.cloned.1.call-update) | async-done | bytes 1048592 | tf_op jit(solution)/shard_map/psum | solution.py:67
  343.0 1.7 broadcast_multiply_fusion.1
  344.8 40.1 %all-gather.8.cloned.1.call-done = f32[64,4096]{1,0:T(8,128)} async-done(((f32[64,512]{1,0:T(8,128)}), f32[64,4096]{1,0:T(8,128)}) %all-gather.8.cloned.1.call-update) | async-done | bytes 1048592 | tf_op jit(solution)/shard_map/all_gather | solution.py:62
  388.8 3.6 collective-permute-done.5
  393.8 2.0 gather_fusion.2
  395.8 10.1 %fusion.21 = f32[64,64,128]{2,0,1:T(8,128)S(1)} fusion(f32[64,128,128]{2,1,0:T(8,128)} %param.8, f32[64,64,128]{2,1,0:T(8,128)} %gather_fusion.2, pred[64]{0:T(512)(128)(4,1)S(1)} %get-tuple-element.6), kind=kOutput, calls=%fused_computation.20 | convolution fusion | flops 805830656 | bytes 8388672 | tf_op jit(solution)/shard_map/ktb,tab->kta/dot_general | solution.py:57
  405.9 2.3 fusion.6
  409.9 80.6 %all-reduce.9.cloned.1.call-done = f32[64,4096]{1,0:T(8,128)} async-done(((f32[64,4096]{1,0:T(8,128)}), f32[64,4096]{1,0:T(8,128)}) %all-reduce.9.cloned.1.call-update) | async-done | bytes 1048592 | tf_op jit(solution)/shard_map/psum | solution.py:67
  491.8 39.8 %psum.31 = f32[64,64]{0,1:T(8,128)S(1)} all-reduce(f32[64,64]{0,1:T(8,128)S(1)} %convolution_multiply_fusion), channel_id=1, replica_groups=mesh['blk'=8,'rows'=4] {'blk','rows'}, use_global_device_ids=true, to_apply=%region_5.7 | all-reduce | flops 4096 | bytes 32768 | tf_op jit(solution)/shard_map/psum | solution.py:81
  531.7 5.8 %cholesky.16 = f32[64,64]{1,0:T(8,128)S(1)} custom-call(f32[64,64]{1,0:T(8,128)S(1)} %fusion.33), custom_call_target="Cholesky" | custom-call | tf_op jit(solution)/shard_map/jit(cholesky)/cholesky | solution.py:82
  538.9 4.9 custom-call.6
  (53 shorter events, 28.2 us)
Async XLA Ops:
  6.5 83.3 %all-gather.4.cloned.1.call-start = ((), (), s32[]{:S(2)}) async-start(), calls=%async_computation | async-start | bytes 1179648 | tf_op jit(solution)/shard_map/all_gather | solution.py:62
  7.9 42.4 %copy-start.2 = (u32[32]{0:T(128)S(1)}, u32[32]{0:T(128)}, u32[]{:S(2)}) copy-start(u32[32]{0:T(128)} %constant.93) | copy-start | bytes 388
  7.9 43.7 %copy-start = (f32[64,512]{1,0:T(8,128)S(1)}, f32[64,512]{1,0:T(8,128)}, u32[]{:S(2)}) copy-start(f32[64,512]{1,0:T(8,128)} %param.7) | copy-start | bytes 393220
  7.9 85.7 %copy-start.1 = (s32[64]{0:T(128)S(1)}, s32[64]{0:T(128)}, u32[]{:S(2)}) copy-start(s32[64]{0:T(128)} %param.10) | copy-start | bytes 772
  52.3 143.1 %all-reduce.5.cloned.1.call-start = ((), (), s32[]{:S(2)}) async-start(), calls=%async_computation.1 | async-start | bytes 2097152 | tf_op jit(solution)/shard_map/psum | solution.py:67
  90.9 2.7 collective-permute-start
  92.3 5.1 collective-permute-start.1
  114.8 122.8 %all-gather.6.cloned.1.call-start = ((), (), s32[]{:S(2)}) async-start(), calls=%async_computation.2 | async-start | bytes 1179648 | tf_op jit(solution)/shard_map/all_gather | solution.py:62
  197.0 146.0 %all-reduce.7.cloned.1.call-start = ((), (), s32[]{:S(2)}) async-start(), calls=%async_computation.3 | async-start | bytes 2097152 | tf_op jit(solution)/shard_map/psum | solution.py:67
  238.7 2.8 collective-permute-start.2
  240.0 5.1 collective-permute-start.3
  262.6 122.2 %all-gather.8.cloned.1.call-start = ((), (), s32[]{:S(2)}) async-start(), calls=%async_computation.4 | async-start | bytes 1179648 | tf_op jit(solution)/shard_map/all_gather | solution.py:62
  344.7 145.8 %all-reduce.9.cloned.1.call-start = ((), (), s32[]{:S(2)}) async-start(), calls=%async_computation.5 | async-start | bytes 2097152 | tf_op jit(solution)/shard_map/psum | solution.py:67
  385.9 2.8 collective-permute-start.4
  387.3 5.1 collective-permute-start.5
Sparse Core Ops, SparseCore 0:
  52.4 37.4 all-gather.3
  115.0 80.3 all-reduce.4
  197.8 39.7 all-gather.5
  262.7 80.2 all-reduce.6
  345.0 39.7 all-gather.7
  410.0 80.3 all-reduce.8
where the time goes:
time: 552 us
  waiting for transfers between devices  371 us (67%)
  blocking collectives  78.6 us (14%)
  matrix products  38.6 us (7%)
  other arithmetic  25.5 us (5%)
  between operations  15 us (3%)
  local copies, waits for them, and re-layouts  14.7 us (3%)
  starting transfers between devices  8.4 us (2%)
    psum x3, waiting for transfers between devices, apply_operator(): summed = lax.psum(partial_value, 'blk')  241 us
    all_gather x3, waiting for transfers between devices, apply_operator(): gathered = lax.all_gather(scaled, 'blk', axis=1, tiled=True)  118 us
    psum x1, blocking collectives, on_device(): gram_sum = lax.psum(gram_part, ('blk', 'rows'))  39.8 us
    unnamed x1, blocking collectives  38.9 us
    dot_general x3, matrix products, tile_products(): jnp.einsum('ktb,tab->kta', picked, values, precision=lax.Precision.HIGHEST)  30.2 us
  transfers between devices with their start and end apart: 12, of which 9 were waited for; matrix products, arithmetic and copies ran while one was open for 0% of the time, Pallas kernels for 0%

commit v1 on v0

v1 whole, which is shorter than its diff:
```python
import functools

import jax
import jax.numpy as jnp
from jax import lax
from jax.experimental import pallas as pl
from jax.experimental.pallas import tpu as pltpu
from jax.sharding import PartitionSpec as P

STEPS = 3
CHAINS = 2
OUTER = 4
GROUP = 16
VMEM_BYTES = 40 << 20

shift_term = -0.25
half_width = 0.75


def split_bf16(x):
    high = x.astype(jnp.bfloat16)
    return high, (x - high.astype(jnp.float32)).astype(jnp.bfloat16)


def prepare_kernel(rows_ref, live_ref, vals_ref, cat_ref, degree_ref, *, tile):
    step = pl.program_id(0)

    @pl.when(step == 0)
    def _():
        degree_ref[...] = jnp.zeros_like(degree_ref)

    ones = jnp.ones((8, 2 * tile), jnp.bfloat16)
    for item in range(vals_ref.shape[0]):
        slot = step * vals_ref.shape[0] + item
        values = vals_ref[item] * (slot < live_ref[0]).astype(jnp.float32)
        high, low = split_bf16(values)
        cat_ref[item, :, :tile] = high
        cat_ref[item, :, tile:] = low
        sums = lax.dot_general(
            ones, cat_ref[item], (((1,), (1,)), ((), ())), preferred_element_type=jnp.float32
        )
        degree_ref[pl.ds(rows_ref[slot], 1), :] += sums[:1]


def prepare_tiles(tile_vals, row_local, live_count, group_blocks):
    slots, tile, _ = tile_vals.shape
    return pl.pallas_call(
        functools.partial(prepare_kernel, tile=tile),
        grid_spec=pltpu.PrefetchScalarGridSpec(
            num_scalar_prefetch=2,
            grid=(slots // GROUP,),
            in_specs=[pl.BlockSpec((GROUP, tile, tile), lambda i, *_: (i, 0, 0))],
            out_specs=[
                pl.BlockSpec((GROUP, tile, 2 * tile), lambda i, *_: (i, 0, 0)),
                pl.BlockSpec((group_blocks, tile), lambda i, *_: (0, 0)),
            ],
        ),
        out_shape=[
            jax.ShapeDtypeStruct((slots, tile, 2 * tile), jnp.bfloat16),
            jax.ShapeDtypeStruct((group_blocks, tile), jnp.float32),
        ],
        compiler_params=pltpu.CompilerParams(vmem_limit_bytes=VMEM_BYTES),
        name="prepare_tiles",
    )(row_local, live_count, tile_vals)


def store_split(cat_ref, slot, value):
    width, tile = value.shape
    high, low = split_bf16(value)
    cat_ref[slot, :width, :tile] = high
    cat_ref[slot, :width, tile:] = high
    cat_ref[slot, width:, :tile] = low
    cat_ref[slot, width:, tile:] = low


def product_kernel(cols_ref, rows_ref, place_ref, *refs, kind, inner, outer, own):
    refs = list(refs)
    pieces = [refs.pop(0) for _ in range(inner)]
    near, far = refs.pop(0), refs.pop(0)
    if kind == "first":
        inv_ref = refs.pop(0)
    else:
        last_ref = refs.pop(0)
        older_ref = refs.pop(0) if kind == "third" else None
    tiles_ref = refs.pop(0)
    state_ref = refs.pop(0)
    parts = [refs.pop(0) for _ in range(inner)]
    cat_ref, total_ref = refs
    step = pl.program_id(0)
    width, tile = state_ref.shape[1:]
    reach = inner * own

    @pl.when(step == 0)
    def _():
        total_ref[...] = jnp.zeros_like(total_ref)
        outer_index, inner_index, odd = place_ref[0], place_ref[1], place_ref[2]

        def advance(slot, value):
            if kind != "first":
                value = (2.0 / half_width) * (shift_term * last_ref[slot] - value)
                if kind == "third":
                    value = value - older_ref[slot]
                else:
                    value = 0.5 * value
            state_ref[slot] = value
            store_split(cat_ref, slot, value)

        for k in range(inner):
            block_inner = inner_index ^ k
            for z in range(outer):
                for j in range(own):
                    block = (z * inner + block_inner) * own + j
                    if kind == "first":
                        value = pieces[k][z ^ outer_index, j] * inv_ref[pl.ds(block, 1), :]
                    else:
                        value = pieces[k][z, j]
                    advance(reach + block, value)
            for j in range(own):
                offset = block_inner * own + j
                span = outer * reach + reach
                advance(jnp.where(odd == 1, 0, span) + offset, near[k, j])
                advance(jnp.where(odd == 1, span, 0) + offset, far[k, j])

    for item in range(tiles_ref.shape[0]):
        slot = step * tiles_ref.shape[0] + item
        both = lax.dot_general(
            cat_ref[cols_ref[slot]],
            tiles_ref[item],
            (((1,), (1,)), ((), ())),
            preferred_element_type=jnp.float32,
        )
        total_ref[rows_ref[slot]] += both[:width] + both[width:]

    @pl.when(step == pl.num_programs(0) - 1)
    def _():
        size = outer * own
        for k in range(inner):
            parts[k][...] = total_ref[k * size : (k + 1) * size].reshape(parts[k].shape)


def tile_products(kind, cols, rows, place, pieces, near, far, extra, tiles, inner):
    outer, own, width, tile = pieces[0].shape
    group_blocks = inner * outer * own
    window = group_blocks + 2 * inner * own
    slots = tiles.shape[0]
    whole = lambda shape: pl.BlockSpec(shape, lambda i, *_: (0,) * len(shape))
    operands = [*pieces, near, far, *extra]
    return pl.pallas_call(
        functools.partial(product_kernel, kind=kind, inner=inner, outer=outer, own=own),
        grid_spec=pltpu.PrefetchScalarGridSpec(
            num_scalar_prefetch=3,
            grid=(slots // GROUP,),
            in_specs=[whole(x.shape) for x in operands]
            + [pl.BlockSpec((GROUP, tile, 2 * tile), lambda i, *_: (i, 0, 0))],
            out_specs=[whole((window, width, tile))]
            + [whole((outer, own, width, tile))] * inner,
            scratch_shapes=[
                pltpu.VMEM((window, 2 * width, 2 * tile), jnp.bfloat16),
                pltpu.VMEM((group_blocks, width, tile), jnp.float32),
            ],
        ),
        out_shape=[jax.ShapeDtypeStruct((window, width, tile), jnp.float32)]
        + [jax.ShapeDtypeStruct((outer, own, width, tile), jnp.float32)] * inner,
        compiler_params=pltpu.CompilerParams(vmem_limit_bytes=VMEM_BYTES),
        name="products_" + kind,
    )(cols, rows, place, *operands, tiles)


def on_device(start_block, tile_vals, tile_rows, tile_cols, tile_count):
    vec_width, local_rows = start_block.shape
    tile = tile_vals.shape[1]
    own = local_rows // tile
    blk_count = lax.axis_size("blk")
    row_count = lax.axis_size("rows")
    outer = OUTER
    inner = blk_count // outer
    group_blocks = own * blk_count
    reach = group_blocks // outer
    rows_total = local_rows * blk_count * row_count
    group_index = lax.axis_index("rows")
    blk_index = lax.axis_index("blk")
    outer_index, inner_index = blk_index // inner, blk_index % inner
    odd = group_index % 2

    def over_inner(x, k):
        return lax.ppermute(
            x, "blk", [(z * inner + y, z * inner + (y ^ k)) for z in range(outer) for y in range(inner)]
        )

    def over_outer(x, k):
        return lax.ppermute(
            x, "blk", [(z * inner + y, (z ^ k) * inner + y) for z in range(outer) for y in range(inner)]
        )

    def over_rows(x, k):
        return lax.ppermute(x, "rows", [(i, i ^ k) for i in range(row_count)])

    def with_near(x):
        return lax.ppermute(x, "rows", [(i, i ^ 1) for i in range(row_count)])

    def with_far(x):
        pairs = [(i, i + 1) for i in range(1, row_count - 1, 2)]
        return lax.ppermute(x, "rows", pairs + [(b, a) for a, b in pairs])

    row_local = tile_rows - group_index * group_blocks
    col_local = tile_cols - (group_index * group_blocks - reach)
    place = jnp.stack([outer_index, inner_index, odd]).astype(jnp.int32)
    row_outer = row_local // reach
    row_inner = row_local // own % inner
    row_item = row_local % own
    rows_flat = ((row_inner ^ inner_index) * outer + row_outer) * own + row_item
    rows_last = ((row_inner ^ inner_index) * outer + (row_outer ^ outer_index)) * own + row_item

    tiles, degree = prepare_tiles(tile_vals, row_local, tile_count.reshape(1), group_blocks)

    blocks = start_block.reshape(vec_width, own, tile).transpose(1, 0, 2)
    chains = jnp.split(blocks, CHAINS, axis=1)
    gathered = []
    for chain in chains:
        stack = jnp.stack([chain] + [over_outer(chain, k) for k in range(1, outer)])
        gathered.append([stack] + [over_inner(stack, k) for k in range(1, inner)])

    bit = 1
    while bit < inner:
        degree = degree + over_inner(degree, bit)
        bit *= 2
    bit = 1
    while bit < outer:
        degree = degree + over_outer(degree, bit)
        bit *= 2
    inv_root = 1.0 / jnp.sqrt(degree)
    by_inner = (1.0 / degree).reshape(outer, inner, own, 1, tile)
    inv_own = lax.dynamic_index_in_dim(by_inner, inner_index, 1, keepdims=False)
    by_root = inv_root.reshape(outer, inner, own, 1, tile)

    def halo_pair(near_payload, far_payload):
        return with_near(near_payload), with_far(far_payload)

    near_outer = jnp.where(odd == 1, 0, outer - 1)
    far_outer = jnp.where(odd == 1, outer - 1, 0)

    def first_payload(pieces, which):
        rel = which ^ outer_index
        return jnp.stack(
            [
                lax.dynamic_index_in_dim(pieces[k], rel, 0, keepdims=False)
                * lax.dynamic_index_in_dim(
                    lax.dynamic_index_in_dim(by_root, which, 0, keepdims=False),
                    inner_index ^ k,
                    0,
                    keepdims=False,
                )
                for k in range(inner)
            ]
        )

    def later_payload(pieces, which):
        return jnp.stack([lax.dynamic_index_in_dim(p, which, 0, keepdims=False) for p in pieces])

    states = [[] for _ in range(CHAINS)]
    parts = [None] * CHAINS
    for c in range(CHAINS):
        near, far = halo_pair(
            first_payload(gathered[c], near_outer), first_payload(gathered[c], far_outer)
        )
        state, *parts[c] = tile_products(
            "first", col_local, rows_flat, place, gathered[c], near, far, [inv_root], tiles, inner
        )
        states[c].append(state)

    for index in range(1, STEPS):
        for c in range(CHAINS):
            total = parts[c][0]
            for k in range(1, inner):
                total = total + over_inner(parts[c][k], k)
            bit = 1
            while bit < outer:
                total = total + over_outer(total, bit)
                bit *= 2
            total = total * inv_own
            pieces = [total] + [over_inner(total, k) for k in range(1, inner)]
            near, far = halo_pair(
                later_payload(pieces, near_outer), later_payload(pieces, far_outer)
            )
            kind = "second" if index == 1 else "third"
            extra = [states[c][-1]] if index == 1 else [states[c][-1], states[c][-2]]
            rows = rows_last if index == STEPS - 1 else rows_flat
            state, *parts[c] = tile_products(
                kind, col_local, rows, place, pieces, near, far, extra, tiles, inner
            )
            states[c].append(state)

    own_degree = lax.dynamic_slice_in_dim(degree, blk_index * own, own, 0)[:, None, :]
    start = reach + blk_index * own
    filtered = []
    for c in range(CHAINS):
        total = parts[c][0]
        for k in range(1, inner):
            total = total + over_inner(parts[c][k], k)
        own_sum = total[0]
        for k in range(1, outer):
            own_sum = own_sum + over_outer(total[k], k)
        last = lax.dynamic_slice_in_dim(states[c][-1], start, own, 0)
        older = lax.dynamic_slice_in_dim(states[c][-2], start, own, 0)
        scaled = (2.0 / half_width) * (shift_term * last - own_sum / own_degree) - older
        filtered.append(scaled * jnp.sqrt(own_degree))
    current = jnp.concatenate(filtered, axis=1).transpose(1, 0, 2).reshape(vec_width, local_rows)

    gram_sum = jnp.dot(current, current.T, precision=lax.Precision.HIGHEST) / rows_total
    bit = 1
    while bit < row_count:
        gram_sum = gram_sum + over_rows(gram_sum, bit)
        bit *= 2
    bit = 1
    while bit < inner:
        gram_sum = gram_sum + over_inner(gram_sum, bit)
        bit *= 2
    bit = 1
    while bit < outer:
        gram_sum = gram_sum + over_outer(gram_sum, bit)
        bit *= 2
    factor = jnp.linalg.cholesky(gram_sum, symmetrize_input=False)
    return lax.linalg.triangular_solve(factor, current, left_side=True, lower=True)


def solution(mesh):
    in_specs = (
        P(None, ("rows", "blk")),
        P(("rows", "blk"), None, None),
        P(("rows", "blk")),
        P(("rows", "blk")),
        P("rows", "blk"),
    )
    out_specs = P(None, ("rows", "blk"))
    return jax.shard_map(
        on_device, mesh=mesh, in_specs=in_specs, out_specs=out_specs, check_vma=False
    )
```

time: 552 us -> 247 us (0.45)
  waiting for transfers between devices: 371 us -> 138 us
  blocking collectives: 78.6 us -> 0 us
  starting transfers between devices: 8.4 us -> 61.3 us
  matrix products: 38.6 us -> 1.25 us
  Pallas kernels: 0 us -> 19.5 us
  between operations: 15 us -> 1.29 us
  other arithmetic: 25.5 us -> 16.5 us
  local copies, waits for them, and re-layouts: 14.7 us -> 8.15 us
    psum x3 -> x0, waiting for transfers between devices: 241 us -> none  [apply_operator(): summed = lax.psum(partial_value, 'blk')]
    ppermute x6 -> x52, waiting for transfers between devices: 11 us -> 138 us  [the longest x24 86 us: over_outer(): lax.ppermute(x, 'blk', [(z * inner + y, (z ^ k) * inner + y) for z in ran...]
    all_gather x3 -> x0, waiting for transfers between devices: 118 us -> none  [apply_operator(): gathered = lax.all_gather(scaled, 'blk', axis=1, tiled=True)]
    ppermute x6 -> x52, starting transfers between devices: 8.19 us -> 61.3 us  [the longest x24 23.3 us: over_outer(): lax.ppermute(x, 'blk', [(z * inner + y, (z ^ k) * inner + y) for z in ran...]
    psum x1 -> x0, blocking collectives: 39.8 us -> none  [on_device(): gram_sum = lax.psum(gram_part, ('blk', 'rows'))]
    unnamed x1 -> x0, blocking collectives: 38.9 us -> none
    dot_general x7 -> x0, matrix products: 37.3 us -> none  [the longest x3 30.2 us: tile_products(): jnp.einsum('ktb,tab->kta', picked, values, precision=lax.Precision.HIGHEST)]
    pallas_call x0 -> x7, Pallas kernels: none -> 19.5 us  [the longest x6 17.2 us: tile_products(): pl.pallas_call(functools.partial(product_kernel, kind=kind, inner=inner,...]
  transfers between devices with their start and end apart: 12 -> 52, of which waited for: 9 -> 34; matrix products, arithmetic and copies ran while one was open for 0% -> 1% of each run, Pallas kernels for 0% -> 5%
where the time goes in v1:
time: 247 us; the launch traced here: 246 us
  waiting for transfers between devices  138 us (56%)
  starting transfers between devices  61.3 us (25%)
  Pallas kernels  19.5 us (8%)
  other arithmetic  16.5 us (7%)
  local copies, waits for them, and re-layouts  8.15 us (3%)
    ppermute x24, waiting for transfers between devices, over_outer(): lax.ppermute(x, 'blk', [(z * inner + y, (z ^ k) * inner + y) for z in ran...  86 us
    ppermute x14, waiting for transfers between devices, over_inner(): lax.ppermute(x, 'blk', [(z * inner + y, z * inner + (y ^ k)) for z in ran...  47.6 us
    ppermute x24, starting transfers between devices, over_outer(): lax.ppermute(x, 'blk', [(z * inner + y, (z ^ k) * inner + y) for z in ran...  23.3 us
    ppermute x14, starting transfers between devices, over_inner(): lax.ppermute(x, 'blk', [(z * inner + y, z * inner + (y ^ k)) for z in ran...  20.5 us
    pallas_call x6, Pallas kernels, tile_products(): pl.pallas_call(functools.partial(product_kernel, kind=kind, inner=inner,...  17.2 us
    ppermute x6, starting transfers between devices, with_near(): return lax.ppermute(x, 'rows', [(i, i ^ 1) for i in range(row_count)])  10.9 us
    unnamed x14, local copies, waits for them, and re-layouts  7.3 us
    another operation x3, other arithmetic, on_device(): factor = jnp.linalg.cholesky(gram_sum, symmetrize_input=False)  6.52 us
  transfers between devices with their start and end apart: 52, of which 34 were waited for; matrix products, arithmetic and copies ran while one was open for 1% of the time, Pallas kernels for 5%

profile of v1, /device:TPU:0, one launch (start us, length us, event | category | flops | bytes accessed | tf_op | source)
XLA Modules:
  0.0 246.4 jit_solution(9156222544340547211)
XLA Ops:
  7.8 3.0 %collective-permute-start.4 = (f32[32,128]{1,0:T(8,128)S(1)}, f32[32,128]{1,0:T(8,128)S(1)}, u32[]{:S(2)}, u32[]{:S(2)}) collective-permute-start(f32[32,128]{1,0:T(8,128)S(1)} %get-tuple-element.25), channel_id=1, source_target_pairs={{0,4},{4,0},{8,12},{12,8},{16,20},{20,16},{24,28},{28,24},{1,5},{5... | collective-permute-start | bytes 49160 | tf_op jit(solution)/shard_map/ppermute | solution.py:186
  34.7 3.2 %collective-permute-done.3.refs_1_ = f32[4,4,32,128]{3,2,1,0:T(8,128)S(1)} collective-permute-done((f32[4,4,32,128]{3,2,1,0:T(8,128)S(1)}, f32[4,4,32,128]{3,2,1,0:T(8,128)S(1)}, u32[]{:S(2)}, u32[]{:S(2)}) %collective-permute-start.3) | collective-permute-done | bytes 262176 | tf_op jit(solution)/shard_map/ppermute | solution.py:186
  41.4 3.1 %collective-permute-start.7 = (f32[2,4,32,128]{3,2,1,0:T(8,128)S(1)}, f32[2,4,32,128]{3,2,1,0:T(8,128)S(1)}, u32[]{:S(2)}, u32[]{:S(2)}) collective-permute-start(f32[2,4,32,128]{3,2,1,0:T(8,128)S(1)} %pad_maximum_fusion.2), channel_id=1, source_target_pairs={{0,1},{1,0},{2,3},{3,2},{4,5},{5,4},{6,7},{7,6},{8,9},{9,8},{10,11... | collective-permute-start | bytes 393224 | tf_op jit(solution)/shard_map/ppermute | solution.py:199
  52.1 7.1 %collective-permute-done.9 = f32[4,4,32,128]{3,2,1,0:T(8,128)S(1)} collective-permute-done((f32[4,4,32,128]{3,2,1,0:T(8,128)S(1)}, f32[4,4,32,128]{3,2,1,0:T(8,128)S(1)}, u32[]{:S(2)}, u32[]{:S(2)}) %collective-permute-start.9) | collective-permute-done | bytes 262176 | tf_op jit(solution)/shard_map/ppermute | solution.py:186
  59.3 8.6 %collective-permute-done.10 = f32[4,4,32,128]{3,2,1,0:T(8,128)S(1)} collective-permute-done((f32[4,4,32,128]{3,2,1,0:T(8,128)S(1)}, f32[4,4,32,128]{3,2,1,0:T(8,128)S(1)}, u32[]{:S(2)}, u32[]{:S(2)}) %collective-permute-start.10) | collective-permute-done | bytes 262176 | tf_op jit(solution)/shard_map/ppermute | solution.py:191
  68.8 13.4 %collective-permute-done.11 = f32[4,4,32,128]{3,2,1,0:T(8,128)S(1)} collective-permute-done((f32[4,4,32,128]{3,2,1,0:T(8,128)S(1)}, f32[4,4,32,128]{3,2,1,0:T(8,128)S(1)}, u32[]{:S(2)}, u32[]{:S(2)}) %collective-permute-start.11) | collective-permute-done | bytes 262176 | tf_op jit(solution)/shard_map/ppermute | solution.py:191
  84.7 5.9 %collective-permute-done.12.refs_1_ = f32[4,4,32,128]{3,2,1,0:T(8,128)S(1)} collective-permute-done((f32[4,4,32,128]{3,2,1,0:T(8,128)S(1)}, f32[4,4,32,128]{3,2,1,0:T(8,128)S(1)}, u32[]{:S(2)}, u32[]{:S(2)}) %collective-permute-start.12) | collective-permute-done | bytes 262176 | tf_op jit(solution)/shard_map/ppermute | solution.py:186
  99.3 3.5 %collective-permute-done.31 = f32[4,4,32,128]{3,2,1,0:T(8,128)S(1)} collective-permute-done((f32[4,4,32,128]{3,2,1,0:T(8,128)S(1)}, f32[4,4,32,128]{3,2,1,0:T(8,128)S(1)}, u32[]{:S(2)}, u32[]{:S(2)}) %collective-permute-start.31) | collective-permute-done | bytes 262176 | tf_op jit(solution)/shard_map/ppermute | solution.py:186
  102.8 5.5 %collective-permute-done.15 = f32[4,4,32,128]{3,2,1,0:T(8,128)S(1)} collective-permute-done((f32[4,4,32,128]{3,2,1,0:T(8,128)S(1)}, f32[4,4,32,128]{3,2,1,0:T(8,128)S(1)}, u32[]{:S(2)}, u32[]{:S(2)}) %collective-permute-start.15) | collective-permute-done | bytes 262176 | tf_op jit(solution)/shard_map/ppermute | solution.py:186
  108.5 3.0 %collective-permute-done.32 = f32[4,4,32,128]{3,2,1,0:T(8,128)S(1)} collective-permute-done((f32[4,4,32,128]{3,2,1,0:T(8,128)S(1)}, f32[4,4,32,128]{3,2,1,0:T(8,128)S(1)}, u32[]{:S(2)}, u32[]{:S(2)}) %collective-permute-start.32) | collective-permute-done | bytes 262176 | tf_op jit(solution)/shard_map/ppermute | solution.py:191
  111.8 8.1 %collective-permute-done.16 = f32[4,4,32,128]{3,2,1,0:T(8,128)S(1)} collective-permute-done((f32[4,4,32,128]{3,2,1,0:T(8,128)S(1)}, f32[4,4,32,128]{3,2,1,0:T(8,128)S(1)}, u32[]{:S(2)}, u32[]{:S(2)}) %collective-permute-start.16) | collective-permute-done | bytes 262176 | tf_op jit(solution)/shard_map/ppermute | solution.py:191
  120.0 12.8 %collective-permute-done.33 = f32[4,4,32,128]{3,2,1,0:T(8,128)S(1)} collective-permute-done((f32[4,4,32,128]{3,2,1,0:T(8,128)S(1)}, f32[4,4,32,128]{3,2,1,0:T(8,128)S(1)}, u32[]{:S(2)}, u32[]{:S(2)}) %collective-permute-start.33) | collective-permute-done | bytes 262176 | tf_op jit(solution)/shard_map/ppermute | solution.py:191
  132.8 5.1 %collective-permute-done.17 = f32[4,4,32,128]{3,2,1,0:T(8,128)S(1)} collective-permute-done((f32[4,4,32,128]{3,2,1,0:T(8,128)S(1)}, f32[4,4,32,128]{3,2,1,0:T(8,128)S(1)}, u32[]{:S(2)}, u32[]{:S(2)}) %collective-permute-start.17) | collective-permute-done | bytes 262176 | tf_op jit(solution)/shard_map/ppermute | solution.py:191
  139.7 6.3 %collective-permute-done.34.refs_1_ = f32[4,4,32,128]{3,2,1,0:T(8,128)S(1)} collective-permute-done((f32[4,4,32,128]{3,2,1,0:T(8,128)S(1)}, f32[4,4,32,128]{3,2,1,0:T(8,128)S(1)}, u32[]{:S(2)}, u32[]{:S(2)}) %collective-permute-start.34) | collective-permute-done | bytes 262176 | tf_op jit(solution)/shard_map/ppermute | solution.py:186
  151.9 4.9 %collective-permute-done.37 = f32[4,4,32,128]{3,2,1,0:T(8,128)S(1)} collective-permute-done((f32[4,4,32,128]{3,2,1,0:T(8,128)S(1)}, f32[4,4,32,128]{3,2,1,0:T(8,128)S(1)}, u32[]{:S(2)}, u32[]{:S(2)}) %collective-permute-start.37) | collective-permute-done | bytes 262176 | tf_op jit(solution)/shard_map/ppermute | solution.py:186
  158.5 4.8 %collective-permute-done.38 = f32[4,4,32,128]{3,2,1,0:T(8,128)S(1)} collective-permute-done((f32[4,4,32,128]{3,2,1,0:T(8,128)S(1)}, f32[4,4,32,128]{3,2,1,0:T(8,128)S(1)}, u32[]{:S(2)}, u32[]{:S(2)}) %collective-permute-start.38) | collective-permute-done | bytes 262176 | tf_op jit(solution)/shard_map/ppermute | solution.py:191
  164.1 4.7 %collective-permute-start.19 = (f32[2,4,32,128]{3,2,1,0:T(8,128)S(1)}, f32[2,4,32,128]{3,2,1,0:T(8,128)S(1)}, u32[]{:S(2)}, u32[]{:S(2)}) collective-permute-start(f32[2,4,32,128]{3,2,1,0:T(8,128)S(1)} %pad_maximum_fusion.6), channel_id=1, source_target_pairs={{0,1},{1,0},{2,3},{3,2},{4,5},{5,4},{6,7},{7,6},{8,9},{9,8},{10,11... | collective-permute-start | bytes 393224 | tf_op jit(solution)/shard_map/ppermute | solution.py:199
  168.8 9.4 %collective-permute-done.39 = f32[4,4,32,128]{3,2,1,0:T(8,128)S(1)} collective-permute-done((f32[4,4,32,128]{3,2,1,0:T(8,128)S(1)}, f32[4,4,32,128]{3,2,1,0:T(8,128)S(1)}, u32[]{:S(2)}, u32[]{:S(2)}) %collective-permute-start.39) | collective-permute-done | bytes 262176 | tf_op jit(solution)/shard_map/ppermute | solution.py:191
  209.3 4.7 %collective-permute-done.45 = f32[4,32,128]{2,1,0:T(8,128)S(1)} collective-permute-done((f32[4,32,128]{2,1,0:T(8,128)S(1)}, f32[4,32,128]{2,1,0:T(8,128)S(1)}, u32[]{:S(2)}, u32[]{:S(2)}) %collective-permute-start.45) | collective-permute-done | bytes 65568 | tf_op jit(solution)/shard_map/ppermute | solution.py:191
  221.3 3.2 %collective-permute-done.49 = f32[64,64]{1,0:T(8,128)S(1)} collective-permute-done((f32[64,64]{1,0:T(8,128)S(1)}, f32[64,64]{1,0:T(8,128)S(1)}, u32[]{:S(2)}, u32[]{:S(2)}) %collective-permute-start.49) | collective-permute-done | bytes 16416 | tf_op jit(solution)/shard_map/ppermute | solution.py:186
  224.6 3.9 %collective-permute-done.50 = f32[64,64]{1,0:T(8,128)S(1)} collective-permute-done((f32[64,64]{1,0:T(8,128)S(1)}, f32[64,64]{1,0:T(8,128)S(1)}, u32[]{:S(2)}, u32[]{:S(2)}) %collective-permute-start.50) | collective-permute-done | bytes 16416 | tf_op jit(solution)/shard_map/ppermute | solution.py:191
  228.9 4.4 %collective-permute-done.51 = f32[64,64]{1,0:T(8,128)S(1)} collective-permute-done((f32[64,64]{1,0:T(8,128)S(1)}, f32[64,64]{1,0:T(8,128)S(1)}, u32[]{:S(2)}, u32[]{:S(2)}) %collective-permute-start.51) | collective-permute-done | bytes 16416 | tf_op jit(solution)/shard_map/ppermute | solution.py:191
  233.3 5.8 %cholesky.16 = f32[64,64]{1,0:T(8,128)S(1)} custom-call(f32[64,64]{1,0:T(8,128)S(1)} %add.254), custom_call_target="Cholesky" | custom-call | tf_op jit(solution)/shard_map/jit(cholesky)/cholesky | solution.py:322
  240.5 4.9 %custom-call.6 = f32[1,64,64]{1,2,0:T(8,128)S(1)} custom-call(f32[1,64,64]{2,1,0:T(8,128)S(1)} %fusion.22), custom_call_target="InvertDiagBlocksLowerTriangular" | custom-call | tf_op jit(solution)/shard_map/triangular_solve | solution.py:323
  (166 shorter events, 106.0 us)
Async XLA Ops:
  14.6 17.4 %collective-permute-start.26 = (f32[4,32,128]{2,1,0:T(8,128)S(1)}, f32[4,32,128]{2,1,0:T(8,128)S(1)}, u32[]{:S(2)}, u32[]{:S(2)}) collective-permute-start(f32[4,32,128]{2,1,0:T(8,128)S(1)} %get-tuple-element.85), channel_id=1, source_target_pairs={{0,16},{4,20},{8,24},{12,28},{16,0},{20,4},{24,8},{28,12},{1,17},{... | collective-permute-start | bytes 196616 | tf_op jit(solution)/shard_map/ppermute | solution.py:191
  17.3 14.8 %collective-permute-start.25 = (f32[4,32,128]{2,1,0:T(8,128)S(1)}, f32[4,32,128]{2,1,0:T(8,128)S(1)}, u32[]{:S(2)}, u32[]{:S(2)}) collective-permute-start(f32[4,32,128]{2,1,0:T(8,128)S(1)} %get-tuple-element.85), channel_id=1, source_target_pairs={{0,8},{4,12},{8,0},{12,4},{16,24},{20,28},{24,16},{28,20},{1,9},{5... | collective-permute-start | bytes 196616 | tf_op jit(solution)/shard_map/ppermute | solution.py:191
  17.7 9.2 %collective-permute-start.1 = (f32[4,32,128]{2,1,0:T(8,128)S(1)}, f32[4,32,128]{2,1,0:T(8,128)S(1)}, u32[]{:S(2)}, u32[]{:S(2)}) collective-permute-start(f32[4,32,128]{2,1,0:T(8,128)S(1)} %get-tuple-element.86), channel_id=1, source_target_pairs={{0,16},{4,20},{8,24},{12,28},{16,0},{20,4},{24,8},{28,12},{1,17},{... | collective-permute-start | bytes 196616 | tf_op jit(solution)/shard_map/ppermute | solution.py:191
  17.8 10.5 %collective-permute-start = (f32[4,32,128]{2,1,0:T(8,128)S(1)}, f32[4,32,128]{2,1,0:T(8,128)S(1)}, u32[]{:S(2)}, u32[]{:S(2)}) collective-permute-start(f32[4,32,128]{2,1,0:T(8,128)S(1)} %get-tuple-element.86), channel_id=1, source_target_pairs={{0,8},{4,12},{8,0},{12,4},{16,24},{20,28},{24,16},{28,20},{1,9},{5... | collective-permute-start | bytes 196616 | tf_op jit(solution)/shard_map/ppermute | solution.py:191
  33.0 7.6 %collective-permute-start.28 = (f32[4,4,32,128]{3,2,1,0:T(8,128)S(1)}, f32[4,4,32,128]{3,2,1,0:T(8,128)S(1)}, u32[]{:S(2)}, u32[]{:S(2)}) collective-permute-start(f32[4,4,32,128]{3,2,1,0:T(8,128)S(1)} %pad_maximum_fusion.1.refs_0_), channel_id=1, source_target_pairs={{0,4},{4,0},{8,12},{12,8},{16,20},{20,16},{24,28},{28,24},{1,5},{5... | collective-permute-start | bytes 786440 | tf_op jit(solution)/shard_map/ppermute | solution.py:186
  50.5 8.7 %collective-permute-start.9 = (f32[4,4,32,128]{3,2,1,0:T(8,128)S(1)}, f32[4,4,32,128]{3,2,1,0:T(8,128)S(1)}, u32[]{:S(2)}, u32[]{:S(2)}) collective-permute-start(f32[4,4,32,128]{3,2,1,0:T(8,128)S(1)} %get-tuple-element.28), channel_id=1, source_target_pairs={{0,4},{4,0},{8,12},{12,8},{16,20},{20,16},{24,28},{28,24},{1,5},{5... | collective-permute-start | bytes 786440 | tf_op jit(solution)/shard_map/ppermute | solution.py:186
  59.2 8.6 %collective-permute-start.10 = (f32[4,4,32,128]{3,2,1,0:T(8,128)S(1)}, f32[4,4,32,128]{3,2,1,0:T(8,128)S(1)}, u32[]{:S(2)}, u32[]{:S(2)}) collective-permute-start(f32[4,4,32,128]{3,2,1,0:T(8,128)S(1)} %add.227), channel_id=1, source_target_pairs={{0,8},{4,12},{8,0},{12,4},{16,24},{20,28},{24,16},{28,20},{1,9},{5... | collective-permute-start | bytes 786440 | tf_op jit(solution)/shard_map/ppermute | solution.py:191
  67.9 14.3 %collective-permute-start.11 = (f32[4,4,32,128]{3,2,1,0:T(8,128)S(1)}, f32[4,4,32,128]{3,2,1,0:T(8,128)S(1)}, u32[]{:S(2)}, u32[]{:S(2)}) collective-permute-start(f32[4,4,32,128]{3,2,1,0:T(8,128)S(1)} %add.228), channel_id=1, source_target_pairs={{0,16},{4,20},{8,24},{12,28},{16,0},{20,4},{24,8},{28,12},{1,17},{... | collective-permute-start | bytes 786440 | tf_op jit(solution)/shard_map/ppermute | solution.py:191
  82.3 8.3 %collective-permute-start.12 = (f32[4,4,32,128]{3,2,1,0:T(8,128)S(1)}, f32[4,4,32,128]{3,2,1,0:T(8,128)S(1)}, u32[]{:S(2)}, u32[]{:S(2)}) collective-permute-start(f32[4,4,32,128]{3,2,1,0:T(8,128)S(1)} %add_multiply_fusion.3.refs_0_), channel_id=1, source_target_pairs={{0,4},{4,0},{8,12},{12,8},{16,20},{20,16},{24,28},{28,24},{1,5},{5... | collective-permute-start | bytes 786440 | tf_op jit(solution)/shard_map/ppermute | solution.py:186
  83.9 7.5 %collective-permute-start.29 = (f32[2,4,32,128]{3,2,1,0:T(8,128)S(1)}, f32[2,4,32,128]{3,2,1,0:T(8,128)S(1)}, u32[]{:S(2)}, u32[]{:S(2)}) collective-permute-start(f32[2,4,32,128]{3,2,1,0:T(8,128)S(1)} %pad_maximum_fusion.8), channel_id=1, source_target_pairs={{0,1},{1,0},{2,3},{3,2},{4,5},{5,4},{6,7},{7,6},{8,9},{9,8},{10,11... | collective-permute-start | bytes 393224 | tf_op jit(solution)/shard_map/ppermute | solution.py:199
  94.2 8.5 %collective-permute-start.31 = (f32[4,4,32,128]{3,2,1,0:T(8,128)S(1)}, f32[4,4,32,128]{3,2,1,0:T(8,128)S(1)}, u32[]{:S(2)}, u32[]{:S(2)}) collective-permute-start(f32[4,4,32,128]{3,2,1,0:T(8,128)S(1)} %get-tuple-element.37), channel_id=1, source_target_pairs={{0,4},{4,0},{8,12},{12,8},{16,20},{20,16},{24,28},{28,24},{1,5},{5... | collective-permute-start | bytes 786440 | tf_op jit(solution)/shard_map/ppermute | solution.py:186
  98.7 9.6 %collective-permute-start.15 = (f32[4,4,32,128]{3,2,1,0:T(8,128)S(1)}, f32[4,4,32,128]{3,2,1,0:T(8,128)S(1)}, u32[]{:S(2)}, u32[]{:S(2)}) collective-permute-start(f32[4,4,32,128]{3,2,1,0:T(8,128)S(1)} %get-tuple-element.31), channel_id=1, source_target_pairs={{0,4},{4,0},{8,12},{12,8},{16,20},{20,16},{24,28},{28,24},{1,5},{5... | collective-permute-start | bytes 786440 | tf_op jit(solution)/shard_map/ppermute | solution.py:186
  102.8 8.7 %collective-permute-start.32 = (f32[4,4,32,128]{3,2,1,0:T(8,128)S(1)}, f32[4,4,32,128]{3,2,1,0:T(8,128)S(1)}, u32[]{:S(2)}, u32[]{:S(2)}) collective-permute-start(f32[4,4,32,128]{3,2,1,0:T(8,128)S(1)} %add.240), channel_id=1, source_target_pairs={{0,8},{4,12},{8,0},{12,4},{16,24},{20,28},{24,16},{28,20},{1,9},{5... | collective-permute-start | bytes 786440 | tf_op jit(solution)/shard_map/ppermute | solution.py:191
  108.4 11.5 %collective-permute-start.16 = (f32[4,4,32,128]{3,2,1,0:T(8,128)S(1)}, f32[4,4,32,128]{3,2,1,0:T(8,128)S(1)}, u32[]{:S(2)}, u32[]{:S(2)}) collective-permute-start(f32[4,4,32,128]{3,2,1,0:T(8,128)S(1)} %add.230), channel_id=1, source_target_pairs={{0,8},{4,12},{8,0},{12,4},{16,24},{20,28},{24,16},{28,20},{1,9},{5... | collective-permute-start | bytes 786440 | tf_op jit(solution)/shard_map/ppermute | solution.py:191
  111.5 21.4 %collective-permute-start.33 = (f32[4,4,32,128]{3,2,1,0:T(8,128)S(1)}, f32[4,4,32,128]{3,2,1,0:T(8,128)S(1)}, u32[]{:S(2)}, u32[]{:S(2)}) collective-permute-start(f32[4,4,32,128]{3,2,1,0:T(8,128)S(1)} %add.241), channel_id=1, source_target_pairs={{0,16},{4,20},{8,24},{12,28},{16,0},{20,4},{24,8},{28,12},{1,17},{... | collective-permute-start | bytes 786440 | tf_op jit(solution)/shard_map/ppermute | solution.py:191
  119.9 18.1 %collective-permute-start.17 = (f32[4,4,32,128]{3,2,1,0:T(8,128)S(1)}, f32[4,4,32,128]{3,2,1,0:T(8,128)S(1)}, u32[]{:S(2)}, u32[]{:S(2)}) collective-permute-start(f32[4,4,32,128]{3,2,1,0:T(8,128)S(1)} %add.231), channel_id=1, source_target_pairs={{0,16},{4,20},{8,24},{12,28},{16,0},{20,4},{24,8},{28,12},{1,17},{... | collective-permute-start | bytes 786440 | tf_op jit(solution)/shard_map/ppermute | solution.py:191
  138.1 7.9 %collective-permute-start.34 = (f32[4,4,32,128]{3,2,1,0:T(8,128)S(1)}, f32[4,4,32,128]{3,2,1,0:T(8,128)S(1)}, u32[]{:S(2)}, u32[]{:S(2)}) collective-permute-start(f32[4,4,32,128]{3,2,1,0:T(8,128)S(1)} %get-tuple-element.92.refs_0_), channel_id=1, source_target_pairs={{0,4},{4,0},{8,12},{12,8},{16,20},{20,16},{24,28},{28,24},{1,5},{5... | collective-permute-start | bytes 786440 | tf_op jit(solution)/shard_map/ppermute | solution.py:186
  163.3 14.9 %collective-permute-start.39 = (f32[4,4,32,128]{3,2,1,0:T(8,128)S(1)}, f32[4,4,32,128]{3,2,1,0:T(8,128)S(1)}, u32[]{:S(2)}, u32[]{:S(2)}) collective-permute-start(f32[4,4,32,128]{3,2,1,0:T(8,128)S(1)} %add.244), channel_id=1, source_target_pairs={{0,16},{4,20},{8,24},{12,28},{16,0},{20,4},{24,8},{28,12},{1,17},{... | collective-permute-start | bytes 786440 | tf_op jit(solution)/shard_map/ppermute | solution.py:191
  164.1 16.4 %collective-permute-start.19 = (f32[2,4,32,128]{3,2,1,0:T(8,128)S(1)}, f32[2,4,32,128]{3,2,1,0:T(8,128)S(1)}, u32[]{:S(2)}, u32[]{:S(2)}) collective-permute-start(f32[2,4,32,128]{3,2,1,0:T(8,128)S(1)} %pad_maximum_fusion.6), channel_id=1, source_target_pairs={{0,1},{1,0},{2,3},{3,2},{4,5},{5,4},{6,7},{7,6},{8,9},{9,8},{10,11... | collective-permute-start | bytes 393224 | tf_op jit(solution)/shard_map/ppermute | solution.py:199
  178.2 8.8 %collective-permute-start.40 = (f32[4,4,32,128]{3,2,1,0:T(8,128)S(1)}, f32[4,4,32,128]{3,2,1,0:T(8,128)S(1)}, u32[]{:S(2)}, u32[]{:S(2)}) collective-permute-start(f32[4,4,32,128]{3,2,1,0:T(8,128)S(1)} %add_multiply_fusion.refs_0_), channel_id=1, source_target_pairs={{0,4},{4,0},{8,12},{12,8},{16,20},{20,16},{24,28},{28,24},{1,5},{5... | collective-permute-start | bytes 786440 | tf_op jit(solution)/shard_map/ppermute | solution.py:186
  183.4 12.9 %collective-permute-start.21 = (f32[4,4,32,128]{3,2,1,0:T(8,128)S(1)}, f32[4,4,32,128]{3,2,1,0:T(8,128)}, u32[]{:S(2)}, u32[]{:S(2)}) collective-permute-start(f32[4,4,32,128]{3,2,1,0:T(8,128)S(1)} %get-tuple-element.35), channel_id=1, source_target_pairs={{0,4},{4,0},{8,12},{12,8},{16,20},{20,16},{24,28},{28,24},{1,5},{5... | collective-permute-start | bytes 786440 | tf_op jit(solution)/shard_map/ppermute | solution.py:186
  197.3 7.6 %collective-permute-start.22 = (f32[4,32,128]{2,1,0:T(8,128)S(1)}, f32[4,32,128]{2,1,0:T(8,128)S(1)}, u32[]{:S(2)}, u32[]{:S(2)}) collective-permute-start(f32[4,32,128]{2,1,0:T(8,128)S(1)} %get-tuple-element.53), channel_id=1, source_target_pairs={{0,8},{4,12},{8,0},{12,4},{16,24},{20,28},{24,16},{28,20},{1,9},{5... | collective-permute-start | bytes 196616 | tf_op jit(solution)/shard_map/ppermute | solution.py:191
  197.4 9.1 %collective-permute-start.24 = (f32[4,32,128]{2,1,0:T(8,128)S(1)}, f32[4,32,128]{2,1,0:T(8,128)S(1)}, u32[]{:S(2)}, u32[]{:S(2)}) collective-permute-start(f32[4,32,128]{2,1,0:T(8,128)S(1)} %get-tuple-element.54), channel_id=1, source_target_pairs={{0,24},{4,28},{8,16},{12,20},{16,8},{20,12},{24,0},{28,4},{1,25},{... | collective-permute-start | bytes 196616 | tf_op jit(solution)/shard_map/ppermute | solution.py:191
  204.8 9.1 %collective-permute-start.45 = (f32[4,32,128]{2,1,0:T(8,128)S(1)}, f32[4,32,128]{2,1,0:T(8,128)S(1)}, u32[]{:S(2)}, u32[]{:S(2)}) collective-permute-start(f32[4,32,128]{2,1,0:T(8,128)S(1)} %get-tuple-element.70), channel_id=1, source_target_pairs={{0,16},{4,20},{8,24},{12,28},{16,0},{20,4},{24,8},{28,12},{1,17},{... | collective-permute-start | bytes 196616 | tf_op jit(solution)/shard_map/ppermute | solution.py:191
  (35 other events, 201.4 us)

commit v2 on v0

v2 whole, which is shorter than its diff:
```python
import functools

import jax
import jax.numpy as jnp
from jax import lax
from jax.experimental import pallas as pl
from jax.experimental.pallas import tpu as pltpu
from jax.sharding import PartitionSpec as P

STEPS = 3
CHAINS = 2
GROUP = 16
VMEM_BYTES = 40 << 20

shift_term = -0.25
half_width = 0.75


def split_bf16(x):
    high = x.astype(jnp.bfloat16)
    return high, (x - high.astype(jnp.float32)).astype(jnp.bfloat16)


def prepare_kernel(rows_ref, live_ref, vals_hbm, cat_hbm, degree_ref, vals_ref, cat_ref, in_sems, out_sems):
    slots, tile, _ = vals_ref.shape
    groups = [pl.ds(g * GROUP, GROUP) for g in range(slots // GROUP)]
    loads = [
        pltpu.make_async_copy(vals_hbm.at[g], vals_ref.at[g], in_sems.at[i])
        for i, g in enumerate(groups)
    ]
    stores = [
        pltpu.make_async_copy(cat_ref.at[g], cat_hbm.at[g], out_sems.at[i])
        for i, g in enumerate(groups)
    ]
    for load in loads:
        load.start()
    degree_ref[...] = jnp.zeros_like(degree_ref)
    ones = jnp.ones((8, 2 * tile), jnp.bfloat16)
    for slot in range(slots):
        if slot % GROUP == 0:
            loads[slot // GROUP].wait()
        values = vals_ref[slot] * (slot < live_ref[0]).astype(jnp.float32)
        high, low = split_bf16(values)
        cat_ref[slot, :, :tile] = high
        cat_ref[slot, :, tile:] = low
        sums = lax.dot_general(
            ones, cat_ref[slot], (((1,), (1,)), ((), ())), preferred_element_type=jnp.float32
        )
        degree_ref[pl.ds(rows_ref[slot], 1), :] += sums[:1]
        if slot % GROUP == GROUP - 1:
            stores[slot // GROUP].start()
    for store in stores:
        store.wait()


def prepare_tiles(tile_vals, row_local, live_count, group_blocks):
    slots, tile, _ = tile_vals.shape
    smem = pl.BlockSpec(memory_space=pltpu.SMEM)
    hbm = pl.BlockSpec(memory_space=pltpu.HBM)
    return pl.pallas_call(
        prepare_kernel,
        in_specs=[smem, smem, hbm],
        out_specs=[hbm, pl.BlockSpec(memory_space=pltpu.VMEM)],
        out_shape=[
            jax.ShapeDtypeStruct((slots, tile, 2 * tile), jnp.bfloat16),
            jax.ShapeDtypeStruct((group_blocks, tile), jnp.float32),
        ],
        scratch_shapes=[
            pltpu.VMEM(tile_vals.shape, jnp.float32),
            pltpu.VMEM((slots, tile, 2 * tile), jnp.bfloat16),
            pltpu.SemaphoreType.DMA((slots // GROUP,)),
            pltpu.SemaphoreType.DMA((slots // GROUP,)),
        ],
        compiler_params=pltpu.CompilerParams(vmem_limit_bytes=VMEM_BYTES),
        cost_estimate=pl.CostEstimate(
            flops=2_000_000_000, bytes_accessed=2 * tile_vals.size * 4, transcendentals=0
        ),
        name="prepare_tiles",
    )(row_local, live_count, tile_vals)


def store_split(cat_ref, slot, value):
    width, tile = value.shape
    high, low = split_bf16(value)
    cat_ref[slot, :width, :tile] = high
    cat_ref[slot, :width, tile:] = high
    cat_ref[slot, width:, :tile] = low
    cat_ref[slot, width:, tile:] = low


def product_kernel(cols_ref, rows_ref, place_ref, *refs, kind, pieces_count, outer_half):
    refs = list(refs)
    pieces = [refs.pop(0) for _ in range(pieces_count)]
    near, far = refs.pop(0), refs.pop(0)
    if kind == "first":
        inv_ref = refs.pop(0)
    else:
        last_ref = refs.pop(0)
        older_ref = refs.pop(0) if kind == "third" else None
    tiles_hbm, state_ref = refs.pop(0), refs.pop(0)
    parts = [refs.pop(0) for _ in range(pieces_count)]
    cat_ref, total_ref, tiles_ref, sems = refs
    width, tile = state_ref.shape[1:]
    reach = near.shape[0]
    part = total_ref.shape[0] // pieces_count
    slots = tiles_ref.shape[0]
    copies = [
        pltpu.make_async_copy(
            tiles_hbm.at[pl.ds(g * GROUP, GROUP)], tiles_ref.at[pl.ds(g * GROUP, GROUP)], sems.at[g]
        )
        for g in range(slots // GROUP)
    ]
    for copy in copies:
        copy.start()
    total_ref[...] = jnp.zeros_like(total_ref)
    quad, high, odd = place_ref[0], place_ref[1], place_ref[2]

    def advance(slot, value):
        if kind != "first":
            value = (2.0 / half_width) * (shift_term * last_ref[slot] - value)
            if kind == "third":
                value = value - older_ref[slot]
            else:
                value = 0.5 * value
        state_ref[slot] = value
        store_split(cat_ref, slot, value)

    for k in range(pieces_count):
        who = quad ^ k
        if kind == "first":
            own = part // outer_half
            for h in range(outer_half):
                block = ((h ^ high) * pieces_count + who) * own
                for j in range(own):
                    value = pieces[k][h * own + j] * inv_ref[pl.ds(block + j, 1), :]
                    advance(reach + block + j, value)
        else:
            for j in range(part):
                advance(reach + who * part + j, pieces[k][j])
    span = total_ref.shape[0] + reach
    for j in range(reach):
        advance(jnp.where(odd == 1, 0, span) + j, near[j])
        advance(jnp.where(odd == 1, span, 0) + j, far[j])

    for slot in range(slots):
        if slot % GROUP == 0:
            copies[slot // GROUP].wait()
        both = lax.dot_general(
            cat_ref[cols_ref[slot]],
            tiles_ref[slot],
            (((1,), (1,)), ((), ())),
            preferred_element_type=jnp.float32,
        )
        total_ref[rows_ref[slot]] += both[:width] + both[width:]

    for k in range(pieces_count):
        parts[k][...] = total_ref[k * part : (k + 1) * part]


def tile_products(kind, cols, rows, place, pieces, near, far, extra, tiles, outer_half):
    part, width, tile = pieces[0].shape
    count = len(pieces)
    group_blocks = count * part
    window = group_blocks + 2 * near.shape[0]
    slots = tiles.shape[0]
    vmem = pl.BlockSpec(memory_space=pltpu.VMEM)
    smem = pl.BlockSpec(memory_space=pltpu.SMEM)
    operands = [*pieces, near, far, *extra]
    return pl.pallas_call(
        functools.partial(
            product_kernel, kind=kind, pieces_count=count, outer_half=outer_half
        ),
        in_specs=[smem] * 3 + [vmem] * len(operands) + [pl.BlockSpec(memory_space=pltpu.HBM)],
        out_specs=[vmem] * (1 + count),
        scratch_shapes=[
            pltpu.VMEM((window, 2 * width, 2 * tile), jnp.bfloat16),
            pltpu.VMEM((group_blocks, width, tile), jnp.float32),
            pltpu.VMEM(tiles.shape, tiles.dtype),
            pltpu.SemaphoreType.DMA((slots // GROUP,)),
        ],
        out_shape=[jax.ShapeDtypeStruct((window, width, tile), jnp.float32)]
        + [jax.ShapeDtypeStruct((part, width, tile), jnp.float32)] * count,
        compiler_params=pltpu.CompilerParams(vmem_limit_bytes=VMEM_BYTES),
        cost_estimate=pl.CostEstimate(
            flops=3_000_000_000, bytes_accessed=slots * tile * tile * 4, transcendentals=0
        ),
        name="products_" + kind,
    )(cols, rows, place, *operands, tiles)


def on_device(start_block, tile_vals, tile_rows, tile_cols, tile_count):
    vec_width, local_rows = start_block.shape
    tile = tile_vals.shape[1]
    own = local_rows // tile
    blk_count = lax.axis_size("blk")
    row_count = lax.axis_size("rows")
    high_count = 2
    quad_count = blk_count // high_count
    group_blocks = own * blk_count
    part = group_blocks // quad_count
    reach = group_blocks // 4
    rows_total = local_rows * blk_count * row_count
    group_index = lax.axis_index("rows")
    blk_index = lax.axis_index("blk")
    high, quad = blk_index // quad_count, blk_index % quad_count
    odd = group_index % 2

    def over_blk(x, k):
        return lax.ppermute(x, "blk", [(i, i ^ k) for i in range(blk_count)])

    def over_rows(x, k):
        return lax.ppermute(x, "rows", [(i, i ^ k) for i in range(row_count)])

    def with_far(x):
        pairs = [(i, i + 1) for i in range(1, row_count - 1, 2)]
        return lax.ppermute(x, "rows", pairs + [(b, a) for a, b in pairs])

    def spread(x):
        return [x] + [over_blk(x, k) for k in range(1, quad_count)]

    def gather_sum(parts):
        total = parts[0]
        for k in range(1, quad_count):
            total = total + over_blk(parts[k], k)
        return total

    def all_sum(x):
        return x + over_blk(x, quad_count)

    row_local = tile_rows - group_index * group_blocks
    col_local = tile_cols - (group_index * group_blocks - reach)
    place = jnp.stack([quad, high, odd]).astype(jnp.int32)
    rows_flat = ((row_local // part) ^ quad) * part + row_local % part
    row_blk = row_local // own
    rows_last = ((row_blk % quad_count) ^ quad) * part
    rows_last = rows_last + ((row_blk // quad_count) ^ high) * own + row_local % own

    blocks = start_block.reshape(vec_width, own, tile).transpose(1, 0, 2)
    chains = jnp.split(blocks, CHAINS, axis=1)
    gathered = [
        spread(jnp.concatenate([chain, over_blk(chain, quad_count)])) for chain in chains
    ]

    tiles, degree = prepare_tiles(tile_vals, row_local, tile_count.reshape(1), group_blocks)
    degree = all_sum(sum(spread(degree)))
    inv_root = 1.0 / jnp.sqrt(degree)
    inv_part = lax.dynamic_slice_in_dim(1.0 / degree, quad * part, part, 0)[:, None, :]

    def select(pieces, which):
        value = pieces[0]
        for k in range(1, len(pieces)):
            value = jnp.where(which == k, pieces[k], value)
        return value

    def halos(block_of):
        near_base = jnp.where(odd == 1, 0, group_blocks - reach)
        far_base = jnp.where(odd == 1, group_blocks - reach, 0)
        return over_rows(block_of(near_base), 1), with_far(block_of(far_base))

    def first_blocks(pieces, base):
        found = []
        for m in range(reach // own):
            blk = base // own + m
            piece = select(pieces, (blk % quad_count) ^ quad)
            half = (blk // quad_count) ^ high
            found.append(jnp.where(half == 0, piece[:own], piece[own:]))
        root = lax.dynamic_slice_in_dim(inv_root, base, reach, 0)
        return jnp.concatenate(found) * root[:, None, :]

    def later_blocks(pieces, base):
        return jnp.concatenate(
            [select(pieces, (base // part + m) ^ quad) for m in range(reach // part)]
        )

    states = [[] for _ in range(CHAINS)]
    parts = [None] * CHAINS
    for c in range(CHAINS):
        near, far = halos(functools.partial(first_blocks, gathered[c]))
        state, *parts[c] = tile_products(
            "first", col_local, rows_flat, place, gathered[c], near, far, [inv_root], tiles, high_count
        )
        states[c].append(state)

    for index in range(1, STEPS):
        for c in range(CHAINS):
            total = all_sum(gather_sum(parts[c])) * inv_part
            pieces = spread(total)
            near, far = halos(functools.partial(later_blocks, pieces))
            kind = "second" if index == 1 else "third"
            extra = [states[c][-1]] if index == 1 else [states[c][-1], states[c][-2]]
            rows = rows_last if index == STEPS - 1 else rows_flat
            state, *parts[c] = tile_products(
                kind, col_local, rows, place, pieces, near, far, extra, tiles, high_count
            )
            states[c].append(state)

    own_degree = lax.dynamic_slice_in_dim(degree, blk_index * own, own, 0)[:, None, :]
    start = reach + blk_index * own
    filtered = []
    for c in range(CHAINS):
        total = gather_sum(parts[c])
        own_sum = total[:own] + over_blk(total[own:], quad_count)
        last = lax.dynamic_slice_in_dim(states[c][-1], start, own, 0)
        older = lax.dynamic_slice_in_dim(states[c][-2], start, own, 0)
        scaled = (2.0 / half_width) * (shift_term * last - own_sum / own_degree) - older
        filtered.append(scaled * jnp.sqrt(own_degree))
    current = jnp.concatenate(filtered, axis=1).transpose(1, 0, 2).reshape(vec_width, local_rows)

    gram_sum = jnp.dot(current, current.T, precision=lax.Precision.HIGHEST) / rows_total
    bit = 1
    while bit < row_count:
        gram_sum = gram_sum + over_rows(gram_sum, bit)
        bit *= 2
    gram_sum = all_sum(sum(spread(gram_sum)))
    factor = jnp.linalg.cholesky(gram_sum, symmetrize_input=False)
    return lax.linalg.triangular_solve(factor, current, left_side=True, lower=True)


def solution(mesh):
    in_specs = (
        P(None, ("rows", "blk")),
        P(("rows", "blk"), None, None),
        P(("rows", "blk")),
        P(("rows", "blk")),
        P("rows", "blk"),
    )
    out_specs = P(None, ("rows", "blk"))
    return jax.shard_map(
        on_device, mesh=mesh, in_specs=in_specs, out_specs=out_specs, check_vma=False
    )
```

time: 552 us -> 210 us (0.38)
  waiting for transfers between devices: 371 us -> 80.6 us
  blocking collectives: 78.6 us -> 0 us
  starting transfers between devices: 8.4 us -> 81.2 us
  matrix products: 38.6 us -> 1.25 us
  Pallas kernels: 0 us -> 21.4 us
  between operations: 15 us -> 1.16 us
  other arithmetic: 25.5 us -> 14.4 us
    psum x3 -> x0, waiting for transfers between devices: 241 us -> none  [apply_operator(): summed = lax.psum(partial_value, 'blk')]
    all_gather x3 -> x0, waiting for transfers between devices: 118 us -> none  [apply_operator(): gathered = lax.all_gather(scaled, 'blk', axis=1, tiled=True)]
    ppermute x6 -> x66, starting transfers between devices: 8.19 us -> 81.2 us  [the longest x52 61.1 us: over_blk(): return lax.ppermute(x, 'blk', [(i, i ^ k) for i in range(blk_count)])]
    ppermute x6 -> x66, waiting for transfers between devices: 11 us -> 80.6 us  [the longest x52 76.1 us: over_blk(): return lax.ppermute(x, 'blk', [(i, i ^ k) for i in range(blk_count)])]
    psum x1 -> x0, blocking collectives: 39.8 us -> none  [on_device(): gram_sum = lax.psum(gram_part, ('blk', 'rows'))]
    unnamed x1 -> x0, blocking collectives: 38.9 us -> none
    dot_general x7 -> x0, matrix products: 37.3 us -> none  [the longest x3 30.2 us: tile_products(): jnp.einsum('ktb,tab->kta', picked, values, precision=lax.Precision.HIGHEST)]
    pallas_call x0 -> x7, Pallas kernels: none -> 21.4 us  [the longest x6 18.5 us: tile_products(): pl.pallas_call(functools.partial(product_kernel, kind=kind, pieces_count=...]
  transfers between devices with their start and end apart: 12 -> 66, of which waited for: 9 -> 41; matrix products, arithmetic and copies ran while one was open for 0% -> 1% of each run, Pallas kernels for 0% -> 6%
where the time goes in v2:
time: 210 us; the launch traced here: 209 us
  starting transfers between devices  81.2 us (39%)
  waiting for transfers between devices  80.6 us (38%)
  Pallas kernels  21.4 us (10%)
  other arithmetic  14.4 us (7%)
  local copies, waits for them, and re-layouts  9.32 us (4%)
    ppermute x52, waiting for transfers between devices, over_blk(): return lax.ppermute(x, 'blk', [(i, i ^ k) for i in range(blk_count)])  76.1 us
    ppermute x52, starting transfers between devices, over_blk(): return lax.ppermute(x, 'blk', [(i, i ^ k) for i in range(blk_count)])  61.1 us
    pallas_call x6, Pallas kernels, tile_products(): pl.pallas_call(functools.partial(product_kernel, kind=kind, pieces_count=...  18.5 us
    ppermute x8, starting transfers between devices, over_rows(): return lax.ppermute(x, 'rows', [(i, i ^ k) for i in range(row_count)])  15.9 us
    unnamed x22, local copies, waits for them, and re-layouts  8.6 us
    another operation x3, other arithmetic, on_device(): factor = jnp.linalg.cholesky(gram_sum, symmetrize_input=False)  6.52 us
    another operation x2, other arithmetic, on_device(): lax.linalg.triangular_solve(factor, current, left_side=True, lower=True)  5.55 us
    ppermute x8, waiting for transfers between devices, over_rows(): return lax.ppermute(x, 'rows', [(i, i ^ k) for i in range(row_count)])  4.55 us
  transfers between devices with their start and end apart: 66, of which 41 were waited for; matrix products, arithmetic and copies ran while one was open for 1% of the time, Pallas kernels for 6%

profile of v2, /device:TPU:0, one launch (start us, length us, event | category | flops | bytes accessed | tf_op | source)
XLA Modules:
  0.0 209.3 jit_solution(2884049054299807023)
XLA Ops:
  3.6 2.9 %prepare_tiles.1 = (bf16[64,128,256]{2,1,0:T(8,128)(2,1)S(1)}, f32[32,128]{1,0:T(8,128)S(1)}) custom-call(s32[64]{0:T(128)S(1)} %get-tuple-element.74.rows_ref, s32[1]{0:T(128)} %bitcast.30.live_ref, f32[64,128,128]{2,1,0:T(8,128)S(1)} %copy-done.1), custom_call_target="tpu_custom_call" | custom-call | flops 2000000000 | bytes 8388608 | tf_op jit(solution)/shard_map/prepare_tiles/pallas_call | solution.py:60
  8.5 4.0 %collective-permute-start.6 = (f32[32,128]{1,0:T(8,128)S(1)}, f32[32,128]{1,0:T(8,128)S(1)}, u32[]{:S(2)}, u32[]{:S(2)}) collective-permute-start(f32[32,128]{1,0:T(8,128)S(1)} %get-tuple-element.37), channel_id=1, source_target_pairs={{0,12},{4,8},{8,4},{12,0},{16,28},{20,24},{24,20},{28,16},{1,13},{... | collective-permute-start | bytes 49160 | tf_op jit(solution)/shard_map/ppermute | solution.py:209
  16.6 2.6 %collective-permute-start.7 = (f32[32,128]{1,0:T(8,128)S(1)}, f32[32,128]{1,0:T(8,128)S(1)}, u32[]{:S(2)}, u32[]{:S(2)}) collective-permute-start(f32[32,128]{1,0:T(8,128)S(1)} %add_add_fusion.7), channel_id=1, source_target_pairs={{0,16},{4,20},{8,24},{12,28},{16,0},{20,4},{24,8},{28,12},{1,17},{... | collective-permute-start | bytes 49160 | tf_op jit(solution)/shard_map/ppermute | solution.py:209
  19.6 2.6 %collective-permute-start.32 = (f32[4,32,128]{2,1,0:T(8,128)S(1)}, f32[4,32,128]{2,1,0:T(8,128)S(1)}, u32[]{:S(2)}, u32[]{:S(2)}) collective-permute-start(f32[4,32,128]{2,1,0:T(8,128)S(1)} %get-tuple-element.90), channel_id=1, source_target_pairs={{0,16},{4,20},{8,24},{12,28},{16,0},{20,4},{24,8},{28,12},{1,17},{... | collective-permute-start | bytes 196616 | tf_op jit(solution)/shard_map/ppermute | solution.py:209
  22.3 4.5 %collective-permute-done.32 = f32[4,32,128]{2,1,0:T(8,128)S(1)} collective-permute-done((f32[4,32,128]{2,1,0:T(8,128)S(1)}, f32[4,32,128]{2,1,0:T(8,128)S(1)}, u32[]{:S(2)}, u32[]{:S(2)}) %collective-permute-start.32) | collective-permute-done | bytes 65568 | tf_op jit(solution)/shard_map/ppermute | solution.py:209
  40.7 3.1 %products_first.2 = (f32[48,32,128]{2,1,0:T(8,128)S(1)}, f32[8,32,128]{2,1,0:T(8,128)S(1)}, f32[8,32,128]{2,1,0:T(8,128)S(1)}, f32[8,32,128]{2,1,0:T(8,128)S(1)}, f32[8,32,128]{2,1,0:T(8,128)S(1)}) custom-call(s32[64]{0:T(128)S(1)} %broadcast_subtract_fusion.1.cols_ref, s32[64]{0:T(128)S(1)} %get-tuple-element.73.rows_ref, s32[3]{0:T(128)S(1)} %pad_add_fusion.place_ref, ...), custom_call_target="tpu_custom_call" | custom-call | flops 3000000000 | bytes 4194304 | tf_op jit(solution)/shard_map/products_first/pallas_call | solution.py:169
  44.7 2.7 %collective-permute-start.12 = (f32[8,32,128]{2,1,0:T(8,128)S(1)}, f32[8,32,128]{2,1,0:T(8,128)S(1)}, u32[]{:S(2)}, u32[]{:S(2)}) collective-permute-start(f32[8,32,128]{2,1,0:T(8,128)S(1)} %get-tuple-element.42), channel_id=1, source_target_pairs={{0,12},{4,8},{8,4},{12,0},{16,28},{20,24},{24,20},{28,16},{1,13},{... | collective-permute-start | bytes 393224 | tf_op jit(solution)/shard_map/ppermute | solution.py:209
  54.1 5.0 %collective-permute-done.13 = f32[8,32,128]{2,1,0:T(8,128)S(1)} collective-permute-done((f32[8,32,128]{2,1,0:T(8,128)S(1)}, f32[8,32,128]{2,1,0:T(8,128)S(1)}, u32[]{:S(2)}, u32[]{:S(2)}) %collective-permute-start.13) | collective-permute-done | bytes 131104 | tf_op jit(solution)/shard_map/ppermute | solution.py:209
  68.7 7.7 %collective-permute-start.17 = (f32[8,32,128]{2,1,0:T(8,128)S(1)}, f32[8,32,128]{2,1,0:T(8,128)S(1)}, u32[]{:S(2)}, u32[]{:S(2)}) collective-permute-start(f32[8,32,128]{2,1,0:T(8,128)S(1)} %get-tuple-element.78), channel_id=1, source_target_pairs={{0,1},{1,0},{2,3},{3,2},{4,5},{5,4},{6,7},{7,6},{8,9},{9,8},{10,11... | collective-permute-start | bytes 393224 | tf_op jit(solution)/shard_map/ppermute | solution.py:212
  78.6 3.1 %products_first.3 = (f32[48,32,128]{2,1,0:T(8,128)S(1)}, f32[8,32,128]{2,1,0:T(8,128)S(1)}, f32[8,32,128]{2,1,0:T(8,128)S(1)}, f32[8,32,128]{2,1,0:T(8,128)S(1)}, f32[8,32,128]{2,1,0:T(8,128)S(1)}) custom-call(s32[64]{0:T(128)S(1)} %broadcast_subtract_fusion.1.cols_ref, s32[64]{0:T(128)S(1)} %get-tuple-element.73.rows_ref, s32[3]{0:T(128)S(1)} %pad_add_fusion.place_ref, ...), custom_call_target="tpu_custom_call" | custom-call | flops 3000000000 | bytes 4194304 | tf_op jit(solution)/shard_map/products_first/pallas_call | solution.py:169
  85.3 3.1 %products_second.2 = (f32[48,32,128]{2,1,0:T(8,128)S(1)}, f32[8,32,128]{2,1,0:T(8,128)S(1)}, f32[8,32,128]{2,1,0:T(8,128)S(1)}, f32[8,32,128]{2,1,0:T(8,128)S(1)}, f32[8,32,128]{2,1,0:T(8,128)S(1)}) custom-call(s32[64]{0:T(128)S(1)} %broadcast_subtract_fusion.1.cols_ref, s32[64]{0:T(128)S(1)} %get-tuple-element.73.rows_ref, s32[3]{0:T(128)S(1)} %pad_add_fusion.place_ref, ...), custom_call_target="tpu_custom_call" | custom-call | flops 3000000000 | bytes 4194304 | tf_op jit(solution)/shard_map/products_second/pallas_call | solution.py:169
  97.0 2.7 %collective-permute-done.21 = f32[8,32,128]{2,1,0:T(8,128)S(1)} collective-permute-done((f32[8,32,128]{2,1,0:T(8,128)S(1)}, f32[8,32,128]{2,1,0:T(8,128)S(1)}, u32[]{:S(2)}, u32[]{:S(2)}) %collective-permute-start.21) | collective-permute-done | bytes 131104 | tf_op jit(solution)/shard_map/ppermute | solution.py:209
  100.5 6.3 %collective-permute-done.22 = f32[8,32,128]{2,1,0:T(8,128)S(1)} collective-permute-done((f32[8,32,128]{2,1,0:T(8,128)S(1)}, f32[8,32,128]{2,1,0:T(8,128)S(1)}, u32[]{:S(2)}, u32[]{:S(2)}) %collective-permute-start.22) | collective-permute-done | bytes 131104 | tf_op jit(solution)/shard_map/ppermute | solution.py:209
  117.9 3.1 %products_second.3 = (f32[48,32,128]{2,1,0:T(8,128)S(1)}, f32[8,32,128]{2,1,0:T(8,128)S(1)}, f32[8,32,128]{2,1,0:T(8,128)S(1)}, f32[8,32,128]{2,1,0:T(8,128)S(1)}, f32[8,32,128]{2,1,0:T(8,128)S(1)}) custom-call(s32[64]{0:T(128)S(1)} %broadcast_subtract_fusion.1.cols_ref, s32[64]{0:T(128)S(1)} %get-tuple-element.73.rows_ref, s32[3]{0:T(128)S(1)} %pad_add_fusion.place_ref, ...), custom_call_target="tpu_custom_call" | custom-call | flops 3000000000 | bytes 4194304 | tf_op jit(solution)/shard_map/products_second/pallas_call | solution.py:169
  128.5 3.1 %collective-permute-done.49 = f32[8,32,128]{2,1,0:T(8,128)S(1)} collective-permute-done((f32[8,32,128]{2,1,0:T(8,128)S(1)}, f32[8,32,128]{2,1,0:T(8,128)S(1)}, u32[]{:S(2)}, u32[]{:S(2)}) %collective-permute-start.49) | collective-permute-done | bytes 131104 | tf_op jit(solution)/shard_map/ppermute | solution.py:209
  131.8 2.6 %collective-permute-start.25 = (f32[8,32,128]{2,1,0:T(8,128)S(1)}, f32[8,32,128]{2,1,0:T(8,128)S(1)}, u32[]{:S(2)}, u32[]{:S(2)}) collective-permute-start(f32[8,32,128]{2,1,0:T(8,128)S(1)} %get-tuple-element.95.refs_0_), channel_id=1, source_target_pairs={{0,12},{4,8},{8,4},{12,0},{16,28},{20,24},{24,20},{28,16},{1,13},{... | collective-permute-start | bytes 393224 | tf_op jit(solution)/shard_map/ppermute | solution.py:209
  135.4 5.1 %collective-permute-done.50 = f32[8,32,128]{2,1,0:T(8,128)S(1)} collective-permute-done((f32[8,32,128]{2,1,0:T(8,128)S(1)}, f32[8,32,128]{2,1,0:T(8,128)S(1)}, u32[]{:S(2)}, u32[]{:S(2)}) %collective-permute-start.50) | collective-permute-done | bytes 131104 | tf_op jit(solution)/shard_map/ppermute | solution.py:209
  154.3 3.1 %products_third.2 = (f32[48,32,128]{2,1,0:T(8,128)S(1)}, f32[8,32,128]{2,1,0:T(8,128)S(1)}, f32[8,32,128]{2,1,0:T(8,128)S(1)}, f32[8,32,128]{2,1,0:T(8,128)S(1)}, f32[8,32,128]{2,1,0:T(8,128)S(1)}) custom-call(s32[64]{0:T(128)S(1)} %broadcast_subtract_fusion.1.cols_ref, s32[64]{0:T(128)S(1)} %fusion.18.rows_ref, s32[3]{0:T(128)S(1)} %pad_add_fusion.place_ref, ...), custom_call_target="tpu_custom_call" | custom-call | flops 3000000000 | bytes 4194304 | tf_op jit(solution)/shard_map/products_third/pallas_call | solution.py:169
  160.9 3.1 %products_third.3 = (f32[48,32,128]{2,1,0:T(8,128)S(1)}, f32[8,32,128]{2,1,0:T(8,128)S(1)}, f32[8,32,128]{2,1,0:T(8,128)S(1)}, f32[8,32,128]{2,1,0:T(8,128)S(1)}, f32[8,32,128]{2,1,0:T(8,128)S(1)}) custom-call(s32[64]{0:T(128)S(1)} %broadcast_subtract_fusion.1.cols_ref, s32[64]{0:T(128)S(1)} %fusion.18.rows_ref, s32[3]{0:T(128)S(1)} %pad_add_fusion.place_ref, ...), custom_call_target="tpu_custom_call" | custom-call | flops 3000000000 | bytes 4194304 | tf_op jit(solution)/shard_map/products_third/pallas_call | solution.py:169
  168.1 2.8 %collective-permute-done.56 = f32[8,32,128]{2,1,0:T(8,128)S(1)} collective-permute-done((f32[8,32,128]{2,1,0:T(8,128)S(1)}, f32[8,32,128]{2,1,0:T(8,128)S(1)}, u32[]{:S(2)}, u32[]{:S(2)}) %collective-permute-start.56) | collective-permute-done | bytes 131104 | tf_op jit(solution)/shard_map/ppermute | solution.py:209
  175.2 4.2 %collective-permute-done.59 = f32[4,32,128]{2,1,0:T(8,128)S(1)} collective-permute-done((f32[4,32,128]{2,1,0:T(8,128)S(1)}, f32[4,32,128]{2,1,0:T(8,128)S(1)}, u32[]{:S(2)}, u32[]{:S(2)}) %collective-permute-start.59) | collective-permute-done | bytes 65568 | tf_op jit(solution)/shard_map/ppermute | solution.py:209
  192.0 4.3 %collective-permute-done.65 = f32[64,64]{1,0:T(8,128)S(1)} collective-permute-done((f32[64,64]{1,0:T(8,128)S(1)}, f32[64,64]{1,0:T(8,128)S(1)}, u32[]{:S(2)}, u32[]{:S(2)}) %collective-permute-start.65) | collective-permute-done | bytes 16416 | tf_op jit(solution)/shard_map/ppermute | solution.py:209
  196.3 5.8 %cholesky.16 = f32[64,64]{1,0:T(8,128)S(1)} custom-call(f32[64,64]{1,0:T(8,128)S(1)} %add.249), custom_call_target="Cholesky" | custom-call | tf_op jit(solution)/shard_map/jit(cholesky)/cholesky | solution.py:315
  203.4 4.9 %custom-call.6 = f32[1,64,64]{1,2,0:T(8,128)S(1)} custom-call(f32[1,64,64]{2,1,0:T(8,128)S(1)} %fusion.16), custom_call_target="InvertDiagBlocksLowerTriangular" | custom-call | tf_op jit(solution)/shard_map/triangular_solve | solution.py:316
  (187 shorter events, 115.8 us)
Async XLA Ops:
  19.2 11.1 %collective-permute-start = (f32[4,32,128]{2,1,0:T(8,128)S(1)}, f32[4,32,128]{2,1,0:T(8,128)S(1)}, u32[]{:S(2)}, u32[]{:S(2)}) collective-permute-start(f32[4,32,128]{2,1,0:T(8,128)S(1)} %get-tuple-element.89), channel_id=1, source_target_pairs={{0,16},{4,20},{8,24},{12,28},{16,0},{20,4},{24,8},{28,12},{1,17},{... | collective-permute-start | bytes 196616 | tf_op jit(solution)/shard_map/ppermute | solution.py:209
  26.9 8.2 %collective-permute-start.34 = (f32[8,32,128]{2,1,0:T(8,128)S(1)}, f32[8,32,128]{2,1,0:T(8,128)S(1)}, u32[]{:S(2)}, u32[]{:S(2)}) collective-permute-start(f32[8,32,128]{2,1,0:T(8,128)S(1)} %pad_maximum_fusion.1.refs_0_), channel_id=1, source_target_pairs={{0,8},{4,12},{8,0},{12,4},{16,24},{20,28},{24,16},{28,20},{1,9},{5... | collective-permute-start | bytes 393224 | tf_op jit(solution)/shard_map/ppermute | solution.py:209
  62.7 13.7 %collective-permute-start.36 = (f32[8,32,128]{2,1,0:T(8,128)S(1)}, f32[8,32,128]{2,1,0:T(8,128)S(1)}, u32[]{:S(2)}, u32[]{:S(2)}) collective-permute-start(f32[8,32,128]{2,1,0:T(8,128)S(1)} %get-tuple-element.100), channel_id=1, source_target_pairs={{0,1},{1,0},{2,3},{3,2},{4,5},{5,4},{6,7},{7,6},{8,9},{9,8},{10,11... | collective-permute-start | bytes 393224 | tf_op jit(solution)/shard_map/ppermute | solution.py:212
  64.8 11.6 %collective-permute-start.37 = (f32[8,32,128]{2,1,0:T(8,128)S(1)}, f32[8,32,128]{2,1,0:T(8,128)S(1)}, u32[]{:S(2)}, u32[]{:S(2)}) collective-permute-start(f32[8,32,128]{2,1,0:T(8,128)S(1)} %get-tuple-element.98), channel_id=1, source_target_pairs={{1,2},{2,1},{5,6},{6,5},{9,10},{10,9},{13,14},{14,13},{17,18},{18,... | collective-permute-start | bytes 393224 | tf_op jit(solution)/shard_map/ppermute | solution.py:216
  68.0 17.3 %collective-permute-start.18 = (f32[8,32,128]{2,1,0:T(8,128)S(1)}, f32[8,32,128]{2,1,0:T(8,128)S(1)}, u32[]{:S(2)}, u32[]{:S(2)}) collective-permute-start(f32[8,32,128]{2,1,0:T(8,128)S(1)} %get-tuple-element.77), channel_id=1, source_target_pairs={{1,2},{2,1},{5,6},{6,5},{9,10},{10,9},{13,14},{14,13},{17,18},{18,... | collective-permute-start | bytes 393224 | tf_op jit(solution)/shard_map/ppermute | solution.py:216
  68.7 16.6 %collective-permute-start.17 = (f32[8,32,128]{2,1,0:T(8,128)S(1)}, f32[8,32,128]{2,1,0:T(8,128)S(1)}, u32[]{:S(2)}, u32[]{:S(2)}) collective-permute-start(f32[8,32,128]{2,1,0:T(8,128)S(1)} %get-tuple-element.78), channel_id=1, source_target_pairs={{0,1},{1,0},{2,3},{3,2},{4,5},{5,4},{6,7},{7,6},{8,9},{9,8},{10,11... | collective-permute-start | bytes 393224 | tf_op jit(solution)/shard_map/ppermute | solution.py:212
  81.7 8.7 %collective-permute-start.38 = (f32[8,32,128]{2,1,0:T(8,128)S(1)}, f32[8,32,128]{2,1,0:T(8,128)S(1)}, u32[]{:S(2)}, u32[]{:S(2)}) collective-permute-start(f32[8,32,128]{2,1,0:T(8,128)S(1)} %get-tuple-element.55), channel_id=1, source_target_pairs={{0,4},{4,0},{8,12},{12,8},{16,20},{20,16},{24,28},{28,24},{1,5},{5... | collective-permute-start | bytes 393224 | tf_op jit(solution)/shard_map/ppermute | solution.py:209
  83.0 9.0 %collective-permute-start.39 = (f32[8,32,128]{2,1,0:T(8,128)S(1)}, f32[8,32,128]{2,1,0:T(8,128)S(1)}, u32[]{:S(2)}, u32[]{:S(2)}) collective-permute-start(f32[8,32,128]{2,1,0:T(8,128)S(1)} %get-tuple-element.56), channel_id=1, source_target_pairs={{0,8},{4,12},{8,0},{12,4},{16,24},{20,28},{24,16},{28,20},{1,9},{5... | collective-permute-start | bytes 393224 | tf_op jit(solution)/shard_map/ppermute | solution.py:209
  83.8 8.2 %collective-permute-start.40 = (f32[8,32,128]{2,1,0:T(8,128)S(1)}, f32[8,32,128]{2,1,0:T(8,128)S(1)}, u32[]{:S(2)}, u32[]{:S(2)}) collective-permute-start(f32[8,32,128]{2,1,0:T(8,128)S(1)} %get-tuple-element.57), channel_id=1, source_target_pairs={{0,12},{4,8},{8,4},{12,0},{16,28},{20,24},{24,20},{28,16},{1,13},{... | collective-permute-start | bytes 393224 | tf_op jit(solution)/shard_map/ppermute | solution.py:209
  90.4 9.3 %collective-permute-start.21 = (f32[8,32,128]{2,1,0:T(8,128)S(1)}, f32[8,32,128]{2,1,0:T(8,128)S(1)}, u32[]{:S(2)}, u32[]{:S(2)}) collective-permute-start(f32[8,32,128]{2,1,0:T(8,128)S(1)} %get-tuple-element.47), channel_id=1, source_target_pairs={{0,12},{4,8},{8,4},{12,0},{16,28},{20,24},{24,20},{28,16},{1,13},{... | collective-permute-start | bytes 393224 | tf_op jit(solution)/shard_map/ppermute | solution.py:209
  92.0 8.6 %collective-permute-start.41 = (f32[8,32,128]{2,1,0:T(8,128)S(1)}, f32[8,32,128]{2,1,0:T(8,128)S(1)}, u32[]{:S(2)}, u32[]{:S(2)}) collective-permute-start(f32[8,32,128]{2,1,0:T(8,128)S(1)} %add_add_fusion.2), channel_id=1, source_target_pairs={{0,16},{4,20},{8,24},{12,28},{16,0},{20,4},{24,8},{28,12},{1,17},{... | collective-permute-start | bytes 393224 | tf_op jit(solution)/shard_map/ppermute | solution.py:209
  122.3 9.3 %collective-permute-start.49 = (f32[8,32,128]{2,1,0:T(8,128)S(1)}, f32[8,32,128]{2,1,0:T(8,128)S(1)}, u32[]{:S(2)}, u32[]{:S(2)}) collective-permute-start(f32[8,32,128]{2,1,0:T(8,128)S(1)} %get-tuple-element.62), channel_id=1, source_target_pairs={{0,12},{4,8},{8,4},{12,0},{16,28},{20,24},{24,20},{28,16},{1,13},{... | collective-permute-start | bytes 393224 | tf_op jit(solution)/shard_map/ppermute | solution.py:209
  131.6 8.9 %collective-permute-start.50 = (f32[8,32,128]{2,1,0:T(8,128)S(1)}, f32[8,32,128]{2,1,0:T(8,128)S(1)}, u32[]{:S(2)}, u32[]{:S(2)}) collective-permute-start(f32[8,32,128]{2,1,0:T(8,128)S(1)} %add_add_fusion.1), channel_id=1, source_target_pairs={{0,16},{4,20},{8,24},{12,28},{16,0},{20,4},{24,8},{28,12},{1,17},{... | collective-permute-start | bytes 393224 | tf_op jit(solution)/shard_map/ppermute | solution.py:209
  131.8 12.0 %collective-permute-start.25 = (f32[8,32,128]{2,1,0:T(8,128)S(1)}, f32[8,32,128]{2,1,0:T(8,128)S(1)}, u32[]{:S(2)}, u32[]{:S(2)}) collective-permute-start(f32[8,32,128]{2,1,0:T(8,128)S(1)} %get-tuple-element.95.refs_0_), channel_id=1, source_target_pairs={{0,12},{4,8},{8,4},{12,0},{16,28},{20,24},{24,20},{28,16},{1,13},{... | collective-permute-start | bytes 393224 | tf_op jit(solution)/shard_map/ppermute | solution.py:209
  134.4 10.4 %collective-permute-start.24 = (f32[8,32,128]{2,1,0:T(8,128)S(1)}, f32[8,32,128]{2,1,0:T(8,128)S(1)}, u32[]{:S(2)}, u32[]{:S(2)}) collective-permute-start(f32[8,32,128]{2,1,0:T(8,128)S(1)} %get-tuple-element.95.refs_0_), channel_id=1, source_target_pairs={{0,8},{4,12},{8,0},{12,4},{16,24},{20,28},{24,16},{28,20},{1,9},{5... | collective-permute-start | bytes 393224 | tf_op jit(solution)/shard_map/ppermute | solution.py:209
  134.4 10.4 %collective-permute-start.23 = (f32[8,32,128]{2,1,0:T(8,128)S(1)}, f32[8,32,128]{2,1,0:T(8,128)S(1)}, u32[]{:S(2)}, u32[]{:S(2)}) collective-permute-start(f32[8,32,128]{2,1,0:T(8,128)S(1)} %get-tuple-element.95.refs_0_), channel_id=1, source_target_pairs={{0,4},{4,0},{8,12},{12,8},{16,20},{20,16},{24,28},{28,24},{1,5},{5... | collective-permute-start | bytes 393224 | tf_op jit(solution)/shard_map/ppermute | solution.py:209
  141.3 8.6 %collective-permute-start.52 = (f32[8,32,128]{2,1,0:T(8,128)S(1)}, f32[8,32,128]{2,1,0:T(8,128)S(1)}, u32[]{:S(2)}, u32[]{:S(2)}) collective-permute-start(f32[8,32,128]{2,1,0:T(8,128)S(1)} %add_multiply_fusion.refs_0_), channel_id=1, source_target_pairs={{0,8},{4,12},{8,0},{12,4},{16,24},{20,28},{24,16},{28,20},{1,9},{5... | collective-permute-start | bytes 393224 | tf_op jit(solution)/shard_map/ppermute | solution.py:209
  150.4 10.5 %collective-permute-start.55 = (f32[8,32,128]{2,1,0:T(8,128)S(1)}, f32[8,32,128]{2,1,0:T(8,128)S(1)}, u32[]{:S(2)}, u32[]{:S(2)}) collective-permute-start(f32[8,32,128]{2,1,0:T(8,128)S(1)} %get-tuple-element.82), channel_id=1, source_target_pairs={{1,2},{2,1},{5,6},{6,5},{9,10},{10,9},{13,14},{14,13},{17,18},{18,... | collective-permute-start | bytes 393224 | tf_op jit(solution)/shard_map/ppermute | solution.py:216
  151.1 9.8 %collective-permute-start.54 = (f32[8,32,128]{2,1,0:T(8,128)S(1)}, f32[8,32,128]{2,1,0:T(8,128)S(1)}, u32[]{:S(2)}, u32[]{:S(2)}) collective-permute-start(f32[8,32,128]{2,1,0:T(8,128)S(1)} %get-tuple-element.83), channel_id=1, source_target_pairs={{0,1},{1,0},{2,3},{3,2},{4,5},{5,4},{6,7},{7,6},{8,9},{9,8},{10,11... | collective-permute-start | bytes 393224 | tf_op jit(solution)/shard_map/ppermute | solution.py:212
  157.4 7.7 %collective-permute-start.28 = (f32[8,32,128]{2,1,0:T(8,128)S(1)}, f32[8,32,128]{2,1,0:T(8,128)S(1)}, u32[]{:S(2)}, u32[]{:S(2)}) collective-permute-start(f32[8,32,128]{2,1,0:T(8,128)S(1)} %get-tuple-element.51), channel_id=1, source_target_pairs={{0,4},{4,0},{8,12},{12,8},{16,20},{20,16},{24,28},{28,24},{1,5},{5... | collective-permute-start | bytes 393224 | tf_op jit(solution)/shard_map/ppermute | solution.py:209
  158.4 9.2 %collective-permute-start.29 = (f32[8,32,128]{2,1,0:T(8,128)S(1)}, f32[8,32,128]{2,1,0:T(8,128)S(1)}, u32[]{:S(2)}, u32[]{:S(2)}) collective-permute-start(f32[8,32,128]{2,1,0:T(8,128)S(1)} %get-tuple-element.52), channel_id=1, source_target_pairs={{0,8},{4,12},{8,0},{12,4},{16,24},{20,28},{24,16},{28,20},{1,9},{5... | collective-permute-start | bytes 393224 | tf_op jit(solution)/shard_map/ppermute | solution.py:209
  158.4 9.2 %collective-permute-start.30 = (f32[8,32,128]{2,1,0:T(8,128)S(1)}, f32[8,32,128]{2,1,0:T(8,128)S(1)}, u32[]{:S(2)}, u32[]{:S(2)}) collective-permute-start(f32[8,32,128]{2,1,0:T(8,128)S(1)} %get-tuple-element.53), channel_id=1, source_target_pairs={{0,12},{4,8},{8,4},{12,0},{16,28},{20,24},{24,20},{28,16},{1,13},{... | collective-permute-start | bytes 393224 | tf_op jit(solution)/shard_map/ppermute | solution.py:209
  165.1 9.0 %collective-permute-start.58 = (f32[8,32,128]{2,1,0:T(8,128)S(1)}, f32[8,32,128]{2,1,0:T(8,128)S(1)}, u32[]{:S(2)}, u32[]{:S(2)}) collective-permute-start(f32[8,32,128]{2,1,0:T(8,128)S(1)} %get-tuple-element.68), channel_id=1, source_target_pairs={{0,12},{4,8},{8,4},{12,0},{16,28},{20,24},{24,20},{28,16},{1,13},{... | collective-permute-start | bytes 393224 | tf_op jit(solution)/shard_map/ppermute | solution.py:209
  167.7 7.6 %collective-permute-start.31 = (f32[4,32,128]{2,1,0:T(8,128)S(1)}, f32[4,32,128]{2,1,0:T(8,128)S(1)}, u32[]{:S(2)}, u32[]{:S(2)}) collective-permute-start(f32[4,32,128]{2,1,0:T(8,128)S(1)} %slice.99), channel_id=1, source_target_pairs={{0,16},{4,20},{8,24},{12,28},{16,0},{20,4},{24,8},{28,12},{1,17},{... | collective-permute-start | bytes 196616 | tf_op jit(solution)/shard_map/ppermute | solution.py:209
  (53 other events, 432.0 us)

commit v3 on v2

--- a/solution.py
+++ b/solution.py
@@ -10,7 +10,7 @@
 STEPS = 3
 CHAINS = 2
 GROUP = 16
-VMEM_BYTES = 40 << 20
+VMEM_BYTES = 16 << 20
 
 shift_term = -0.25
 half_width = 0.75
@@ -21,16 +21,13 @@
     return high, (x - high.astype(jnp.float32)).astype(jnp.bfloat16)
 
 
-def prepare_kernel(rows_ref, live_ref, vals_hbm, cat_hbm, degree_ref, vals_ref, cat_ref, in_sems, out_sems):
+def prepare_kernel(rows_ref, live_ref, vals_hbm, cat_ref, degree_ref, vals_ref, sems):
     slots, tile, _ = vals_ref.shape
-    groups = [pl.ds(g * GROUP, GROUP) for g in range(slots // GROUP)]
     loads = [
-        pltpu.make_async_copy(vals_hbm.at[g], vals_ref.at[g], in_sems.at[i])
-        for i, g in enumerate(groups)
-    ]
-    stores = [
-        pltpu.make_async_copy(cat_ref.at[g], cat_hbm.at[g], out_sems.at[i])
-        for i, g in enumerate(groups)
+        pltpu.make_async_copy(
+            vals_hbm.at[pl.ds(g * GROUP, GROUP)], vals_ref.at[pl.ds(g * GROUP, GROUP)], sems.at[g]
+        )
+        for g in range(slots // GROUP)
     ]
     for load in loads:
         load.start()
@@ -47,28 +44,22 @@
             ones, cat_ref[slot], (((1,), (1,)), ((), ())), preferred_element_type=jnp.float32
         )
         degree_ref[pl.ds(rows_ref[slot], 1), :] += sums[:1]
-        if slot % GROUP == GROUP - 1:
-            stores[slot // GROUP].start()
-    for store in stores:
-        store.wait()
 
 
 def prepare_tiles(tile_vals, row_local, live_count, group_blocks):
     slots, tile, _ = tile_vals.shape
     smem = pl.BlockSpec(memory_space=pltpu.SMEM)
-    hbm = pl.BlockSpec(memory_space=pltpu.HBM)
+    vmem = pl.BlockSpec(memory_space=pltpu.VMEM)
     return pl.pallas_call(
         prepare_kernel,
-        in_specs=[smem, smem, hbm],
-        out_specs=[hbm, pl.BlockSpec(memory_space=pltpu.VMEM)],
+        in_specs=[smem, smem, pl.BlockSpec(memory_space=pl.ANY)],
+        out_specs=[vmem, vmem],
         out_shape=[
-            jax.ShapeDtypeStruct((slots, tile, 2 * tile), jnp.bfloat16),
+            pltpu.VMEM((slots, tile, 2 * tile), jnp.bfloat16),
             jax.ShapeDtypeStruct((group_blocks, tile), jnp.float32),
         ],
         scratch_shapes=[
             pltpu.VMEM(tile_vals.shape, jnp.float32),
-            pltpu.VMEM((slots, tile, 2 * tile), jnp.bfloat16),
-            pltpu.SemaphoreType.DMA((slots // GROUP,)),
             pltpu.SemaphoreType.DMA((slots // GROUP,)),
         ],
         compiler_params=pltpu.CompilerParams(vmem_limit_bytes=VMEM_BYTES),
@@ -76,7 +67,7 @@
             flops=2_000_000_000, bytes_accessed=2 * tile_vals.size * 4, transcendentals=0
         ),
         name="prepare_tiles",
-    )(row_local, live_count, tile_vals)
+    )(row_local, live_count, pltpu.with_memory_space_constraint(tile_vals, pltpu.HBM))
 
 
 def store_split(cat_ref, slot, value):
@@ -97,21 +88,13 @@
     else:
         last_ref = refs.pop(0)
         older_ref = refs.pop(0) if kind == "third" else None
-    tiles_hbm, state_ref = refs.pop(0), refs.pop(0)
+    tiles_ref, state_ref = refs.pop(0), refs.pop(0)
     parts = [refs.pop(0) for _ in range(pieces_count)]
-    cat_ref, total_ref, tiles_ref, sems = refs
+    cat_ref, total_ref = refs
     width, tile = state_ref.shape[1:]
     reach = near.shape[0]
     part = total_ref.shape[0] // pieces_count
     slots = tiles_ref.shape[0]
-    copies = [
-        pltpu.make_async_copy(
-            tiles_hbm.at[pl.ds(g * GROUP, GROUP)], tiles_ref.at[pl.ds(g * GROUP, GROUP)], sems.at[g]
-        )
-        for g in range(slots // GROUP)
-    ]
-    for copy in copies:
-        copy.start()
     total_ref[...] = jnp.zeros_like(total_ref)
     quad, high, odd = place_ref[0], place_ref[1], place_ref[2]
 
@@ -143,8 +126,6 @@
         advance(jnp.where(odd == 1, span, 0) + j, far[j])
 
     for slot in range(slots):
-        if slot % GROUP == 0:
-            copies[slot // GROUP].wait()
         both = lax.dot_general(
             cat_ref[cols_ref[slot]],
             tiles_ref[slot],
@@ -170,13 +151,11 @@
         functools.partial(
             product_kernel, kind=kind, pieces_count=count, outer_half=outer_half
         ),
-        in_specs=[smem] * 3 + [vmem] * len(operands) + [pl.BlockSpec(memory_space=pltpu.HBM)],
+        in_specs=[smem] * 3 + [vmem] * (len(operands) + 1),
         out_specs=[vmem] * (1 + count),
         scratch_shapes=[
             pltpu.VMEM((window, 2 * width, 2 * tile), jnp.bfloat16),
             pltpu.VMEM((group_blocks, width, tile), jnp.float32),
-            pltpu.VMEM(tiles.shape, tiles.dtype),
-            pltpu.SemaphoreType.DMA((slots // GROUP,)),
         ],
         out_shape=[jax.ShapeDtypeStruct((window, width, tile), jnp.float32)]
         + [jax.ShapeDtypeStruct((part, width, tile), jnp.float32)] * count,
@@ -185,7 +164,124 @@
             flops=3_000_000_000, bytes_accessed=slots * tile * tile * 4, transcendentals=0
         ),
         name="products_" + kind,
-    )(cols, rows, place, *operands, tiles)
+    )(cols, rows, place, *operands, pltpu.with_memory_space_constraint(tiles, pltpu.VMEM))
+
+
+def gram_kernel(place_ref, *refs, chains, own):
+    refs = list(refs)
+    groups = [[refs.pop(0) for _ in range(4)] for _ in range(chains)]
+    degree_ref, filtered_ref, gram_ref, all_ref = refs
+    halves = groups[0][0].shape[0] // own
+    width = groups[0][0].shape[1]
+    for h in range(halves):
+        for j in range(own):
+            block = place_ref[h] + j
+            degree = degree_ref[pl.ds(block, 1), :]
+            for c, (mine, other, last, older) in enumerate(groups):
+                total = mine[h * own + j] + other[(halves - 1 - h) * own + j]
+                slot = place_ref[halves] + block
+                value = (2.0 / half_width) * (shift_term * last[slot] - total / degree)
+                value = (value - older[slot]) * jnp.sqrt(degree)
+                all_ref[h * own + j, c * width : (c + 1) * width, :] = value
+                if h == 0:
+                    filtered_ref[j, c * width : (c + 1) * width, :] = value
+    gram = jnp.zeros(gram_ref.shape, jnp.float32)
+    for i in range(halves * own):
+        block = all_ref[i]
+        gram += lax.dot_general(
+            block,
+            block,
+            (((1,), (1,)), ((), ())),
+            precision=lax.Precision.HIGHEST,
+            preferred_element_type=jnp.float32,
+        )
+    gram_ref[...] = gram
+
+
+def gram_of(place, groups, degree, own):
+    part, width, tile = groups[0][0].shape
+    total = width * len(groups)
+    smem = pl.BlockSpec(memory_space=pltpu.SMEM)
+    vmem = pl.BlockSpec(memory_space=pltpu.VMEM)
+    operands = [x for group in groups for x in group] + [degree]
+    return pl.pallas_call(
+        functools.partial(gram_kernel, chains=len(groups), own=own),
+        in_specs=[smem] + [vmem] * len(operands),
+        out_specs=[vmem, vmem],
+        out_shape=[
+            jax.ShapeDtypeStruct((own, total, tile), jnp.float32),
+            jax.ShapeDtypeStruct((total, total), jnp.float32),
+        ],
+        scratch_shapes=[pltpu.VMEM((part, total, tile), jnp.float32)],
+        compiler_params=pltpu.CompilerParams(vmem_limit_bytes=VMEM_BYTES),
+        name="gram",
+    )(place, *operands)
+
+
+def solve_kernel(*refs, pieces, scale):
+    parts, filtered_ref, out_ref, work_ref = refs[:pieces], *refs[pieces:]
+    size = parts[0].shape[0]
+    tile = filtered_ref.shape[2]
+    gram = parts[0][...]
+    for part in parts[1:]:
+        gram = gram + part[...]
+    row = lax.broadcasted_iota(jnp.int32, (size, size), 0)
+    column = lax.broadcasted_iota(jnp.int32, (size, size), 1)
+    work_ref[:, :size] = gram * scale
+    work_ref[:, size:] = (row == column).astype(jnp.float32)
+    step = 8
+    wide = 2 * size
+    count = size // step
+    rows = [work_ref[step * i : step * (i + 1), :] for i in range(count)]
+    sub = lax.broadcasted_iota(jnp.int32, (step, wide), 0)
+
+    def spread_row(x, j):
+        return jnp.broadcast_to(x[j : j + 1, :], (step, wide))
+
+    for p in range(count):
+        columns = {
+            i: [
+                jnp.broadcast_to(rows[i][:, step * p + j : step * p + j + 1], (step, wide))
+                for j in range(step)
+            ]
+            for i in range(p, count)
+        }
+        for j in range(step):
+            root = lax.rsqrt(spread_row(columns[p][j], j))
+            pivot = spread_row(rows[p], j) * root
+            heads = {k: spread_row(columns[p][k], j) * root for k in range(j + 1, step)}
+            for i in range(p, count):
+                factor = columns[i][j] * root
+                if i == p:
+                    factor = jnp.where(sub > j, factor, 0.0)
+                rows[i] = rows[i] - factor * pivot
+                for k in range(j + 1, step):
+                    columns[i][k] = columns[i][k] - factor * heads[k]
+            rows[p] = jnp.where(sub == j, pivot, rows[p])
+        work_ref[step * p : step * (p + 1), :] = rows[p]
+    inverse = work_ref[:, size:]
+    for j in range(filtered_ref.shape[0]):
+        out_ref[:, j * tile : (j + 1) * tile] = lax.dot_general(
+            inverse,
+            filtered_ref[j],
+            (((1,), (0,)), ((), ())),
+            precision=lax.Precision.HIGHEST,
+            preferred_element_type=jnp.float32,
+        )
+
+
+def solve(parts, filtered, scale):
+    own, total, tile = filtered.shape
+    vmem = pl.BlockSpec(memory_space=pltpu.VMEM)
+    return pl.pallas_call(
+        functools.partial(solve_kernel, pieces=len(parts), scale=scale),
+        in_specs=[vmem] * (len(parts) + 1),
+        out_specs=vmem,
+        out_shape=jax.ShapeDtypeStruct((total, own * tile), jnp.float32),
+        scratch_shapes=[pltpu.VMEM((total, 2 * total), jnp.float32)],
+        compiler_params=pltpu.CompilerParams(vmem_limit_bytes=VMEM_BYTES),
+        name="solve",
+    )(*parts, filtered)
 
 
 def on_device(start_block, tile_vals, tile_rows, tile_cols, tile_count):
@@ -224,6 +320,9 @@
             total = total + over_blk(parts[k], k)
         return total
 
+    def after(x, y):
+        return lax.optimization_barrier((x, y))[0]
+
     def all_sum(x):
         return x + over_blk(x, quad_count)
 
@@ -237,9 +336,9 @@
 
     blocks = start_block.reshape(vec_width, own, tile).transpose(1, 0, 2)
     chains = jnp.split(blocks, CHAINS, axis=1)
-    gathered = [
-        spread(jnp.concatenate([chain, over_blk(chain, quad_count)])) for chain in chains
-    ]
+    others = [over_blk(chain, quad_count) for chain in chains]
+    gathered = [spread(jnp.concatenate(pair)) for pair in zip(chains, others)]
+    tile_vals = after(tile_vals, others[0])
 
     tiles, degree = prepare_tiles(tile_vals, row_local, tile_count.reshape(1), group_blocks)
     degree = all_sum(sum(spread(degree)))
@@ -282,38 +381,59 @@
         states[c].append(state)
 
     for index in range(1, STEPS):
+        kind = "second" if index == 1 else "third"
+        rows = rows_last if index == STEPS - 1 else rows_flat
+        first_sums = [gather_sum(parts[c]) for c in range(CHAINS)]
+        for c in range(CHAINS - 1):
+            first_sums[c] = after(first_sums[c], parts[c + 1][0])
+        totals = [all_sum(x) * inv_part for x in first_sums]
+        for c in range(CHAINS - 1):
+            totals[c] = after(totals[c], first_sums[c + 1])
+        pieces = []
         for c in range(CHAINS):
-            total = all_sum(gather_sum(parts[c])) * inv_part
-            pieces = spread(total)
-            near, far = halos(functools.partial(later_blocks, pieces))
-            kind = "second" if index == 1 else "third"
-            extra = [states[c][-1]] if index == 1 else [states[c][-1], states[c][-2]]
-            rows = rows_last if index == STEPS - 1 else rows_flat
+            if c:
+                totals[c] = after(totals[c], pieces[c - 1][1])
+            pieces.append(spread(totals[c]))
+        for c in range(CHAINS):
+            mine = pieces[c] if c == CHAINS - 1 else after(pieces[c], totals[c + 1])
+            near, far = halos(functools.partial(later_blocks, mine))
+            if c < CHAINS - 1:
+                near = after(near, pieces[c + 1][1:])
             state, *parts[c] = tile_products(
-                kind, col_local, rows, place, pieces, near, far, extra, tiles, high_count
+                kind, col_local, rows, place, mine, near, far,
+                [states[c][-1 - i] for i in range(index)], tiles, high_count,
             )
             states[c].append(state)
 
-    own_degree = lax.dynamic_slice_in_dim(degree, blk_index * own, own, 0)[:, None, :]
-    start = reach + blk_index * own
-    filtered = []
-    for c in range(CHAINS):
-        total = gather_sum(parts[c])
-        own_sum = total[:own] + over_blk(total[own:], quad_count)
-        last = lax.dynamic_slice_in_dim(states[c][-1], start, own, 0)
-        older = lax.dynamic_slice_in_dim(states[c][-2], start, own, 0)
-        scaled = (2.0 / half_width) * (shift_term * last - own_sum / own_degree) - older
-        filtered.append(scaled * jnp.sqrt(own_degree))
-    current = jnp.concatenate(filtered, axis=1).transpose(1, 0, 2).reshape(vec_width, local_rows)
-
-    gram_sum = jnp.dot(current, current.T, precision=lax.Precision.HIGHEST) / rows_total
-    bit = 1
-    while bit < row_count:
-        gram_sum = gram_sum + over_rows(gram_sum, bit)
-        bit *= 2
-    gram_sum = all_sum(sum(spread(gram_sum)))
-    factor = jnp.linalg.cholesky(gram_sum, symmetrize_input=False)
-    return lax.linalg.triangular_solve(factor, current, left_side=True, lower=True)
+    last_sums = [gather_sum(parts[c]) for c in range(CHAINS)]
+    groups = [
+        [last_sums[c], over_blk(last_sums[c], quad_count), states[c][-1], states[c][-2]]
+        for c in range(CHAINS)
+    ]
+    offsets = [((h ^ high) * quad_count + quad) * own for h in range(high_count)]
+    gram_place = jnp.stack([*offsets, jnp.full((), reach, offsets[0].dtype)]).astype(jnp.int32)
+    filtered, gram = gram_of(gram_place, groups, degree, own)
+
+    def over_all(x, rows_bit, blk_bit):
+        pairs = [
+            (i * row_count + j, (i ^ blk_bit) * row_count + (j ^ rows_bit))
+            for i in range(blk_count)
+            for j in range(row_count)
+        ]
+        return lax.ppermute(x, ("blk", "rows"), pairs)
+
+    bits = [(1 << i, 0) for i in range(1, row_count.bit_length() - 1)]
+    bits += [(0, 1 << i) for i in range(quad_count.bit_length() - 1)]
+    stages = [[(1, 0)]]
+    while bits:
+        first, *second = bits[:2]
+        bits = bits[2:]
+        stages.append([first] + [x for y in second for x in (y, (first[0] ^ y[0], first[1] ^ y[1]))])
+    pieces = [gram]
+    for stage in stages:
+        gram = sum(pieces[1:], pieces[0])
+        pieces = [gram] + [over_all(gram, *bit) for bit in stage]
+    return solve(pieces, filtered, 1.0 / rows_total)
 
 
 def solution(mesh):

time: 210 us -> 181 us (0.86)
  other arithmetic: 14.4 us -> 1.74 us
  starting transfers between devices: 81.2 us -> 70.4 us
  local copies, waits for them, and re-layouts: 9.32 us -> 4.27 us
    another operation x5 -> x1, other arithmetic: 12.1 us -> 0.08 us  [on_device(): jnp.stack([*offsets, jnp.full((), reach, offsets[0].dtype)])]
    ppermute x8 -> x6, starting transfers between devices: 15.9 us -> 4.54 us  [over_rows(): return lax.ppermute(x, 'rows', [(i, i ^ k) for i in range(row_count)])]
    ppermute x0 -> x5, waiting for transfers between devices: none -> 7.28 us  [over_all(): return lax.ppermute(x, ('blk', 'rows'), pairs)]
    pallas_call x1 -> x3, Pallas kernels: 2.87 us -> 7.84 us  [the longest x1 3.5 us: prepare_tiles(): pl.pallas_call(prepare_kernel, in_specs=[smem, smem, pl.BlockSpec(memory_...]
    ppermute x8 -> x6, waiting for transfers between devices: 4.55 us -> 0.02 us  [over_rows(): return lax.ppermute(x, 'rows', [(i, i ^ k) for i in range(row_count)])]
    unnamed x22 -> x18, local copies, waits for them, and re-layouts: 8.6 us -> 4.25 us
    pallas_call x6, Pallas kernels: 18.5 us -> 14.2 us  [tile_products(): pl.pallas_call(functools.partial(product_kernel, kind=kind, pieces_count=...]
    ppermute x0 -> x5, starting transfers between devices: none -> 3.64 us  [over_all(): return lax.ppermute(x, ('blk', 'rows'), pairs)]
  transfers between devices with their start and end apart: 66 -> 65, of which waited for: 41 -> 34; matrix products, arithmetic and copies ran while one was open for 1% -> 1% of each run, Pallas kernels for 6% -> 10%
where the time goes in v3:
time: 181 us
  waiting for transfers between devices  80.7 us (45%)
  starting transfers between devices  70.4 us (39%)
  Pallas kernels  22 us (12%)
  local copies, waits for them, and re-layouts  4.27 us (2%)
    ppermute x48, waiting for transfers between devices, over_blk(): return lax.ppermute(x, 'blk', [(i, i ^ k) for i in range(blk_count)])  73.4 us
    ppermute x48, starting transfers between devices, over_blk(): return lax.ppermute(x, 'blk', [(i, i ^ k) for i in range(blk_count)])  58 us
    pallas_call x6, Pallas kernels, tile_products(): pl.pallas_call(functools.partial(product_kernel, kind=kind, pieces_count=...  14.2 us
    ppermute x5, waiting for transfers between devices, over_all(): return lax.ppermute(x, ('blk', 'rows'), pairs)  7.28 us
    ppermute x6, starting transfers between devices, over_rows(): return lax.ppermute(x, 'rows', [(i, i ^ k) for i in range(row_count)])  4.54 us
    unnamed x18, local copies, waits for them, and re-layouts  4.25 us
    ppermute x6, starting transfers between devices, with_far(): return lax.ppermute(x, 'rows', pairs + [(b, a) for a, b in pairs])  4.17 us
    ppermute x5, starting transfers between devices, over_all(): return lax.ppermute(x, ('blk', 'rows'), pairs)  3.64 us
  transfers between devices with their start and end apart: 65, of which 34 were waited for; matrix products, arithmetic and copies ran while one was open for 1% of the time, Pallas kernels for 10%

profile of v3, /device:TPU:0, one launch (start us, length us, event | category | flops | bytes accessed | tf_op | source)
XLA Modules:
  0.0 180.5 jit_solution(11651779977514270466)
XLA Ops:
  0.9 4.1 %collective-permute-start = (f32[4,32,128]{2,1,0:T(8,128)S(1)}, f32[4,32,128]{2,1,0:T(8,128)S(1)}, u32[]{:S(2)}, u32[]{:S(2)}) collective-permute-start(f32[4,32,128]{2,1,0:T(8,128)S(1)} %get-tuple-element.126), channel_id=1, source_target_pairs={{0,16},{4,20},{8,24},{12,28},{16,0},{20,4},{24,8},{28,12},{1,17},{... | collective-permute-start | bytes 196616 | tf_op jit(solution)/shard_map/ppermute | solution.py:305
  8.7 3.5 %prepare_tiles.1 = (bf16[64,128,256]{2,1,0:T(8,128)(2,1)S(1)}, f32[32,128]{1,0:T(8,128)S(1)}) custom-call(s32[64]{0:T(128)S(1)} %get-tuple-element.110.rows_ref, s32[1]{0:T(128)} %bitcast.13.live_ref, f32[64,128,128]{2,1,0:T(8,128)} %vals_hbm), custom_call_target="tpu_custom_call" | custom-call | flops 2000000000 | bytes 8388608 | tf_op jit(solution)/shard_map/prepare_tiles/pallas_call | solution.py:53
  20.8 3.4 %collective-permute-start.7 = (f32[32,128]{1,0:T(8,128)S(1)}, f32[32,128]{1,0:T(8,128)S(1)}, u32[]{:S(2)}, u32[]{:S(2)}) collective-permute-start(f32[32,128]{1,0:T(8,128)S(1)} %add_add_fusion.7), channel_id=1, source_target_pairs={{0,16},{4,20},{8,24},{12,28},{16,0},{20,4},{24,8},{28,12},{1,17},{... | collective-permute-start | bytes 49160 | tf_op jit(solution)/shard_map/ppermute | solution.py:305
  25.9 2.8 %collective-permute-start.15 = (f32[8,32,128]{2,1,0:T(8,128)S(1)}, f32[8,32,128]{2,1,0:T(8,128)S(1)}, u32[]{:S(2)}, u32[]{:S(2)}) collective-permute-start(f32[8,32,128]{2,1,0:T(8,128)S(1)} %pad_maximum_fusion.1.refs_0_), channel_id=1, source_target_pairs={{0,8},{4,12},{8,0},{12,4},{16,24},{20,28},{24,16},{28,20},{1,9},{5... | collective-permute-start | bytes 393224 | tf_op jit(solution)/shard_map/ppermute | solution.py:305
  29.3 3.4 %collective-permute-done.15.refs_2_ = f32[8,32,128]{2,1,0:T(8,128)S(1)} collective-permute-done((f32[8,32,128]{2,1,0:T(8,128)S(1)}, f32[8,32,128]{2,1,0:T(8,128)S(1)}, u32[]{:S(2)}, u32[]{:S(2)}) %collective-permute-start.15) | collective-permute-done | bytes 131104 | tf_op jit(solution)/shard_map/ppermute | solution.py:305
  35.7 2.9 %collective-permute-start.8 = (f32[8,32,128]{2,1,0:T(8,128)S(1)}, f32[8,32,128]{2,1,0:T(8,128)S(1)}, u32[]{:S(2)}, u32[]{:S(2)}) collective-permute-start(f32[8,32,128]{2,1,0:T(8,128)S(1)} %get-tuple-element.136), channel_id=1, source_target_pairs={{0,1},{1,0},{2,3},{3,2},{4,5},{5,4},{6,7},{7,6},{8,9},{9,8},{10,11... | collective-permute-start | bytes 393224 | tf_op jit(solution)/shard_map/ppermute | solution.py:308
  46.6 2.4 %products_first.3 = (f32[48,32,128]{2,1,0:T(8,128)S(1)}, f32[8,32,128]{2,1,0:T(8,128)S(1)}, f32[8,32,128]{2,1,0:T(8,128)S(1)}, f32[8,32,128]{2,1,0:T(8,128)S(1)}, f32[8,32,128]{2,1,0:T(8,128)S(1)}) custom-call(s32[64]{0:T(128)S(1)} %broadcast_subtract_fusion.1.cols_ref, s32[64]{0:T(128)S(1)} %get-tuple-element.109.rows_ref, s32[3]{0:T(128)S(1)} %pad_add_fusion.1.place_ref, ...), custom_call_target="tpu_custom_call" | custom-call | flops 3000000000 | bytes 4194304 | tf_op jit(solution)/shard_map/products_first/pallas_call | solution.py:150
  57.9 3.0 %collective-permute-done.22 = f32[8,32,128]{2,1,0:T(8,128)S(1)} collective-permute-done((f32[8,32,128]{2,1,0:T(8,128)S(1)}, f32[8,32,128]{2,1,0:T(8,128)S(1)}, u32[]{:S(2)}, u32[]{:S(2)}) %collective-permute-start.22) | collective-permute-done | bytes 131104 | tf_op jit(solution)/shard_map/ppermute | solution.py:305
  61.8 5.9 %collective-permute-done.26 = f32[8,32,128]{2,1,0:T(8,128)S(1)} collective-permute-done((f32[8,32,128]{2,1,0:T(8,128)S(1)}, f32[8,32,128]{2,1,0:T(8,128)S(1)}, u32[]{:S(2)}, u32[]{:S(2)}) %collective-permute-start.26) | collective-permute-done | bytes 131104 | tf_op jit(solution)/shard_map/ppermute | solution.py:305
  68.6 2.7 %collective-permute-start.25 = (f32[8,32,128]{2,1,0:T(8,128)S(1)}, f32[8,32,128]{2,1,0:T(8,128)S(1)}, u32[]{:S(2)}, u32[]{:S(2)}) collective-permute-start(f32[8,32,128]{2,1,0:T(8,128)S(1)} %get-tuple-element.70.refs_0_), channel_id=1, source_target_pairs={{0,12},{4,8},{8,4},{12,0},{16,28},{20,24},{24,20},{28,16},{1,13},{... | collective-permute-start | bytes 393224 | tf_op jit(solution)/shard_map/ppermute | solution.py:305
  71.3 2.9 %collective-permute-done.23.refs_1_ = f32[8,32,128]{2,1,0:T(8,128)S(1)} collective-permute-done((f32[8,32,128]{2,1,0:T(8,128)S(1)}, f32[8,32,128]{2,1,0:T(8,128)S(1)}, u32[]{:S(2)}, u32[]{:S(2)}) %collective-permute-start.23) | collective-permute-done | bytes 131104 | tf_op jit(solution)/shard_map/ppermute | solution.py:305
  83.0 2.8 %collective-permute-done.30.refs_3_ = f32[8,32,128]{2,1,0:T(8,128)S(1)} collective-permute-done((f32[8,32,128]{2,1,0:T(8,128)S(1)}, f32[8,32,128]{2,1,0:T(8,128)S(1)}, u32[]{:S(2)}, u32[]{:S(2)}) %collective-permute-start.30) | collective-permute-done | bytes 131104 | tf_op jit(solution)/shard_map/ppermute | solution.py:305
  103.1 3.4 %collective-permute-done.38 = f32[8,32,128]{2,1,0:T(8,128)S(1)} collective-permute-done((f32[8,32,128]{2,1,0:T(8,128)S(1)}, f32[8,32,128]{2,1,0:T(8,128)S(1)}, u32[]{:S(2)}, u32[]{:S(2)}) %collective-permute-start.38) | collective-permute-done | bytes 131104 | tf_op jit(solution)/shard_map/ppermute | solution.py:305
  106.5 4.2 %collective-permute-done.40 = f32[8,32,128]{2,1,0:T(8,128)S(1)} collective-permute-done((f32[8,32,128]{2,1,0:T(8,128)S(1)}, f32[8,32,128]{2,1,0:T(8,128)S(1)}, u32[]{:S(2)}, u32[]{:S(2)}) %collective-permute-start.40) | collective-permute-done | bytes 131104 | tf_op jit(solution)/shard_map/ppermute | solution.py:305
  110.8 8.5 %collective-permute-done.44 = f32[8,32,128]{2,1,0:T(8,128)S(1)} collective-permute-done((f32[8,32,128]{2,1,0:T(8,128)S(1)}, f32[8,32,128]{2,1,0:T(8,128)S(1)}, u32[]{:S(2)}, u32[]{:S(2)}) %collective-permute-start.44) | collective-permute-done | bytes 131104 | tf_op jit(solution)/shard_map/ppermute | solution.py:305
  120.5 2.4 %collective-permute-start.43 = (f32[8,32,128]{2,1,0:T(8,128)S(1)}, f32[8,32,128]{2,1,0:T(8,128)S(1)}, u32[]{:S(2)}, u32[]{:S(2)}) collective-permute-start(f32[8,32,128]{2,1,0:T(8,128)S(1)} %get-tuple-element.88.refs_0_), channel_id=1, source_target_pairs={{0,12},{4,8},{8,4},{12,0},{16,28},{20,24},{24,20},{28,16},{1,13},{... | collective-permute-start | bytes 393224 | tf_op jit(solution)/shard_map/ppermute | solution.py:305
  126.0 2.4 %collective-permute-start.48 = (f32[8,32,128]{2,1,0:T(8,128)S(1)}, f32[8,32,128]{2,1,0:T(8,128)S(1)}, u32[]{:S(2)}, u32[]{:S(2)}) collective-permute-start(f32[8,32,128]{2,1,0:T(8,128)S(1)} %get-tuple-element.87.refs_0_), channel_id=1, source_target_pairs={{0,12},{4,8},{8,4},{12,0},{16,28},{20,24},{24,20},{28,16},{1,13},{... | collective-permute-start | bytes 393224 | tf_op jit(solution)/shard_map/ppermute | solution.py:305
  135.6 2.4 %products_third.2 = (f32[48,32,128]{2,1,0:T(8,128)S(1)}, f32[8,32,128]{2,1,0:T(8,128)S(1)}, f32[8,32,128]{2,1,0:T(8,128)S(1)}, f32[8,32,128]{2,1,0:T(8,128)S(1)}, f32[8,32,128]{2,1,0:T(8,128)S(1)}) custom-call(s32[64]{0:T(128)S(1)} %broadcast_subtract_fusion.1.cols_ref, s32[64]{0:T(128)S(1)} %fusion.rows_ref, s32[3]{0:T(128)S(1)} %pad_add_fusion.1.place_ref, ...), custom_call_target="tpu_custom_call" | custom-call | flops 3000000000 | bytes 4194304 | tf_op jit(solution)/shard_map/products_third/pallas_call | solution.py:150
  141.5 2.4 %products_third.3 = (f32[48,32,128]{2,1,0:T(8,128)S(1)}, f32[8,32,128]{2,1,0:T(8,128)S(1)}, f32[8,32,128]{2,1,0:T(8,128)S(1)}, f32[8,32,128]{2,1,0:T(8,128)S(1)}, f32[8,32,128]{2,1,0:T(8,128)S(1)}) custom-call(s32[64]{0:T(128)S(1)} %broadcast_subtract_fusion.1.cols_ref, s32[64]{0:T(128)S(1)} %fusion.rows_ref, s32[3]{0:T(128)S(1)} %pad_add_fusion.1.place_ref, ...), custom_call_target="tpu_custom_call" | custom-call | flops 3000000000 | bytes 4194304 | tf_op jit(solution)/shard_map/products_third/pallas_call | solution.py:150
  151.8 4.9 %collective-permute-done.58 = f32[8,32,128]{2,1,0:T(8,128)S(1)} collective-permute-done((f32[8,32,128]{2,1,0:T(8,128)S(1)}, f32[8,32,128]{2,1,0:T(8,128)S(1)}, u32[]{:S(2)}, u32[]{:S(2)}) %collective-permute-start.58) | collective-permute-done | bytes 131104 | tf_op jit(solution)/shard_map/ppermute | solution.py:305
  157.9 7.3 %collective-permute-done.59.refs_5_ = f32[8,32,128]{2,1,0:T(8,128)} collective-permute-done((f32[8,32,128]{2,1,0:T(8,128)S(1)}, f32[8,32,128]{2,1,0:T(8,128)}, u32[]{:S(2)}, u32[]{:S(2)}) %collective-permute-start.59) | collective-permute-done | bytes 131104 | tf_op jit(solution)/shard_map/ppermute | solution.py:305
  168.9 2.6 %collective-permute-start.63 = (f32[64,64]{1,0:T(8,128)S(1)}, f32[64,64]{1,0:T(8,128)S(1)}, u32[]{:S(2)}, u32[]{:S(2)}) collective-permute-start(f32[64,64]{1,0:T(8,128)S(1)} %add.214), channel_id=1, source_target_pairs={{0,6},{1,7},{2,4},{3,5},{4,2},{5,3},{6,0},{7,1},{8,14},{9,15},{10,... | collective-permute-start | bytes 49160 | tf_op jit(solution)/shard_map/ppermute | solution.py:423
  173.8 3.9 %collective-permute-done.64.refs_1_ = f32[64,64]{1,0:T(8,128)S(1)} collective-permute-done((f32[64,64]{1,0:T(8,128)S(1)}, f32[64,64]{1,0:T(8,128)S(1)}, u32[]{:S(2)}, u32[]{:S(2)}) %collective-permute-start.64) | collective-permute-done | bytes 16416 | tf_op jit(solution)/shard_map/ppermute | solution.py:423
  177.7 2.8 %solve.1 = f32[64,512]{1,0:T(8,128)} custom-call(f32[64,64]{1,0:T(8,128)S(1)} %add_add_fusion.6.refs_0_, f32[64,64]{1,0:T(8,128)S(1)} %collective-permute-done.64.refs_1_, f32[4,64,128]{2,1,0:T(8,128)S(1)} %get-tuple-element.106.refs_2_), custom_call_target="tpu_custom_call" | custom-call | tf_op jit(solution)/shard_map/solve/pallas_call | solution.py:276
  (170 shorter events, 92.2 us)
Async XLA Ops:
  5.0 19.1 %collective-permute-start.13 = (f32[4,32,128]{2,1,0:T(8,128)S(1)}, f32[4,32,128]{2,1,0:T(8,128)S(1)}, u32[]{:S(2)}, u32[]{:S(2)}) collective-permute-start(f32[4,32,128]{2,1,0:T(8,128)S(1)} %get-tuple-element.125), channel_id=1, source_target_pairs={{0,16},{4,20},{8,24},{12,28},{16,0},{20,4},{24,8},{28,12},{1,17},{... | collective-permute-start | bytes 196616 | tf_op jit(solution)/shard_map/ppermute | solution.py:305
  15.9 12.9 %collective-permute-start.1 = (f32[8,32,128]{2,1,0:T(8,128)S(1)}, f32[8,32,128]{2,1,0:T(8,128)S(1)}, u32[]{:S(2)}, u32[]{:S(2)}) collective-permute-start(f32[8,32,128]{2,1,0:T(8,128)S(1)} %pad_maximum_fusion.refs_0_), channel_id=1, source_target_pairs={{0,4},{4,0},{8,12},{12,8},{16,20},{20,16},{24,28},{28,24},{1,5},{5... | collective-permute-start | bytes 393224 | tf_op jit(solution)/shard_map/ppermute | solution.py:305
  17.8 11.3 %collective-permute-start.2 = (f32[8,32,128]{2,1,0:T(8,128)S(1)}, f32[8,32,128]{2,1,0:T(8,128)S(1)}, u32[]{:S(2)}, u32[]{:S(2)}) collective-permute-start(f32[8,32,128]{2,1,0:T(8,128)S(1)} %pad_maximum_fusion.refs_0_), channel_id=1, source_target_pairs={{0,8},{4,12},{8,0},{12,4},{16,24},{20,28},{24,16},{28,20},{1,9},{5... | collective-permute-start | bytes 393224 | tf_op jit(solution)/shard_map/ppermute | solution.py:305
  19.4 9.7 %collective-permute-start.3 = (f32[8,32,128]{2,1,0:T(8,128)S(1)}, f32[8,32,128]{2,1,0:T(8,128)S(1)}, u32[]{:S(2)}, u32[]{:S(2)}) collective-permute-start(f32[8,32,128]{2,1,0:T(8,128)S(1)} %pad_maximum_fusion.refs_0_), channel_id=1, source_target_pairs={{0,12},{4,8},{8,4},{12,0},{16,28},{20,24},{24,20},{28,16},{1,13},{... | collective-permute-start | bytes 393224 | tf_op jit(solution)/shard_map/ppermute | solution.py:305
  38.7 8.0 %collective-permute-start.18 = (f32[8,32,128]{2,1,0:T(8,128)S(1)}, f32[8,32,128]{2,1,0:T(8,128)S(1)}, u32[]{:S(2)}, u32[]{:S(2)}) collective-permute-start(f32[8,32,128]{2,1,0:T(8,128)S(1)} %get-tuple-element.133), channel_id=1, source_target_pairs={{1,2},{2,1},{5,6},{6,5},{9,10},{10,9},{13,14},{14,13},{17,18},{18,... | collective-permute-start | bytes 393224 | tf_op jit(solution)/shard_map/ppermute | solution.py:312
  44.1 8.5 %collective-permute-start.11 = (f32[8,32,128]{2,1,0:T(8,128)S(1)}, f32[8,32,128]{2,1,0:T(8,128)S(1)}, u32[]{:S(2)}, u32[]{:S(2)}) collective-permute-start(f32[8,32,128]{2,1,0:T(8,128)S(1)} %get-tuple-element.61), channel_id=1, source_target_pairs={{0,8},{4,12},{8,0},{12,4},{16,24},{20,28},{24,16},{28,20},{1,9},{5... | collective-permute-start | bytes 393224 | tf_op jit(solution)/shard_map/ppermute | solution.py:305
  45.0 8.2 %collective-permute-start.12 = (f32[8,32,128]{2,1,0:T(8,128)S(1)}, f32[8,32,128]{2,1,0:T(8,128)S(1)}, u32[]{:S(2)}, u32[]{:S(2)}) collective-permute-start(f32[8,32,128]{2,1,0:T(8,128)S(1)} %get-tuple-element.62), channel_id=1, source_target_pairs={{0,12},{4,8},{8,4},{12,0},{16,28},{20,24},{24,20},{28,16},{1,13},{... | collective-permute-start | bytes 393224 | tf_op jit(solution)/shard_map/ppermute | solution.py:305
  51.0 10.0 %collective-permute-start.22 = (f32[8,32,128]{2,1,0:T(8,128)S(1)}, f32[8,32,128]{2,1,0:T(8,128)S(1)}, u32[]{:S(2)}, u32[]{:S(2)}) collective-permute-start(f32[8,32,128]{2,1,0:T(8,128)S(1)} %get-tuple-element.67), channel_id=1, source_target_pairs={{0,12},{4,8},{8,4},{12,0},{16,28},{20,24},{24,20},{28,16},{1,13},{... | collective-permute-start | bytes 393224 | tf_op jit(solution)/shard_map/ppermute | solution.py:305
  53.3 8.5 %collective-permute-start.19 = (f32[8,32,128]{2,1,0:T(8,128)S(1)}, f32[8,32,128]{2,1,0:T(8,128)S(1)}, u32[]{:S(2)}, u32[]{:S(2)}) collective-permute-start(f32[8,32,128]{2,1,0:T(8,128)S(1)} %add_add_fusion.5), channel_id=1, source_target_pairs={{0,16},{4,20},{8,24},{12,28},{16,0},{20,4},{24,8},{28,12},{1,17},{... | collective-permute-start | bytes 393224 | tf_op jit(solution)/shard_map/ppermute | solution.py:305
  85.8 10.0 %collective-permute-start.35 = (f32[8,32,128]{2,1,0:T(8,128)S(1)}, f32[8,32,128]{2,1,0:T(8,128)S(1)}, u32[]{:S(2)}, u32[]{:S(2)}) collective-permute-start(f32[8,32,128]{2,1,0:T(8,128)S(1)} %get-tuple-element.116), channel_id=1, source_target_pairs={{0,1},{1,0},{2,3},{3,2},{4,5},{5,4},{6,7},{7,6},{8,9},{9,8},{10,11... | collective-permute-start | bytes 393224 | tf_op jit(solution)/shard_map/ppermute | solution.py:308
  85.9 9.9 %collective-permute-start.36 = (f32[8,32,128]{2,1,0:T(8,128)S(1)}, f32[8,32,128]{2,1,0:T(8,128)S(1)}, u32[]{:S(2)}, u32[]{:S(2)}) collective-permute-start(f32[8,32,128]{2,1,0:T(8,128)S(1)} %get-tuple-element.115), channel_id=1, source_target_pairs={{1,2},{2,1},{5,6},{6,5},{9,10},{10,9},{13,14},{14,13},{17,18},{18,... | collective-permute-start | bytes 393224 | tf_op jit(solution)/shard_map/ppermute | solution.py:312
  92.2 8.1 %collective-permute-start.32 = (f32[8,32,128]{2,1,0:T(8,128)S(1)}, f32[8,32,128]{2,1,0:T(8,128)S(1)}, u32[]{:S(2)}, u32[]{:S(2)}) collective-permute-start(f32[8,32,128]{2,1,0:T(8,128)S(1)} %get-tuple-element.77), channel_id=1, source_target_pairs={{0,4},{4,0},{8,12},{12,8},{16,20},{20,16},{24,28},{28,24},{1,5},{5... | collective-permute-start | bytes 393224 | tf_op jit(solution)/shard_map/ppermute | solution.py:305
  93.0 8.7 %collective-permute-start.33 = (f32[8,32,128]{2,1,0:T(8,128)S(1)}, f32[8,32,128]{2,1,0:T(8,128)S(1)}, u32[]{:S(2)}, u32[]{:S(2)}) collective-permute-start(f32[8,32,128]{2,1,0:T(8,128)S(1)} %get-tuple-element.78), channel_id=1, source_target_pairs={{0,8},{4,12},{8,0},{12,4},{16,24},{20,28},{24,16},{28,20},{1,9},{5... | collective-permute-start | bytes 393224 | tf_op jit(solution)/shard_map/ppermute | solution.py:305
  98.2 8.3 %collective-permute-start.38 = (f32[8,32,128]{2,1,0:T(8,128)S(1)}, f32[8,32,128]{2,1,0:T(8,128)S(1)}, u32[]{:S(2)}, u32[]{:S(2)}) collective-permute-start(f32[8,32,128]{2,1,0:T(8,128)S(1)} %get-tuple-element.83), channel_id=1, source_target_pairs={{0,4},{4,0},{8,12},{12,8},{16,20},{20,16},{24,28},{28,24},{1,5},{5... | collective-permute-start | bytes 393224 | tf_op jit(solution)/shard_map/ppermute | solution.py:305
  100.3 10.4 %collective-permute-start.40 = (f32[8,32,128]{2,1,0:T(8,128)S(1)}, f32[8,32,128]{2,1,0:T(8,128)S(1)}, u32[]{:S(2)}, u32[]{:S(2)}) collective-permute-start(f32[8,32,128]{2,1,0:T(8,128)S(1)} %get-tuple-element.85), channel_id=1, source_target_pairs={{0,12},{4,8},{8,4},{12,0},{16,28},{20,24},{24,20},{28,16},{1,13},{... | collective-permute-start | bytes 393224 | tf_op jit(solution)/shard_map/ppermute | solution.py:305
  101.8 9.0 %collective-permute-start.37 = (f32[8,32,128]{2,1,0:T(8,128)S(1)}, f32[8,32,128]{2,1,0:T(8,128)S(1)}, u32[]{:S(2)}, u32[]{:S(2)}) collective-permute-start(f32[8,32,128]{2,1,0:T(8,128)S(1)} %add_add_fusion.3), channel_id=1, source_target_pairs={{0,16},{4,20},{8,24},{12,28},{16,0},{20,4},{24,8},{28,12},{1,17},{... | collective-permute-start | bytes 393224 | tf_op jit(solution)/shard_map/ppermute | solution.py:305
  110.7 8.6 %collective-permute-start.44 = (f32[8,32,128]{2,1,0:T(8,128)S(1)}, f32[8,32,128]{2,1,0:T(8,128)S(1)}, u32[]{:S(2)}, u32[]{:S(2)}) collective-permute-start(f32[8,32,128]{2,1,0:T(8,128)S(1)} %add_add_fusion.2), channel_id=1, source_target_pairs={{0,16},{4,20},{8,24},{12,28},{16,0},{20,4},{24,8},{28,12},{1,17},{... | collective-permute-start | bytes 393224 | tf_op jit(solution)/shard_map/ppermute | solution.py:305
  120.5 9.3 %collective-permute-start.43 = (f32[8,32,128]{2,1,0:T(8,128)S(1)}, f32[8,32,128]{2,1,0:T(8,128)S(1)}, u32[]{:S(2)}, u32[]{:S(2)}) collective-permute-start(f32[8,32,128]{2,1,0:T(8,128)S(1)} %get-tuple-element.88.refs_0_), channel_id=1, source_target_pairs={{0,12},{4,8},{8,4},{12,0},{16,28},{20,24},{24,20},{28,16},{1,13},{... | collective-permute-start | bytes 393224 | tf_op jit(solution)/shard_map/ppermute | solution.py:305
  126.0 8.5 %collective-permute-start.48 = (f32[8,32,128]{2,1,0:T(8,128)S(1)}, f32[8,32,128]{2,1,0:T(8,128)S(1)}, u32[]{:S(2)}, u32[]{:S(2)}) collective-permute-start(f32[8,32,128]{2,1,0:T(8,128)S(1)} %get-tuple-element.87.refs_0_), channel_id=1, source_target_pairs={{0,12},{4,8},{8,4},{12,0},{16,28},{20,24},{24,20},{28,16},{1,13},{... | collective-permute-start | bytes 393224 | tf_op jit(solution)/shard_map/ppermute | solution.py:305
  139.1 8.4 %collective-permute-start.51 = (f32[8,32,128]{2,1,0:T(8,128)S(1)}, f32[8,32,128]{2,1,0:T(8,128)S(1)}, u32[]{:S(2)}, u32[]{:S(2)}) collective-permute-start(f32[8,32,128]{2,1,0:T(8,128)S(1)} %get-tuple-element.96), channel_id=1, source_target_pairs={{0,8},{4,12},{8,0},{12,4},{16,24},{20,28},{24,16},{28,20},{1,9},{5... | collective-permute-start | bytes 393224 | tf_op jit(solution)/shard_map/ppermute | solution.py:305
  139.4 8.9 %collective-permute-start.52 = (f32[8,32,128]{2,1,0:T(8,128)S(1)}, f32[8,32,128]{2,1,0:T(8,128)S(1)}, u32[]{:S(2)}, u32[]{:S(2)}) collective-permute-start(f32[8,32,128]{2,1,0:T(8,128)S(1)} %get-tuple-element.97), channel_id=1, source_target_pairs={{0,12},{4,8},{8,4},{12,0},{16,28},{20,24},{24,20},{28,16},{1,13},{... | collective-permute-start | bytes 393224 | tf_op jit(solution)/shard_map/ppermute | solution.py:305
  145.4 11.3 %collective-permute-start.58 = (f32[8,32,128]{2,1,0:T(8,128)S(1)}, f32[8,32,128]{2,1,0:T(8,128)S(1)}, u32[]{:S(2)}, u32[]{:S(2)}) collective-permute-start(f32[8,32,128]{2,1,0:T(8,128)S(1)} %get-tuple-element.103), channel_id=1, source_target_pairs={{0,12},{4,8},{8,4},{12,0},{16,28},{20,24},{24,20},{28,16},{1,13},{... | collective-permute-start | bytes 393224 | tf_op jit(solution)/shard_map/ppermute | solution.py:305
  148.4 9.6 %collective-permute-start.53 = (f32[8,32,128]{2,1,0:T(8,128)S(1)}, f32[8,32,128]{2,1,0:T(8,128)}, u32[]{:S(2)}, u32[]{:S(2)}) collective-permute-start(f32[8,32,128]{2,1,0:T(8,128)S(1)} %add_add_fusion.1.refs_0_), channel_id=1, source_target_pairs={{0,16},{4,20},{8,24},{12,28},{16,0},{20,4},{24,8},{28,12},{1,17},{... | collective-permute-start | bytes 393224 | tf_op jit(solution)/shard_map/ppermute | solution.py:305
  156.7 8.5 %collective-permute-start.59 = (f32[8,32,128]{2,1,0:T(8,128)S(1)}, f32[8,32,128]{2,1,0:T(8,128)}, u32[]{:S(2)}, u32[]{:S(2)}) collective-permute-start(f32[8,32,128]{2,1,0:T(8,128)S(1)} %add_add_fusion.refs_4_), channel_id=1, source_target_pairs={{0,16},{4,20},{8,24},{12,28},{16,0},{20,4},{24,8},{28,12},{1,17},{... | collective-permute-start | bytes 393224 | tf_op jit(solution)/shard_map/ppermute | solution.py:305
  (50 other events, 416.3 us)

commit v4 on v0

v4 whole, which is shorter than its diff:
```python
import functools

import jax
import jax.numpy as jnp
from jax import lax
from jax.experimental import pallas as pl
from jax.experimental.pallas import tpu as pltpu
from jax.sharding import PartitionSpec as P

STEPS = 3
CHAINS = 2
HALVES = 2
GROUP = 16
VMEM_BYTES = 16 << 20

shift_term = -0.25
half_width = 0.75

VMEM = pl.BlockSpec(memory_space=pltpu.VMEM)
SMEM = pl.BlockSpec(memory_space=pltpu.SMEM)
FULL = lax.Precision.HIGHEST


def call(kernel, out_shape, operands, in_specs=None, out_specs=None, scratch=(), flops=0, nbytes=0):
    many = isinstance(out_shape, list)
    return pl.pallas_call(
        kernel,
        in_specs=in_specs or [VMEM] * len(operands),
        out_specs=out_specs or ([VMEM] * len(out_shape) if many else VMEM),
        out_shape=out_shape,
        scratch_shapes=list(scratch),
        compiler_params=pltpu.CompilerParams(vmem_limit_bytes=VMEM_BYTES),
        cost_estimate=pl.CostEstimate(flops=flops, bytes_accessed=nbytes, transcendentals=0),
        name=kernel.func.__name__ if isinstance(kernel, functools.partial) else kernel.__name__,
    )(*operands)


def floats(*shape):
    return jax.ShapeDtypeStruct(shape, jnp.float32)


def split_bf16(x):
    high = x.astype(jnp.bfloat16)
    return high, (x - high.astype(jnp.float32)).astype(jnp.bfloat16)


def contract(a, b, dims, precision=None):
    return lax.dot_general(
        a, b, (dims, ((), ())), precision=precision, preferred_element_type=jnp.float32
    )


def prepare(table_ref, vals_hbm, cat_ref, degree_ref, vals_ref, sems):
    slots, tile, _ = vals_ref.shape
    loads = [
        pltpu.make_async_copy(
            vals_hbm.at[pl.ds(g * GROUP, GROUP)], vals_ref.at[pl.ds(g * GROUP, GROUP)], sems.at[g]
        )
        for g in range(slots // GROUP)
    ]
    for load in loads:
        load.start()
    degree_ref[...] = jnp.zeros_like(degree_ref)
    ones = jnp.ones((8, 2 * tile), jnp.bfloat16)
    live = table_ref[2 * slots]
    for slot in range(slots):
        if slot % GROUP == 0:
            loads[slot // GROUP].wait()
        values = vals_ref[slot] * (slot < live).astype(jnp.float32)
        high, low = split_bf16(values)
        cat_ref[slot, :, :tile] = high
        cat_ref[slot, :, tile:] = low
        sums = contract(ones, cat_ref[slot], ((1,), (1,)))
        degree_ref[pl.ds(table_ref[slots + slot], 1), :] += sums[:1]


def prepare_tiles(tile_vals, table, group_blocks):
    slots, tile, _ = tile_vals.shape
    return call(
        prepare,
        [pltpu.VMEM((slots, tile, 2 * tile), jnp.bfloat16), floats(group_blocks, tile)],
        [table, pltpu.with_memory_space_constraint(tile_vals, pltpu.HBM)],
        in_specs=[SMEM, pl.BlockSpec(memory_space=pl.ANY)],
        scratch=[
            pltpu.VMEM(tile_vals.shape, jnp.float32),
            pltpu.SemaphoreType.DMA((slots // GROUP,)),
        ],
        flops=2_000_000_000,
        nbytes=2 * tile_vals.size * 4,
    )


def join(flags_ref, chain_ref, other_ref, *refs):
    out_ref = refs[-1]
    own = chain_ref.shape[0]
    low = flags_ref[1, :1, :] == 0
    for j in range(own):
        mine, other = chain_ref[j], other_ref[j]
        out_ref[j] = jnp.where(low, mine, other)
        out_ref[own + j] = jnp.where(low, other, mine)
    if len(refs) == 2:
        out_ref[2 * own :] = refs[0][...].reshape(out_ref[2 * own :].shape)


def join_halves(flags, chain, other, degree=None):
    own, width, tile = chain.shape
    extra = 0 if degree is None else degree.shape[0] // width
    operands = [flags, chain, other] + ([] if degree is None else [degree])
    return call(join, floats(2 * own + extra, width, tile), operands)


def add_degrees(*refs, part):
    sources, out_ref = refs[:-1], refs[-1]
    tile = out_ref.shape[1]
    count = out_ref.shape[0] // part
    whole = [
        ref[ref.shape[0] - out_ref.shape[0] * tile // (ref.shape[1] * tile) :].reshape(-1, tile)
        for ref in sources
    ]
    for m in range(count):
        total = whole[0][m * part : (m + 1) * part]
        for k in range(1, len(whole)):
            total = total + whole[k][(m ^ k) * part : ((m ^ k) + 1) * part]
        out_ref[m * part : (m + 1) * part, :] = total


def roots(mine_ref, other_ref, root_ref, degree_ref, inverse_ref):
    degree = mine_ref[...] + other_ref[...]
    root_ref[...] = 1.0 / jnp.sqrt(degree)
    part = degree_ref.shape[0]
    degree_ref[...] = degree[:part]
    inverse_ref[...] = 1.0 / degree[:part]


def add(*refs, scaled):
    refs = list(refs)
    out_ref = refs.pop()
    scale_ref = refs.pop() if scaled else None
    for j in range(out_ref.shape[0]):
        total = refs[0][j]
        for ref in refs[1:]:
            total = total + ref[j]
        out_ref[j] = total * scale_ref[j : j + 1, :] if scaled else total


def add_all(arrays, scale=None):
    return call(
        functools.partial(add, scaled=scale is not None),
        floats(*arrays[0].shape),
        list(arrays) + ([] if scale is None else [scale]),
    )


def halo(flags_ref, *refs, own, rooted):
    refs = list(refs)
    far_ref, near_ref = refs.pop(), refs.pop()
    root_ref = refs.pop() if rooted else None
    count = len(refs)
    part = HALVES * own
    quad, odd = flags_ref[0, :1, :], flags_ref[2, :1, :] == 1
    for m in range(near_ref.shape[0] // own):
        low, high = m, count - near_ref.shape[0] // own + m
        for j in range(own):

            def block(k, h):
                value = refs[k][h * own + j]
                if rooted:
                    at = k * part + h * own + j
                    value = value * root_ref[at : at + 1, :]
                return value

            bottom, top = block(0, 0), block(0, HALVES - 1)
            for k in range(1, count):
                bottom = jnp.where((quad ^ k) == low, block(k, 0), bottom)
                top = jnp.where((quad ^ k) == high, block(k, HALVES - 1), top)
            near_ref[m * own + j] = jnp.where(odd, bottom, top)
            far_ref[m * own + j] = jnp.where(odd, top, bottom)


def halo_payloads(flags, pieces, own, reach, root=None):
    _, width, tile = pieces[0].shape
    operands = [flags, *pieces] + ([] if root is None else [root])
    return call(
        functools.partial(halo, own=own, rooted=root is not None),
        [floats(reach, width, tile)] * 2,
        operands,
    )


def products(table_ref, *refs, count, kind):
    refs = list(refs)
    pieces = [refs.pop(0) for _ in range(count)]
    near, far = refs.pop(0), refs.pop(0)
    if kind == "first":
        root_ref = refs.pop(0)
    else:
        last_ref = refs.pop(0)
        older_ref = refs.pop(0) if kind == "third" else None
    tiles_ref, state_ref = refs.pop(0), refs.pop(0)
    parts = [refs.pop(0) for _ in range(count)]
    cat_ref, total_ref = refs
    _, width, tile = state_ref.shape
    reach = near.shape[0]
    part = total_ref.shape[0] // count
    slots = tiles_ref.shape[0]
    total_ref[...] = jnp.zeros_like(total_ref)

    def advance(slot, value):
        if kind != "first":
            value = (2.0 / half_width) * (shift_term * last_ref[slot] - value)
            if kind == "third":
                value = value - older_ref[slot]
            else:
                value = 0.5 * value
        state_ref[slot] = value
        high, low = split_bf16(value)
        cat_ref[slot, :width, :tile] = high
        cat_ref[slot, :width, tile:] = high
        cat_ref[slot, width:, :tile] = low
        cat_ref[slot, width:, tile:] = low

    for k in range(count):
        for j in range(part):
            slot = k * part + j
            value = pieces[k][j]
            if kind == "first":
                value = value * root_ref[slot : slot + 1, :]
            advance(slot, value)
    for j in range(reach):
        advance(count * part + j, near[j])
        advance(count * part + reach + j, far[j])

    for slot in range(slots):
        both = contract(cat_ref[table_ref[slot]], tiles_ref[slot], ((1,), (1,)))
        total_ref[table_ref[slots + slot]] += both[:width] + both[width:]

    for k in range(count):
        parts[k][...] = total_ref[k * part : (k + 1) * part]


def tile_products(kind, table, pieces, near, far, extra, tiles, group_blocks):
    reach, width, tile = near.shape
    count = len(pieces)
    window = group_blocks + 2 * reach
    operands = [table, *pieces, near, far, *extra]
    operands.append(pltpu.with_memory_space_constraint(tiles, pltpu.VMEM))
    return call(
        functools.partial(products, kind=kind, count=count),
        [floats(window, width, tile)] + [floats(group_blocks // count, width, tile)] * count,
        operands,
        in_specs=[SMEM] + [VMEM] * (len(operands) - 1),
        scratch=[
            pltpu.VMEM((window, 2 * width, 2 * tile), jnp.bfloat16),
            pltpu.VMEM((group_blocks, width, tile), jnp.float32),
        ],
        flops=3_000_000_000,
        nbytes=tiles.size * 2,
    )


def gram(flags_ref, degree_ref, *refs, own):
    refs = list(refs)
    all_ref, gram_ref, filtered_ref = refs.pop(), refs.pop(), refs.pop()
    groups = [refs[i : i + 4] for i in range(0, len(refs), 4)]
    width = groups[0][0].shape[1]
    low = flags_ref[1, :1, :] == 0
    total = jnp.zeros(gram_ref.shape, jnp.float32)
    for i in range(HALVES * own):
        degree = degree_ref[i : i + 1, :]
        root, inverse = jnp.sqrt(degree), 1.0 / degree
        for c, (mine, other, last, older) in enumerate(groups):
            value = (mine[i] + other[i]) * inverse
            value = (2.0 / half_width) * (shift_term * last[i] - value) - older[i]
            all_ref[i, c * width : (c + 1) * width, :] = value * root
        block = all_ref[i]
        total += contract(block, block, ((1,), (1,)), FULL)
    for j in range(own):
        filtered_ref[j] = jnp.where(low, all_ref[j], all_ref[own + j])
    gram_ref[...] = total


def gram_of(flags, degree, groups, own):
    part, width, tile = groups[0][0].shape
    total = width * len(groups)
    return call(
        functools.partial(gram, own=own),
        [floats(own, total, tile), floats(total, total)],
        [flags, degree] + [x for group in groups for x in group],
        scratch=[pltpu.VMEM((part, total, tile), jnp.float32)],
    )


def solve(*refs, scale):
    parts, (filtered_ref, out_ref, work_ref) = refs[:-3], refs[-3:]
    size = parts[0].shape[0]
    tile = filtered_ref.shape[2]
    total = parts[0][...]
    for piece in parts[1:]:
        total = total + piece[...]
    row = lax.broadcasted_iota(jnp.int32, (size, size), 0)
    column = lax.broadcasted_iota(jnp.int32, (size, size), 1)
    work_ref[:, :size] = total * scale
    work_ref[:, size:] = (row == column).astype(jnp.float32)
    step = 8
    wide = 2 * size
    count = size // step
    rows = [work_ref[step * i : step * (i + 1), :] for i in range(count)]
    sub = lax.broadcasted_iota(jnp.int32, (step, wide), 0)

    def spread_row(x, j):
        return jnp.broadcast_to(x[j : j + 1, :], (step, wide))

    for p in range(count):
        columns = {
            i: [
                jnp.broadcast_to(rows[i][:, step * p + j : step * p + j + 1], (step, wide))
                for j in range(step)
            ]
            for i in range(p, count)
        }
        for j in range(step):
            root = lax.rsqrt(spread_row(columns[p][j], j))
            pivot = spread_row(rows[p], j) * root
            heads = {k: spread_row(columns[p][k], j) * root for k in range(j + 1, step)}
            for i in range(p, count):
                factor = columns[i][j] * root
                if i == p:
                    factor = jnp.where(sub > j, factor, 0.0)
                rows[i] = rows[i] - factor * pivot
                for k in range(j + 1, step):
                    columns[i][k] = columns[i][k] - factor * heads[k]
            rows[p] = jnp.where(sub == j, pivot, rows[p])
        work_ref[step * p : step * (p + 1), :] = rows[p]
    inverse = work_ref[:, size:]
    for j in range(filtered_ref.shape[0]):
        out_ref[:, j * tile : (j + 1) * tile] = contract(
            inverse, filtered_ref[j], ((1,), (0,)), FULL
        )


def solve_of(parts, filtered, scale):
    own, total, tile = filtered.shape
    return call(
        functools.partial(solve, scale=scale),
        floats(total, own * tile),
        [*parts, filtered],
        scratch=[pltpu.VMEM((total, 2 * total), jnp.float32)],
    )


def after(x, y):
    return lax.optimization_barrier((x, y))[0]


def on_device(start_block, tile_vals, tile_rows, tile_cols, tile_count):
    vec_width, local_rows = start_block.shape
    tile = tile_vals.shape[1]
    own = local_rows // tile
    blk_count = lax.axis_size("blk")
    row_count = lax.axis_size("rows")
    quad_count = blk_count // HALVES
    group_blocks = own * blk_count
    part = HALVES * own
    reach = group_blocks // 4
    rows_total = local_rows * blk_count * row_count
    width = vec_width // CHAINS
    group_index = lax.axis_index("rows")
    blk_index = lax.axis_index("blk")
    high, quad, odd = blk_index // quad_count, blk_index & (quad_count - 1), group_index & 1

    def over_blk(x, k):
        return lax.ppermute(x, "blk", [(i, i ^ k) for i in range(blk_count)])

    def over_rows(x, k):
        return lax.ppermute(x, "rows", [(i, i ^ k) for i in range(row_count)])

    def over_all(x, rows_bit, blk_bit):
        pairs = [
            (i * row_count + j, (i ^ blk_bit) * row_count + (j ^ rows_bit))
            for i in range(blk_count)
            for j in range(row_count)
        ]
        return lax.ppermute(x, ("blk", "rows"), pairs)

    def with_far(x):
        pairs = [(i, i + 1) for i in range(1, row_count - 1, 2)]
        return lax.ppermute(x, "rows", pairs + [(b, a) for a, b in pairs])

    def spread(x):
        return [x] + [over_blk(x, k) for k in range(1, quad_count)]

    def gather_sum(parts):
        return add_all([parts[0]] + [over_blk(parts[k], k) for k in range(1, quad_count)])

    def place(block):
        blk = block // own
        return ((blk & (quad_count - 1)) ^ quad) * part + (blk // quad_count) * own + block % own

    shift = group_index * group_blocks
    cols, rows = tile_cols - shift, tile_rows - shift
    left = group_blocks + jnp.where(odd == 1, 0, reach) + reach + cols
    right = group_blocks + jnp.where(odd == 1, reach, 0) + cols - group_blocks
    cols = jnp.where(cols < 0, left, jnp.where(cols < group_blocks, place(cols), right))
    table = jnp.concatenate([cols, place(rows), tile_count.reshape(1)])
    flags = jnp.stack([quad, high, odd]).astype(jnp.int32)
    flags = jnp.broadcast_to(flags[:, None, None], (3, 8, tile))
    blocks = start_block.reshape(vec_width, own, tile).transpose(1, 0, 2)
    chains = jnp.split(blocks, CHAINS, axis=1)
    tile_vals, table, flags, chains = lax.optimization_barrier((tile_vals, table, flags, chains))

    tiles, degree = prepare_tiles(tile_vals, table, group_blocks)
    others = [over_blk(chain, quad_count) for chain in chains]
    others[0] = after(others[0], others[1:])
    gathered = [spread(join_halves(flags, chains[0], others[0], degree))]
    for chain, other in zip(chains[1:], others[1:]):
        gathered.append(spread(join_halves(flags, chain, other)))
    degree = call(
        functools.partial(add_degrees, part=part), floats(group_blocks, tile), gathered[0]
    )
    other = after(over_blk(degree, quad_count), [x[1] for x in gathered[1:]])
    root, own_degree, inverse = call(
        roots,
        [floats(group_blocks, tile), floats(part, tile), floats(part, tile)],
        [degree, other],
    )

    states = [[] for _ in range(CHAINS)]
    parts = [None] * CHAINS
    for c in range(CHAINS):
        near, far = halo_payloads(flags, gathered[c], own, reach, root)
        near, far = over_rows(near, 1), with_far(far)
        if c + 1 < CHAINS:
            gathered[c + 1] = gathered[c + 1][:2] + after(gathered[c + 1][2:], near)
        state, *parts[c] = tile_products(
            "first", table, gathered[c], near, far, [root], tiles, group_blocks
        )
        states[c].append(state)

    for index in range(1, STEPS):
        kind = "second" if index == 1 else "third"
        sums = [gather_sum(parts[c]) for c in range(CHAINS)]
        for c in range(CHAINS - 1):
            sums[c] = after(sums[c], parts[c + 1][0])
        totals, pieces = [], []
        for c in range(CHAINS):
            mine = after(sums[c], other) if c else sums[c]
            other = over_blk(mine, quad_count)
            arrived = after(other, pieces[c - 1][1]) if c else other
            totals.append(add_all([mine, arrived], inverse))
            pieces.append(spread(totals[c]))
        for c in range(CHAINS):
            mine = after(pieces[c], totals[c + 1]) if c + 1 < CHAINS else pieces[c]
            near, far = halo_payloads(flags, mine, own, reach)
            near, far = over_rows(near, 1), with_far(far)
            if c + 1 < CHAINS:
                near = after(near, pieces[c + 1][1:])
            state, *parts[c] = tile_products(
                kind, table, mine, near, far,
                [states[c][-1 - i] for i in range(index)], tiles, group_blocks,
            )
            states[c].append(state)

    sums = [gather_sum(parts[c]) for c in range(CHAINS)]
    for c in range(CHAINS - 1):
        sums[c] = after(sums[c], parts[c + 1][0])
    groups = [
        [sums[c], over_blk(sums[c], quad_count), states[c][-1], states[c][-2]]
        for c in range(CHAINS)
    ]
    filtered, total = gram_of(flags, own_degree, groups, own)

    bits = [(1 << i, 0) for i in range(1, row_count.bit_length() - 1)]
    bits += [(0, 1 << i) for i in range(quad_count.bit_length() - 1)]
    stages = [[(1, 0)]]
    while bits:
        first, *second = bits[:2]
        bits = bits[2:]
        stages.append([first] + [x for y in second for x in (y, (first[0] ^ y[0], first[1] ^ y[1]))])
    pieces = [total]
    for stage in stages:
        total = sum(pieces[1:], pieces[0])
        pieces = [total] + [over_all(total, *bit) for bit in stage]
    return solve_of(pieces, filtered, 1.0 / rows_total)


def solution(mesh):
    in_specs = (
        P(None, ("rows", "blk")),
        P(("rows", "blk"), None, None),
        P(("rows", "blk")),
        P(("rows", "blk")),
        P("rows", "blk"),
    )
    out_specs = P(None, ("rows", "blk"))
    return jax.shard_map(
        on_device, mesh=mesh, in_specs=in_specs, out_specs=out_specs, check_vma=False
    )
```

time: 552 us -> 162 us (0.29)
  waiting for transfers between devices: 371 us -> 75.6 us
  blocking collectives: 78.6 us -> 0 us
  starting transfers between devices: 8.4 us -> 61.7 us
  matrix products: 38.6 us -> 0 us
  other arithmetic: 25.5 us -> 0.87 us
  Pallas kernels: 0 us -> 21.9 us
  local copies, waits for them, and re-layouts: 14.7 us -> 0.32 us
  between operations: 15 us -> 1.08 us
    psum x3 -> x0, waiting for transfers between devices: 241 us -> none  [apply_operator(): summed = lax.psum(partial_value, 'blk')]
    all_gather x3 -> x0, waiting for transfers between devices: 118 us -> none  [apply_operator(): gathered = lax.all_gather(scaled, 'blk', axis=1, tiled=True)]
    ppermute x6 -> x62, waiting for transfers between devices: 11 us -> 75.6 us  [the longest x45 67.7 us: over_blk(): return lax.ppermute(x, 'blk', [(i, i ^ k) for i in range(blk_count)])]
    ppermute x6 -> x62, starting transfers between devices: 8.19 us -> 61.7 us  [the longest x45 53.4 us: over_blk(): return lax.ppermute(x, 'blk', [(i, i ^ k) for i in range(blk_count)])]
    psum x1 -> x0, blocking collectives: 39.8 us -> none  [on_device(): gram_sum = lax.psum(gram_part, ('blk', 'rows'))]
    unnamed x1 -> x0, blocking collectives: 38.9 us -> none
    dot_general x8 -> x0, matrix products: 37.6 us -> none  [the longest x3 30.2 us: tile_products(): jnp.einsum('ktb,tab->kta', picked, values, precision=lax.Precision.HIGHEST)]
    pallas_call x0 -> x29, Pallas kernels: none -> 21.9 us  [call(): pl.pallas_call(kernel, in_specs=in_specs or [VMEM] * len(operands), out_s...]
  transfers between devices with their start and end apart: 12 -> 62, of which waited for: 9 -> 33; matrix products, arithmetic and copies ran while one was open for 0% -> 0% of each run, Pallas kernels for 0% -> 11%
where the time goes in v4:
time: 162 us; the launch traced here: 161 us
  waiting for transfers between devices  75.6 us (47%)
  starting transfers between devices  61.7 us (38%)
  Pallas kernels  21.9 us (14%)
    ppermute x45, waiting for transfers between devices, over_blk(): return lax.ppermute(x, 'blk', [(i, i ^ k) for i in range(blk_count)])  67.7 us
    ppermute x45, starting transfers between devices, over_blk(): return lax.ppermute(x, 'blk', [(i, i ^ k) for i in range(blk_count)])  53.4 us
    pallas_call x29, Pallas kernels, call(): pl.pallas_call(kernel, in_specs=in_specs or [VMEM] * len(operands), out_s...  21.9 us
    ppermute x5, waiting for transfers between devices, over_all(): return lax.ppermute(x, ('blk', 'rows'), pairs)  7.93 us
    ppermute x6, starting transfers between devices, with_far(): return lax.ppermute(x, 'rows', pairs + [(b, a) for a, b in pairs])  4.19 us
    ppermute x5, starting transfers between devices, over_all(): return lax.ppermute(x, ('blk', 'rows'), pairs)  3.64 us
  transfers between devices with their start and end apart: 62, of which 33 were waited for; matrix products, arithmetic and copies ran while one was open for 0% of the time, Pallas kernels for 11%

profile of v4, /device:TPU:0, one launch (start us, length us, event | category | flops | bytes accessed | tf_op | source)
XLA Modules:
  0.0 161.5 jit_solution(11898569858337333182)
XLA Ops:
  1.9 4.0 %collective-permute-start.1 = (f32[4,32,128]{2,1,0:T(8,128)S(1)}, f32[4,32,128]{2,1,0:T(8,128)S(1)}, u32[]{:S(2)}, u32[]{:S(2)}) collective-permute-start(f32[4,32,128]{2,1,0:T(8,128)S(1)} %get-tuple-element.82.chain_ref), channel_id=1, source_target_pairs={{0,16},{4,20},{8,24},{12,28},{16,0},{20,4},{24,8},{28,12},{1,17},{... | collective-permute-start | bytes 196616 | tf_op jit(solution)/shard_map/ppermute | solution.py:372
  6.0 3.5 %prepare.1 = (bf16[64,128,256]{2,1,0:T(8,128)(2,1)S(1)}, f32[32,128]{1,0:T(8,128)S(1)}) custom-call(s32[129]{0:T(256)S(1)} %pad_add_fusion.table_ref, f32[64,128,128]{2,1,0:T(8,128)} %vals_hbm), custom_call_target="tpu_custom_call" | custom-call | flops 2000000000 | bytes 8388608 | tf_op jit(solution)/shard_map/prepare/pallas_call | solution.py:26
  9.6 2.8 %collective-permute-done.other_ref = f32[4,32,128]{2,1,0:T(8,128)S(1)} collective-permute-done((f32[4,32,128]{2,1,0:T(8,128)S(1)}, f32[4,32,128]{2,1,0:T(8,128)S(1)}, u32[]{:S(2)}, u32[]{:S(2)}) %collective-permute-start) | collective-permute-done | bytes 65568 | tf_op jit(solution)/shard_map/ppermute | solution.py:372
  28.8 2.4 %collective-permute-done.12.refs_2_ = f32[8,32,128]{2,1,0:T(8,128)S(1)} collective-permute-done((f32[8,32,128]{2,1,0:T(8,128)S(1)}, f32[8,32,128]{2,1,0:T(8,128)S(1)}, u32[]{:S(2)}, u32[]{:S(2)}) %collective-permute-start.12) | collective-permute-done | bytes 131104 | tf_op jit(solution)/shard_map/ppermute | solution.py:372
  50.6 2.7 %collective-permute-done.22.refs_3_ = f32[8,32,128]{2,1,0:T(8,128)S(1)} collective-permute-done((f32[8,32,128]{2,1,0:T(8,128)S(1)}, f32[8,32,128]{2,1,0:T(8,128)S(1)}, u32[]{:S(2)}, u32[]{:S(2)}) %collective-permute-start.22) | collective-permute-done | bytes 131104 | tf_op jit(solution)/shard_map/ppermute | solution.py:372
  53.4 3.5 %collective-permute-done.16.refs_1_ = f32[8,32,128]{2,1,0:T(8,128)S(1)} collective-permute-done((f32[8,32,128]{2,1,0:T(8,128)S(1)}, f32[8,32,128]{2,1,0:T(8,128)S(1)}, u32[]{:S(2)}, u32[]{:S(2)}) %collective-permute-start.16) | collective-permute-done | bytes 131104 | tf_op jit(solution)/shard_map/ppermute | solution.py:372
  61.5 4.5 %collective-permute-done.23.refs_1_ = f32[8,32,128]{2,1,0:T(8,128)S(1)} collective-permute-done((f32[8,32,128]{2,1,0:T(8,128)S(1)}, f32[8,32,128]{2,1,0:T(8,128)S(1)}, u32[]{:S(2)}, u32[]{:S(2)}) %collective-permute-start.23) | collective-permute-done | bytes 131104 | tf_op jit(solution)/shard_map/ppermute | solution.py:372
  66.3 3.4 %collective-permute-start.27 = (f32[8,32,128]{2,1,0:T(8,128)S(1)}, f32[8,32,128]{2,1,0:T(8,128)S(1)}, u32[]{:S(2)}, u32[]{:S(2)}) collective-permute-start(f32[8,32,128]{2,1,0:T(8,128)S(1)} %add.125.refs_0_), channel_id=1, source_target_pairs={{0,12},{4,8},{8,4},{12,0},{16,28},{20,24},{24,20},{28,16},{1,13},{... | collective-permute-start | bytes 393224 | tf_op jit(solution)/shard_map/ppermute | solution.py:372
  71.3 2.8 %collective-permute-done.25.refs_1_ = f32[8,32,128]{2,1,0:T(8,128)S(1)} collective-permute-done((f32[8,32,128]{2,1,0:T(8,128)S(1)}, f32[8,32,128]{2,1,0:T(8,128)S(1)}, u32[]{:S(2)}, u32[]{:S(2)}) %collective-permute-start.25) | collective-permute-done | bytes 131104 | tf_op jit(solution)/shard_map/ppermute | solution.py:372
  76.7 2.4 %products.8 = (f32[48,32,128]{2,1,0:T(8,128)S(1)}, f32[8,32,128]{2,1,0:T(8,128)S(1)}, f32[8,32,128]{2,1,0:T(8,128)S(1)}, f32[8,32,128]{2,1,0:T(8,128)S(1)}, f32[8,32,128]{2,1,0:T(8,128)S(1)}) custom-call(s32[129]{0:T(256)S(1)} %pad_add_fusion.table_ref, f32[8,32,128]{2,1,0:T(8,128)S(1)} %add.123.refs_0_, f32[8,32,128]{2,1,0:T(8,128)S(1)} %collective-permute-done.17.refs_1_, ...), custom_call_target="tpu_custom_call" | custom-call | flops 3000000000 | bytes 4194304 | tf_op jit(solution)/shard_map/products/pallas_call | solution.py:26
  79.6 3.0 %collective-permute-start.31 = (f32[8,32,128]{2,1,0:T(8,128)S(1)}, f32[8,32,128]{2,1,0:T(8,128)S(1)}, u32[]{:S(2)}, u32[]{:S(2)}) collective-permute-start(f32[8,32,128]{2,1,0:T(8,128)S(1)} %get-tuple-element.120), channel_id=1, source_target_pairs={{0,12},{4,8},{8,4},{12,0},{16,28},{20,24},{24,20},{28,16},{1,13},{... | collective-permute-start | bytes 393224 | tf_op jit(solution)/shard_map/ppermute | solution.py:372
  82.7 2.4 %products.9 = (f32[48,32,128]{2,1,0:T(8,128)S(1)}, f32[8,32,128]{2,1,0:T(8,128)S(1)}, f32[8,32,128]{2,1,0:T(8,128)S(1)}, f32[8,32,128]{2,1,0:T(8,128)S(1)}, f32[8,32,128]{2,1,0:T(8,128)S(1)}) custom-call(s32[129]{0:T(256)S(1)} %pad_add_fusion.table_ref, f32[8,32,128]{2,1,0:T(8,128)S(1)} %add.125.refs_0_, f32[8,32,128]{2,1,0:T(8,128)S(1)} %collective-permute-done.25.refs_1_, ...), custom_call_target="tpu_custom_call" | custom-call | flops 3000000000 | bytes 4194304 | tf_op jit(solution)/shard_map/products/pallas_call | solution.py:26
  85.7 2.9 %collective-permute-start.40 = (f32[8,32,128]{2,1,0:T(8,128)S(1)}, f32[8,32,128]{2,1,0:T(8,128)S(1)}, u32[]{:S(2)}, u32[]{:S(2)}) collective-permute-start(f32[8,32,128]{2,1,0:T(8,128)S(1)} %get-tuple-element.128), channel_id=1, source_target_pairs={{0,12},{4,8},{8,4},{12,0},{16,28},{20,24},{24,20},{28,16},{1,13},{... | collective-permute-start | bytes 393224 | tf_op jit(solution)/shard_map/ppermute | solution.py:372
  89.6 3.3 %collective-permute-done.38.refs_1_ = f32[8,32,128]{2,1,0:T(8,128)S(1)} collective-permute-done((f32[8,32,128]{2,1,0:T(8,128)S(1)}, f32[8,32,128]{2,1,0:T(8,128)S(1)}, u32[]{:S(2)}, u32[]{:S(2)}) %collective-permute-start.38) | collective-permute-done | bytes 131104 | tf_op jit(solution)/shard_map/ppermute | solution.py:372
  92.9 5.2 %collective-permute-done.40.refs_3_ = f32[8,32,128]{2,1,0:T(8,128)S(1)} collective-permute-done((f32[8,32,128]{2,1,0:T(8,128)S(1)}, f32[8,32,128]{2,1,0:T(8,128)S(1)}, u32[]{:S(2)}, u32[]{:S(2)}) %collective-permute-start.40) | collective-permute-done | bytes 131104 | tf_op jit(solution)/shard_map/ppermute | solution.py:372
  102.5 4.5 %collective-permute-done.41.refs_1_ = f32[8,32,128]{2,1,0:T(8,128)S(1)} collective-permute-done((f32[8,32,128]{2,1,0:T(8,128)S(1)}, f32[8,32,128]{2,1,0:T(8,128)S(1)}, u32[]{:S(2)}, u32[]{:S(2)}) %collective-permute-start.41) | collective-permute-done | bytes 131104 | tf_op jit(solution)/shard_map/ppermute | solution.py:372
  111.9 3.1 %collective-permute-done.43.refs_1_ = f32[8,32,128]{2,1,0:T(8,128)S(1)} collective-permute-done((f32[8,32,128]{2,1,0:T(8,128)S(1)}, f32[8,32,128]{2,1,0:T(8,128)S(1)}, u32[]{:S(2)}, u32[]{:S(2)}) %collective-permute-start.43) | collective-permute-done | bytes 131104 | tf_op jit(solution)/shard_map/ppermute | solution.py:372
  117.6 2.4 %products.10 = (f32[48,32,128]{2,1,0:T(8,128)S(1)}, f32[8,32,128]{2,1,0:T(8,128)S(1)}, f32[8,32,128]{2,1,0:T(8,128)S(1)}, f32[8,32,128]{2,1,0:T(8,128)S(1)}, f32[8,32,128]{2,1,0:T(8,128)S(1)}) custom-call(s32[129]{0:T(256)S(1)} %pad_add_fusion.table_ref, f32[8,32,128]{2,1,0:T(8,128)S(1)} %add.127.refs_0_, f32[8,32,128]{2,1,0:T(8,128)S(1)} %collective-permute-done.35.refs_1_, ...), custom_call_target="tpu_custom_call" | custom-call | flops 3000000000 | bytes 4194304 | tf_op jit(solution)/shard_map/products/pallas_call | solution.py:26
  123.6 2.4 %products.11 = (f32[48,32,128]{2,1,0:T(8,128)S(1)}, f32[8,32,128]{2,1,0:T(8,128)S(1)}, f32[8,32,128]{2,1,0:T(8,128)S(1)}, f32[8,32,128]{2,1,0:T(8,128)S(1)}, f32[8,32,128]{2,1,0:T(8,128)S(1)}) custom-call(s32[129]{0:T(256)S(1)} %pad_add_fusion.table_ref, f32[8,32,128]{2,1,0:T(8,128)S(1)} %add.129.refs_0_, f32[8,32,128]{2,1,0:T(8,128)S(1)} %collective-permute-done.43.refs_1_, ...), custom_call_target="tpu_custom_call" | custom-call | flops 3000000000 | bytes 4194304 | tf_op jit(solution)/shard_map/products/pallas_call | solution.py:26
  131.3 2.6 %collective-permute-done.53.refs_1_ = f32[8,32,128]{2,1,0:T(8,128)S(1)} collective-permute-done((f32[8,32,128]{2,1,0:T(8,128)S(1)}, f32[8,32,128]{2,1,0:T(8,128)S(1)}, u32[]{:S(2)}, u32[]{:S(2)}) %collective-permute-start.53) | collective-permute-done | bytes 131104 | tf_op jit(solution)/shard_map/ppermute | solution.py:372
  133.8 4.4 %collective-permute-done.55.refs_3_ = f32[8,32,128]{2,1,0:T(8,128)S(1)} collective-permute-done((f32[8,32,128]{2,1,0:T(8,128)S(1)}, f32[8,32,128]{2,1,0:T(8,128)S(1)}, u32[]{:S(2)}, u32[]{:S(2)}) %collective-permute-start.55) | collective-permute-done | bytes 131104 | tf_op jit(solution)/shard_map/ppermute | solution.py:372
  140.0 6.6 %collective-permute-done.56.refs_5_ = f32[8,32,128]{2,1,0:T(8,128)S(1)} collective-permute-done((f32[8,32,128]{2,1,0:T(8,128)S(1)}, f32[8,32,128]{2,1,0:T(8,128)S(1)}, u32[]{:S(2)}, u32[]{:S(2)}) %collective-permute-start.56) | collective-permute-done | bytes 131104 | tf_op jit(solution)/shard_map/ppermute | solution.py:372
  154.8 3.9 %collective-permute-done.61.refs_1_ = f32[64,64]{1,0:T(8,128)S(1)} collective-permute-done((f32[64,64]{1,0:T(8,128)S(1)}, f32[64,64]{1,0:T(8,128)S(1)}, u32[]{:S(2)}, u32[]{:S(2)}) %collective-permute-start.61) | collective-permute-done | bytes 16416 | tf_op jit(solution)/shard_map/ppermute | solution.py:383
  158.7 2.8 %solve.1 = f32[64,512]{1,0:T(8,128)} custom-call(f32[64,64]{1,0:T(8,128)S(1)} %add_add_fusion.refs_0_, f32[64,64]{1,0:T(8,128)S(1)} %collective-permute-done.61.refs_1_, f32[4,64,128]{2,1,0:T(8,128)S(1)} %get-tuple-element.154.refs_2_), custom_call_target="tpu_custom_call" | custom-call | tf_op jit(solution)/shard_map/solve/pallas_call | solution.py:26
  (139 shorter events, 78.7 us)
Async XLA Ops:
  16.0 12.0 %collective-permute-start.6 = (f32[8,32,128]{2,1,0:T(8,128)S(1)}, f32[8,32,128]{2,1,0:T(8,128)S(1)}, u32[]{:S(2)}, u32[]{:S(2)}) collective-permute-start(f32[8,32,128]{2,1,0:T(8,128)S(1)} %join.3.refs_0_), channel_id=1, source_target_pairs={{0,4},{4,0},{8,12},{12,8},{16,20},{20,16},{24,28},{28,24},{1,5},{5... | collective-permute-start | bytes 393224 | tf_op jit(solution)/shard_map/ppermute | solution.py:372
  38.8 8.4 %collective-permute-start.9 = (f32[8,32,128]{2,1,0:T(8,128)S(1)}, f32[8,32,128]{2,1,0:T(8,128)S(1)}, u32[]{:S(2)}, u32[]{:S(2)}) collective-permute-start(f32[8,32,128]{2,1,0:T(8,128)S(1)} %get-tuple-element.94), channel_id=1, source_target_pairs={{0,4},{4,0},{8,12},{12,8},{16,20},{20,16},{24,28},{28,24},{1,5},{5... | collective-permute-start | bytes 393224 | tf_op jit(solution)/shard_map/ppermute | solution.py:372
  42.3 8.4 %collective-permute-start.20 = (f32[8,32,128]{2,1,0:T(8,128)S(1)}, f32[8,32,128]{2,1,0:T(8,128)S(1)}, u32[]{:S(2)}, u32[]{:S(2)}) collective-permute-start(f32[8,32,128]{2,1,0:T(8,128)S(1)} %get-tuple-element.104), channel_id=1, source_target_pairs={{0,4},{4,0},{8,12},{12,8},{16,20},{20,16},{24,28},{28,24},{1,5},{5... | collective-permute-start | bytes 393224 | tf_op jit(solution)/shard_map/ppermute | solution.py:372
  44.2 9.2 %collective-permute-start.22 = (f32[8,32,128]{2,1,0:T(8,128)S(1)}, f32[8,32,128]{2,1,0:T(8,128)S(1)}, u32[]{:S(2)}, u32[]{:S(2)}) collective-permute-start(f32[8,32,128]{2,1,0:T(8,128)S(1)} %get-tuple-element.106), channel_id=1, source_target_pairs={{0,12},{4,8},{8,4},{12,0},{16,28},{20,24},{24,20},{28,16},{1,13},{... | collective-permute-start | bytes 393224 | tf_op jit(solution)/shard_map/ppermute | solution.py:372
  47.3 9.7 %collective-permute-start.16 = (f32[8,32,128]{2,1,0:T(8,128)S(1)}, f32[8,32,128]{2,1,0:T(8,128)S(1)}, u32[]{:S(2)}, u32[]{:S(2)}) collective-permute-start(f32[8,32,128]{2,1,0:T(8,128)S(1)} %add.122.refs_0_), channel_id=1, source_target_pairs={{0,16},{4,20},{8,24},{12,28},{16,0},{20,4},{24,8},{28,12},{1,17},{... | collective-permute-start | bytes 393224 | tf_op jit(solution)/shard_map/ppermute | solution.py:372
  56.9 9.1 %collective-permute-start.23 = (f32[8,32,128]{2,1,0:T(8,128)S(1)}, f32[8,32,128]{2,1,0:T(8,128)S(1)}, u32[]{:S(2)}, u32[]{:S(2)}) collective-permute-start(f32[8,32,128]{2,1,0:T(8,128)S(1)} %add.124.refs_0_), channel_id=1, source_target_pairs={{0,16},{4,20},{8,24},{12,28},{16,0},{20,4},{24,8},{28,12},{1,17},{... | collective-permute-start | bytes 393224 | tf_op jit(solution)/shard_map/ppermute | solution.py:372
  57.0 9.1 %collective-permute-start.17 = (f32[8,32,128]{2,1,0:T(8,128)S(1)}, f32[8,32,128]{2,1,0:T(8,128)S(1)}, u32[]{:S(2)}, u32[]{:S(2)}) collective-permute-start(f32[8,32,128]{2,1,0:T(8,128)S(1)} %add.123.refs_0_), channel_id=1, source_target_pairs={{0,4},{4,0},{8,12},{12,8},{16,20},{20,16},{24,28},{28,24},{1,5},{5... | collective-permute-start | bytes 393224 | tf_op jit(solution)/shard_map/ppermute | solution.py:372
  58.1 11.6 %collective-permute-start.18 = (f32[8,32,128]{2,1,0:T(8,128)S(1)}, f32[8,32,128]{2,1,0:T(8,128)S(1)}, u32[]{:S(2)}, u32[]{:S(2)}) collective-permute-start(f32[8,32,128]{2,1,0:T(8,128)S(1)} %add.123.refs_0_), channel_id=1, source_target_pairs={{0,8},{4,12},{8,0},{12,4},{16,24},{20,28},{24,16},{28,20},{1,9},{5... | collective-permute-start | bytes 393224 | tf_op jit(solution)/shard_map/ppermute | solution.py:372
  60.2 10.3 %collective-permute-start.19 = (f32[8,32,128]{2,1,0:T(8,128)S(1)}, f32[8,32,128]{2,1,0:T(8,128)S(1)}, u32[]{:S(2)}, u32[]{:S(2)}) collective-permute-start(f32[8,32,128]{2,1,0:T(8,128)S(1)} %add.123.refs_0_), channel_id=1, source_target_pairs={{0,12},{4,8},{8,4},{12,0},{16,28},{20,24},{24,20},{28,16},{1,13},{... | collective-permute-start | bytes 393224 | tf_op jit(solution)/shard_map/ppermute | solution.py:372
  66.3 9.6 %collective-permute-start.27 = (f32[8,32,128]{2,1,0:T(8,128)S(1)}, f32[8,32,128]{2,1,0:T(8,128)S(1)}, u32[]{:S(2)}, u32[]{:S(2)}) collective-permute-start(f32[8,32,128]{2,1,0:T(8,128)S(1)} %add.125.refs_0_), channel_id=1, source_target_pairs={{0,12},{4,8},{8,4},{12,0},{16,28},{20,24},{24,20},{28,16},{1,13},{... | collective-permute-start | bytes 393224 | tf_op jit(solution)/shard_map/ppermute | solution.py:372
  79.6 9.0 %collective-permute-start.30 = (f32[8,32,128]{2,1,0:T(8,128)S(1)}, f32[8,32,128]{2,1,0:T(8,128)S(1)}, u32[]{:S(2)}, u32[]{:S(2)}) collective-permute-start(f32[8,32,128]{2,1,0:T(8,128)S(1)} %get-tuple-element.119), channel_id=1, source_target_pairs={{0,8},{4,12},{8,0},{12,4},{16,24},{20,28},{24,16},{28,20},{1,9},{5... | collective-permute-start | bytes 393224 | tf_op jit(solution)/shard_map/ppermute | solution.py:372
  79.6 9.9 %collective-permute-start.31 = (f32[8,32,128]{2,1,0:T(8,128)S(1)}, f32[8,32,128]{2,1,0:T(8,128)S(1)}, u32[]{:S(2)}, u32[]{:S(2)}) collective-permute-start(f32[8,32,128]{2,1,0:T(8,128)S(1)} %get-tuple-element.120), channel_id=1, source_target_pairs={{0,12},{4,8},{8,4},{12,0},{16,28},{20,24},{24,20},{28,16},{1,13},{... | collective-permute-start | bytes 393224 | tf_op jit(solution)/shard_map/ppermute | solution.py:372
  85.7 12.4 %collective-permute-start.40 = (f32[8,32,128]{2,1,0:T(8,128)S(1)}, f32[8,32,128]{2,1,0:T(8,128)S(1)}, u32[]{:S(2)}, u32[]{:S(2)}) collective-permute-start(f32[8,32,128]{2,1,0:T(8,128)S(1)} %get-tuple-element.128), channel_id=1, source_target_pairs={{0,12},{4,8},{8,4},{12,0},{16,28},{20,24},{24,20},{28,16},{1,13},{... | collective-permute-start | bytes 393224 | tf_op jit(solution)/shard_map/ppermute | solution.py:372
  89.5 9.5 %collective-permute-start.34 = (f32[8,32,128]{2,1,0:T(8,128)S(1)}, f32[8,32,128]{2,1,0:T(8,128)S(1)}, u32[]{:S(2)}, u32[]{:S(2)}) collective-permute-start(f32[8,32,128]{2,1,0:T(8,128)S(1)} %add.126.refs_0_), channel_id=1, source_target_pairs={{0,16},{4,20},{8,24},{12,28},{16,0},{20,4},{24,8},{28,12},{1,17},{... | collective-permute-start | bytes 393224 | tf_op jit(solution)/shard_map/ppermute | solution.py:372
  99.0 8.1 %collective-permute-start.41 = (f32[8,32,128]{2,1,0:T(8,128)S(1)}, f32[8,32,128]{2,1,0:T(8,128)S(1)}, u32[]{:S(2)}, u32[]{:S(2)}) collective-permute-start(f32[8,32,128]{2,1,0:T(8,128)S(1)} %add.128.refs_0_), channel_id=1, source_target_pairs={{0,16},{4,20},{8,24},{12,28},{16,0},{20,4},{24,8},{28,12},{1,17},{... | collective-permute-start | bytes 393224 | tf_op jit(solution)/shard_map/ppermute | solution.py:372
  99.0 8.1 %collective-permute-start.35 = (f32[8,32,128]{2,1,0:T(8,128)S(1)}, f32[8,32,128]{2,1,0:T(8,128)S(1)}, u32[]{:S(2)}, u32[]{:S(2)}) collective-permute-start(f32[8,32,128]{2,1,0:T(8,128)S(1)} %add.127.refs_0_), channel_id=1, source_target_pairs={{0,4},{4,0},{8,12},{12,8},{16,20},{20,16},{24,28},{28,24},{1,5},{5... | collective-permute-start | bytes 393224 | tf_op jit(solution)/shard_map/ppermute | solution.py:372
  99.4 11.3 %collective-permute-start.36 = (f32[8,32,128]{2,1,0:T(8,128)S(1)}, f32[8,32,128]{2,1,0:T(8,128)S(1)}, u32[]{:S(2)}, u32[]{:S(2)}) collective-permute-start(f32[8,32,128]{2,1,0:T(8,128)S(1)} %add.127.refs_0_), channel_id=1, source_target_pairs={{0,8},{4,12},{8,0},{12,4},{16,24},{20,28},{24,16},{28,20},{1,9},{5... | collective-permute-start | bytes 393224 | tf_op jit(solution)/shard_map/ppermute | solution.py:372
  100.8 10.3 %collective-permute-start.37 = (f32[8,32,128]{2,1,0:T(8,128)S(1)}, f32[8,32,128]{2,1,0:T(8,128)S(1)}, u32[]{:S(2)}, u32[]{:S(2)}) collective-permute-start(f32[8,32,128]{2,1,0:T(8,128)S(1)} %add.127.refs_0_), channel_id=1, source_target_pairs={{0,12},{4,8},{8,4},{12,0},{16,28},{20,24},{24,20},{28,16},{1,13},{... | collective-permute-start | bytes 393224 | tf_op jit(solution)/shard_map/ppermute | solution.py:372
  108.3 8.3 %collective-permute-start.45 = (f32[8,32,128]{2,1,0:T(8,128)S(1)}, f32[8,32,128]{2,1,0:T(8,128)S(1)}, u32[]{:S(2)}, u32[]{:S(2)}) collective-permute-start(f32[8,32,128]{2,1,0:T(8,128)S(1)} %add.129.refs_0_), channel_id=1, source_target_pairs={{0,12},{4,8},{8,4},{12,0},{16,28},{20,24},{24,20},{28,16},{1,13},{... | collective-permute-start | bytes 393224 | tf_op jit(solution)/shard_map/ppermute | solution.py:372
  121.2 8.4 %collective-permute-start.48 = (f32[8,32,128]{2,1,0:T(8,128)S(1)}, f32[8,32,128]{2,1,0:T(8,128)S(1)}, u32[]{:S(2)}, u32[]{:S(2)}) collective-permute-start(f32[8,32,128]{2,1,0:T(8,128)S(1)} %get-tuple-element.141), channel_id=1, source_target_pairs={{0,8},{4,12},{8,0},{12,4},{16,24},{20,28},{24,16},{28,20},{1,9},{5... | collective-permute-start | bytes 393224 | tf_op jit(solution)/shard_map/ppermute | solution.py:372
  121.5 9.0 %collective-permute-start.49 = (f32[8,32,128]{2,1,0:T(8,128)S(1)}, f32[8,32,128]{2,1,0:T(8,128)S(1)}, u32[]{:S(2)}, u32[]{:S(2)}) collective-permute-start(f32[8,32,128]{2,1,0:T(8,128)S(1)} %get-tuple-element.142), channel_id=1, source_target_pairs={{0,12},{4,8},{8,4},{12,0},{16,28},{20,24},{24,20},{28,16},{1,13},{... | collective-permute-start | bytes 393224 | tf_op jit(solution)/shard_map/ppermute | solution.py:372
  127.4 10.8 %collective-permute-start.55 = (f32[8,32,128]{2,1,0:T(8,128)S(1)}, f32[8,32,128]{2,1,0:T(8,128)S(1)}, u32[]{:S(2)}, u32[]{:S(2)}) collective-permute-start(f32[8,32,128]{2,1,0:T(8,128)S(1)} %get-tuple-element.151), channel_id=1, source_target_pairs={{0,12},{4,8},{8,4},{12,0},{16,28},{20,24},{24,20},{28,16},{1,13},{... | collective-permute-start | bytes 393224 | tf_op jit(solution)/shard_map/ppermute | solution.py:372
  130.5 9.5 %collective-permute-start.52 = (f32[8,32,128]{2,1,0:T(8,128)S(1)}, f32[8,32,128]{2,1,0:T(8,128)S(1)}, u32[]{:S(2)}, u32[]{:S(2)}) collective-permute-start(f32[8,32,128]{2,1,0:T(8,128)S(1)} %add.130.refs_0_), channel_id=1, source_target_pairs={{0,16},{4,20},{8,24},{12,28},{16,0},{20,4},{24,8},{28,12},{1,17},{... | collective-permute-start | bytes 393224 | tf_op jit(solution)/shard_map/ppermute | solution.py:372
  138.3 8.2 %collective-permute-start.56 = (f32[8,32,128]{2,1,0:T(8,128)S(1)}, f32[8,32,128]{2,1,0:T(8,128)S(1)}, u32[]{:S(2)}, u32[]{:S(2)}) collective-permute-start(f32[8,32,128]{2,1,0:T(8,128)S(1)} %add.131.refs_4_), channel_id=1, source_target_pairs={{0,16},{4,20},{8,24},{12,28},{16,0},{20,4},{24,8},{28,12},{1,17},{... | collective-permute-start | bytes 393224 | tf_op jit(solution)/shard_map/ppermute | solution.py:372
  (39 other events, 245.9 us)

commit v5 on v4

--- a/solution.py
+++ b/solution.py
@@ -109,27 +109,16 @@
     return call(join, floats(2 * own + extra, width, tile), operands)
 
 
-def add_degrees(*refs, part):
-    sources, out_ref = refs[:-1], refs[-1]
-    tile = out_ref.shape[1]
-    count = out_ref.shape[0] // part
-    whole = [
-        ref[ref.shape[0] - out_ref.shape[0] * tile // (ref.shape[1] * tile) :].reshape(-1, tile)
-        for ref in sources
-    ]
-    for m in range(count):
-        total = whole[0][m * part : (m + 1) * part]
-        for k in range(1, len(whole)):
-            total = total + whole[k][(m ^ k) * part : ((m ^ k) + 1) * part]
-        out_ref[m * part : (m + 1) * part, :] = total
-
-
-def roots(mine_ref, other_ref, root_ref, degree_ref, inverse_ref):
-    degree = mine_ref[...] + other_ref[...]
-    root_ref[...] = 1.0 / jnp.sqrt(degree)
-    part = degree_ref.shape[0]
-    degree_ref[...] = degree[:part]
-    inverse_ref[...] = 1.0 / degree[:part]
+def roots(*refs, part):
+    sources, (root_ref, degree_ref, inverse_ref) = refs[:-3], refs[-3:]
+    for m in range(root_ref.shape[0] // part):
+        total = sources[0][m * part : (m + 1) * part, :]
+        for k in range(1, len(sources)):
+            total = total + sources[k][(m ^ k) * part : ((m ^ k) + 1) * part, :]
+        root_ref[m * part : (m + 1) * part, :] = 1.0 / jnp.sqrt(total)
+        if m == 0:
+            degree_ref[...] = total
+            inverse_ref[...] = 1.0 / total
 
 
 def add(*refs, scaled):
@@ -187,8 +176,12 @@
     )
 
 
-def products(table_ref, *refs, count, kind):
+def products(table_hbm, *refs, count, kind):
     refs = list(refs)
+    sem = refs.pop()
+    table_ref = refs.pop()
+    fetch = pltpu.make_async_copy(table_hbm, table_ref, sem)
+    fetch.start()
     pieces = [refs.pop(0) for _ in range(count)]
     near, far = refs.pop(0), refs.pop(0)
     if kind == "first":
@@ -230,6 +223,7 @@
         advance(count * part + j, near[j])
         advance(count * part + reach + j, far[j])
 
+    fetch.wait()
     for slot in range(slots):
         both = contract(cat_ref[table_ref[slot]], tiles_ref[slot], ((1,), (1,)))
         total_ref[table_ref[slots + slot]] += both[:width] + both[width:]
@@ -248,10 +242,12 @@
         functools.partial(products, kind=kind, count=count),
         [floats(window, width, tile)] + [floats(group_blocks // count, width, tile)] * count,
         operands,
-        in_specs=[SMEM] + [VMEM] * (len(operands) - 1),
+        in_specs=[pl.BlockSpec(memory_space=pl.ANY)] + [VMEM] * (len(operands) - 1),
         scratch=[
             pltpu.VMEM((window, 2 * width, 2 * tile), jnp.bfloat16),
             pltpu.VMEM((group_blocks, width, tile), jnp.float32),
+            pltpu.SMEM(table.shape, table.dtype),
+            pltpu.SemaphoreType.DMA(()),
         ],
         flops=3_000_000_000,
         nbytes=tiles.size * 2,
@@ -406,22 +402,19 @@
     flags = jnp.broadcast_to(flags[:, None, None], (3, 8, tile))
     blocks = start_block.reshape(vec_width, own, tile).transpose(1, 0, 2)
     chains = jnp.split(blocks, CHAINS, axis=1)
-    tile_vals, table, flags, chains = lax.optimization_barrier((tile_vals, table, flags, chains))
+    tile_vals, table, flags = lax.optimization_barrier((tile_vals, table, flags))
 
     tiles, degree = prepare_tiles(tile_vals, table, group_blocks)
     others = [over_blk(chain, quad_count) for chain in chains]
-    others[0] = after(others[0], others[1:])
-    gathered = [spread(join_halves(flags, chains[0], others[0], degree))]
-    for chain, other in zip(chains[1:], others[1:]):
-        gathered.append(spread(join_halves(flags, chain, other)))
-    degree = call(
-        functools.partial(add_degrees, part=part), floats(group_blocks, tile), gathered[0]
-    )
-    other = after(over_blk(degree, quad_count), [x[1] for x in gathered[1:]])
+    others[0] = after(others[0], [degree, *others[1:]])
+    other = over_blk(degree, quad_count)
+    gathered = [spread(join_halves(flags, x, y)) for x, y in zip(chains, others)]
+    other = after(other, [x[1] for x in gathered])
+    degrees = spread(add_all([degree[None], other[None]])[0])
     root, own_degree, inverse = call(
-        roots,
+        functools.partial(roots, part=part),
         [floats(group_blocks, tile), floats(part, tile), floats(part, tile)],
-        [degree, other],
+        degrees,
     )
 
     states = [[] for _ in range(CHAINS)]
@@ -469,9 +462,9 @@
     ]
     filtered, total = gram_of(flags, own_degree, groups, own)
 
-    bits = [(1 << i, 0) for i in range(1, row_count.bit_length() - 1)]
+    bits = [(1 << i, 0) for i in range(row_count.bit_length() - 1)]
     bits += [(0, 1 << i) for i in range(quad_count.bit_length() - 1)]
-    stages = [[(1, 0)]]
+    stages = []
     while bits:
         first, *second = bits[:2]
         bits = bits[2:]

time: 162 us -> 162 us (level)
  starting transfers between devices: 61.7 us -> 77.6 us
  waiting for transfers between devices: 75.6 us -> 60 us
    ppermute x45 -> x48, starting transfers between devices: 53.4 us -> 67.4 us  [over_blk(): return lax.ppermute(x, 'blk', [(i, i ^ k) for i in range(blk_count)])]
    ppermute x45 -> x48, waiting for transfers between devices: 67.7 us -> 55.1 us  [over_blk(): return lax.ppermute(x, 'blk', [(i, i ^ k) for i in range(blk_count)])]
    ppermute x5 -> x6, waiting for transfers between devices: 7.93 us -> 4.91 us  [over_all(): return lax.ppermute(x, ('blk', 'rows'), pairs)]
    ppermute x5 -> x6, starting transfers between devices: 3.64 us -> 5.48 us  [over_all(): return lax.ppermute(x, ('blk', 'rows'), pairs)]
  transfers between devices with their start and end apart: 62 -> 66, of which waited for: 33 -> 29; matrix products, arithmetic and copies ran while one was open for 0% -> 1% of each run, Pallas kernels for 11% -> 11%
where the time goes in v5:
time: 162 us; the launch traced here: 161 us
  starting transfers between devices  77.6 us (48%)
  waiting for transfers between devices  60 us (37%)
  Pallas kernels  20.8 us (13%)
    ppermute x48, starting transfers between devices, over_blk(): return lax.ppermute(x, 'blk', [(i, i ^ k) for i in range(blk_count)])  67.4 us
    ppermute x48, waiting for transfers between devices, over_blk(): return lax.ppermute(x, 'blk', [(i, i ^ k) for i in range(blk_count)])  55.1 us
    pallas_call x29, Pallas kernels, call(): pl.pallas_call(kernel, in_specs=in_specs or [VMEM] * len(operands), out_s...  20.8 us
    ppermute x6, starting transfers between devices, over_all(): return lax.ppermute(x, ('blk', 'rows'), pairs)  5.48 us
    ppermute x6, waiting for transfers between devices, over_all(): return lax.ppermute(x, ('blk', 'rows'), pairs)  4.91 us
    ppermute x6, starting transfers between devices, with_far(): return lax.ppermute(x, 'rows', pairs + [(b, a) for a, b in pairs])  4.18 us
  transfers between devices with their start and end apart: 66, of which 29 were waited for; matrix products, arithmetic and copies ran while one was open for 1% of the time, Pallas kernels for 11%

profile of v5, /device:TPU:0, one launch (start us, length us, event | category | flops | bytes accessed | tf_op | source)
XLA Modules:
  0.0 161.4 jit_solution(1461443994635186401)
XLA Ops:
  0.9 4.1 %collective-permute-start.2 = (f32[4,32,128]{2,1,0:T(8,128)S(1)}, f32[4,32,128]{2,1,0:T(8,128)S(1)}, u32[]{:S(2)}, u32[]{:S(2)}) collective-permute-start(f32[4,32,128]{2,1,0:T(8,128)S(1)} %get-tuple-element.151.chain_ref), channel_id=1, source_target_pairs={{0,16},{4,20},{8,24},{12,28},{16,0},{20,4},{24,8},{28,12},{1,17},{... | collective-permute-start | bytes 196616 | tf_op jit(solution)/shard_map/ppermute | solution.py:368
  6.7 3.5 %prepare.1 = (bf16[64,128,256]{2,1,0:T(8,128)(2,1)S(1)}, f32[32,128]{1,0:T(8,128)S(1)}) custom-call(s32[129]{0:T(256)S(1)} %pad_add_fusion.table_ref.table_hbm, f32[64,128,128]{2,1,0:T(8,128)} %vals_hbm), custom_call_target="tpu_custom_call" | custom-call | flops 2000000000 | bytes 8388608 | tf_op jit(solution)/shard_map/prepare/pallas_call | solution.py:26
  14.3 2.6 %collective-permute-start.9 = (f32[8,32,128]{2,1,0:T(8,128)S(1)}, f32[8,32,128]{2,1,0:T(8,128)S(1)}, u32[]{:S(2)}, u32[]{:S(2)}) collective-permute-start(f32[8,32,128]{2,1,0:T(8,128)S(1)} %join.2.refs_0_), channel_id=1, source_target_pairs={{0,12},{4,8},{8,4},{12,0},{16,28},{20,24},{24,20},{28,16},{1,13},{... | collective-permute-start | bytes 393224 | tf_op jit(solution)/shard_map/ppermute | solution.py:368
  18.6 3.0 %collective-permute-done = f32[32,128]{1,0:T(8,128)S(1)} collective-permute-done((f32[32,128]{1,0:T(8,128)S(1)}, f32[32,128]{1,0:T(8,128)S(1)}, u32[]{:S(2)}, u32[]{:S(2)}) %collective-permute-start) | collective-permute-done | bytes 16416 | tf_op jit(solution)/shard_map/ppermute | solution.py:368
  21.7 2.5 %collective-permute-start.5 = (f32[32,128]{1,0:T(8,128)S(1)}, f32[32,128]{1,0:T(8,128)S(1)}, u32[]{:S(2)}, u32[]{:S(2)}) collective-permute-start(f32[32,128]{1,0:T(8,128)S(1)} %bitcast.15), channel_id=1, source_target_pairs={{0,4},{4,0},{8,12},{12,8},{16,20},{20,16},{24,28},{28,24},{1,5},{5... | collective-permute-start | bytes 49160 | tf_op jit(solution)/shard_map/ppermute | solution.py:368
  31.5 2.5 %collective-permute-done.16.refs_3_ = f32[8,32,128]{2,1,0:T(8,128)S(1)} collective-permute-done((f32[8,32,128]{2,1,0:T(8,128)S(1)}, f32[8,32,128]{2,1,0:T(8,128)S(1)}, u32[]{:S(2)}, u32[]{:S(2)}) %collective-permute-start.16) | collective-permute-done | bytes 131104 | tf_op jit(solution)/shard_map/ppermute | solution.py:368
  34.9 2.2 %products.6 = (f32[48,32,128]{2,1,0:T(8,128)S(1)}, f32[8,32,128]{2,1,0:T(8,128)S(1)}, f32[8,32,128]{2,1,0:T(8,128)S(1)}, f32[8,32,128]{2,1,0:T(8,128)S(1)}, f32[8,32,128]{2,1,0:T(8,128)S(1)}) custom-call(s32[129]{0:T(256)S(1)} %pad_add_fusion.table_ref.table_hbm, f32[8,32,128]{2,1,0:T(8,128)S(1)} %join.2.refs_0_, ...), custom_call_target="tpu_custom_call" | custom-call | flops 3000000000 | bytes 4194304 | tf_op jit(solution)/shard_map/products/pallas_call | solution.py:26
  40.7 2.2 %products.7 = (f32[48,32,128]{2,1,0:T(8,128)S(1)}, f32[8,32,128]{2,1,0:T(8,128)S(1)}, f32[8,32,128]{2,1,0:T(8,128)S(1)}, f32[8,32,128]{2,1,0:T(8,128)S(1)}, f32[8,32,128]{2,1,0:T(8,128)S(1)}) custom-call(s32[129]{0:T(256)S(1)} %pad_add_fusion.table_ref.table_hbm, f32[8,32,128]{2,1,0:T(8,128)S(1)} %join.3.refs_0_, ...), custom_call_target="tpu_custom_call" | custom-call | flops 3000000000 | bytes 4194304 | tf_op jit(solution)/shard_map/products/pallas_call | solution.py:26
  46.5 2.9 %collective-permute-start.19 = (f32[8,32,128]{2,1,0:T(8,128)S(1)}, f32[8,32,128]{2,1,0:T(8,128)S(1)}, u32[]{:S(2)}, u32[]{:S(2)}) collective-permute-start(f32[8,32,128]{2,1,0:T(8,128)S(1)} %add.120.refs_0_), channel_id=1, source_target_pairs={{0,16},{4,20},{8,24},{12,28},{16,0},{20,4},{24,8},{28,12},{1,17},{... | collective-permute-start | bytes 393224 | tf_op jit(solution)/shard_map/ppermute | solution.py:368
  50.7 5.3 %collective-permute-done.25.refs_3_ = f32[8,32,128]{2,1,0:T(8,128)S(1)} collective-permute-done((f32[8,32,128]{2,1,0:T(8,128)S(1)}, f32[8,32,128]{2,1,0:T(8,128)S(1)}, u32[]{:S(2)}, u32[]{:S(2)}) %collective-permute-start.25) | collective-permute-done | bytes 131104 | tf_op jit(solution)/shard_map/ppermute | solution.py:368
  58.6 2.8 %collective-permute-start.21 = (f32[8,32,128]{2,1,0:T(8,128)S(1)}, f32[8,32,128]{2,1,0:T(8,128)S(1)}, u32[]{:S(2)}, u32[]{:S(2)}) collective-permute-start(f32[8,32,128]{2,1,0:T(8,128)S(1)} %add.121.refs_0_), channel_id=1, source_target_pairs={{0,8},{4,12},{8,0},{12,4},{16,24},{20,28},{24,16},{28,20},{1,9},{5... | collective-permute-start | bytes 393224 | tf_op jit(solution)/shard_map/ppermute | solution.py:368
  61.7 3.9 %collective-permute-done.26.refs_1_ = f32[8,32,128]{2,1,0:T(8,128)S(1)} collective-permute-done((f32[8,32,128]{2,1,0:T(8,128)S(1)}, f32[8,32,128]{2,1,0:T(8,128)S(1)}, u32[]{:S(2)}, u32[]{:S(2)}) %collective-permute-start.26) | collective-permute-done | bytes 131104 | tf_op jit(solution)/shard_map/ppermute | solution.py:368
  70.1 3.1 %collective-permute-done.28.refs_1_ = f32[8,32,128]{2,1,0:T(8,128)S(1)} collective-permute-done((f32[8,32,128]{2,1,0:T(8,128)S(1)}, f32[8,32,128]{2,1,0:T(8,128)S(1)}, u32[]{:S(2)}, u32[]{:S(2)}) %collective-permute-start.28) | collective-permute-done | bytes 131104 | tf_op jit(solution)/shard_map/ppermute | solution.py:368
  75.5 2.2 %products.8 = (f32[48,32,128]{2,1,0:T(8,128)S(1)}, f32[8,32,128]{2,1,0:T(8,128)S(1)}, f32[8,32,128]{2,1,0:T(8,128)S(1)}, f32[8,32,128]{2,1,0:T(8,128)S(1)}, f32[8,32,128]{2,1,0:T(8,128)S(1)}) custom-call(s32[129]{0:T(256)S(1)} %pad_add_fusion.table_ref.table_hbm, f32[8,32,128]{2,1,0:T(8,128)S(1)} %add.121.refs_0_, ...), custom_call_target="tpu_custom_call" | custom-call | flops 3000000000 | bytes 4194304 | tf_op jit(solution)/shard_map/products/pallas_call | solution.py:26
  88.1 2.5 %collective-permute-start.37 = (f32[8,32,128]{2,1,0:T(8,128)S(1)}, f32[8,32,128]{2,1,0:T(8,128)S(1)}, u32[]{:S(2)}, u32[]{:S(2)}) collective-permute-start(f32[8,32,128]{2,1,0:T(8,128)S(1)} %add.124.refs_0_), channel_id=1, source_target_pairs={{0,16},{4,20},{8,24},{12,28},{16,0},{20,4},{24,8},{28,12},{1,17},{... | collective-permute-start | bytes 393224 | tf_op jit(solution)/shard_map/ppermute | solution.py:368
  91.4 5.4 %collective-permute-done.43.refs_3_ = f32[8,32,128]{2,1,0:T(8,128)S(1)} collective-permute-done((f32[8,32,128]{2,1,0:T(8,128)S(1)}, f32[8,32,128]{2,1,0:T(8,128)S(1)}, u32[]{:S(2)}, u32[]{:S(2)}) %collective-permute-start.43) | collective-permute-done | bytes 131104 | tf_op jit(solution)/shard_map/ppermute | solution.py:368
  99.0 3.9 %collective-permute-start.39 = (f32[8,32,128]{2,1,0:T(8,128)S(1)}, f32[8,32,128]{2,1,0:T(8,128)S(1)}, u32[]{:S(2)}, u32[]{:S(2)}) collective-permute-start(f32[8,32,128]{2,1,0:T(8,128)S(1)} %add.125.refs_0_), channel_id=1, source_target_pairs={{0,8},{4,12},{8,0},{12,4},{16,24},{20,28},{24,16},{28,20},{1,9},{5... | collective-permute-start | bytes 393224 | tf_op jit(solution)/shard_map/ppermute | solution.py:368
  103.4 2.6 %collective-permute-done.44.refs_1_ = f32[8,32,128]{2,1,0:T(8,128)S(1)} collective-permute-done((f32[8,32,128]{2,1,0:T(8,128)S(1)}, f32[8,32,128]{2,1,0:T(8,128)S(1)}, u32[]{:S(2)}, u32[]{:S(2)}) %collective-permute-start.44) | collective-permute-done | bytes 131104 | tf_op jit(solution)/shard_map/ppermute | solution.py:368
  117.0 2.2 %products.10 = (f32[48,32,128]{2,1,0:T(8,128)S(1)}, f32[8,32,128]{2,1,0:T(8,128)S(1)}, f32[8,32,128]{2,1,0:T(8,128)S(1)}, f32[8,32,128]{2,1,0:T(8,128)S(1)}, f32[8,32,128]{2,1,0:T(8,128)S(1)}) custom-call(s32[129]{0:T(256)S(1)} %pad_add_fusion.table_ref.table_hbm, f32[8,32,128]{2,1,0:T(8,128)S(1)} %add.125.refs_0_, ...), custom_call_target="tpu_custom_call" | custom-call | flops 3000000000 | bytes 4194304 | tf_op jit(solution)/shard_map/products/pallas_call | solution.py:26
  128.8 2.5 %collective-permute-start.55 = (f32[8,32,128]{2,1,0:T(8,128)S(1)}, f32[8,32,128]{2,1,0:T(8,128)S(1)}, u32[]{:S(2)}, u32[]{:S(2)}) collective-permute-start(f32[8,32,128]{2,1,0:T(8,128)S(1)} %add.128.refs_0_), channel_id=1, source_target_pairs={{0,16},{4,20},{8,24},{12,28},{16,0},{20,4},{24,8},{28,12},{1,17},{... | collective-permute-start | bytes 393224 | tf_op jit(solution)/shard_map/ppermute | solution.py:368
  132.4 5.7 %collective-permute-done.58.refs_3_ = f32[8,32,128]{2,1,0:T(8,128)S(1)} collective-permute-done((f32[8,32,128]{2,1,0:T(8,128)S(1)}, f32[8,32,128]{2,1,0:T(8,128)S(1)}, u32[]{:S(2)}, u32[]{:S(2)}) %collective-permute-start.58) | collective-permute-done | bytes 131104 | tf_op jit(solution)/shard_map/ppermute | solution.py:368
  138.7 8.9 %collective-permute-done.59.refs_5_ = f32[8,32,128]{2,1,0:T(8,128)S(1)} collective-permute-done((f32[8,32,128]{2,1,0:T(8,128)S(1)}, f32[8,32,128]{2,1,0:T(8,128)S(1)}, u32[]{:S(2)}, u32[]{:S(2)}) %collective-permute-start.59) | collective-permute-done | bytes 131104 | tf_op jit(solution)/shard_map/ppermute | solution.py:368
  150.1 2.3 %collective-permute-done.61 = f32[64,64]{1,0:T(8,128)S(1)} collective-permute-done((f32[64,64]{1,0:T(8,128)S(1)}, f32[64,64]{1,0:T(8,128)S(1)}, u32[]{:S(2)}, u32[]{:S(2)}) %collective-permute-start.61) | collective-permute-done | bytes 16416 | tf_op jit(solution)/shard_map/ppermute | solution.py:379
  158.6 2.8 %solve.1 = f32[64,512]{1,0:T(8,128)} custom-call(f32[64,64]{1,0:T(8,128)S(1)} %add_add_fusion.refs_0_, f32[64,64]{1,0:T(8,128)S(1)} %collective-permute-done.63.refs_1_, f32[64,64]{1,0:T(8,128)S(1)} %collective-permute-done.64.refs_2_, f32[64,64]{1,0:T(8,128)S(1)} %collective-permute-done.65.refs_3_, f32[4,64,128]{2,1,0:T(8,128)S(1)} %get-tuple-element.150.refs_4_), custom_call_target="tpu_custom_call" | custom-call | tf_op jit(solution)/shard_map/solve/pallas_call | solution.py:26
  (146 shorter events, 78.7 us)
Async XLA Ops:
  0.9 9.3 %collective-permute-start.2 = (f32[4,32,128]{2,1,0:T(8,128)S(1)}, f32[4,32,128]{2,1,0:T(8,128)S(1)}, u32[]{:S(2)}, u32[]{:S(2)}) collective-permute-start(f32[4,32,128]{2,1,0:T(8,128)S(1)} %get-tuple-element.151.chain_ref), channel_id=1, source_target_pairs={{0,16},{4,20},{8,24},{12,28},{16,0},{20,4},{24,8},{28,12},{1,17},{... | collective-permute-start | bytes 196616 | tf_op jit(solution)/shard_map/ppermute | solution.py:368
  11.5 10.1 %collective-permute-start.3 = (f32[8,32,128]{2,1,0:T(8,128)S(1)}, f32[8,32,128]{2,1,0:T(8,128)S(1)}, u32[]{:S(2)}, u32[]{:S(2)}) collective-permute-start(f32[8,32,128]{2,1,0:T(8,128)S(1)} %join.2.refs_0_), channel_id=1, source_target_pairs={{0,4},{4,0},{8,12},{12,8},{16,20},{20,16},{24,28},{28,24},{1,5},{5... | collective-permute-start | bytes 393224 | tf_op jit(solution)/shard_map/ppermute | solution.py:368
  13.3 8.3 %collective-permute-start.4 = (f32[8,32,128]{2,1,0:T(8,128)S(1)}, f32[8,32,128]{2,1,0:T(8,128)S(1)}, u32[]{:S(2)}, u32[]{:S(2)}) collective-permute-start(f32[8,32,128]{2,1,0:T(8,128)S(1)} %join.3.refs_0_), channel_id=1, source_target_pairs={{0,4},{4,0},{8,12},{12,8},{16,20},{20,16},{24,28},{28,24},{1,5},{5... | collective-permute-start | bytes 393224 | tf_op jit(solution)/shard_map/ppermute | solution.py:368
  13.7 16.7 %collective-permute-start.8 = (f32[8,32,128]{2,1,0:T(8,128)S(1)}, f32[8,32,128]{2,1,0:T(8,128)S(1)}, u32[]{:S(2)}, u32[]{:S(2)}) collective-permute-start(f32[8,32,128]{2,1,0:T(8,128)S(1)} %join.2.refs_0_), channel_id=1, source_target_pairs={{0,8},{4,12},{8,0},{12,4},{16,24},{20,28},{24,16},{28,20},{1,9},{5... | collective-permute-start | bytes 393224 | tf_op jit(solution)/shard_map/ppermute | solution.py:368
  14.3 16.1 %collective-permute-start.9 = (f32[8,32,128]{2,1,0:T(8,128)S(1)}, f32[8,32,128]{2,1,0:T(8,128)S(1)}, u32[]{:S(2)}, u32[]{:S(2)}) collective-permute-start(f32[8,32,128]{2,1,0:T(8,128)S(1)} %join.2.refs_0_), channel_id=1, source_target_pairs={{0,12},{4,8},{8,4},{12,0},{16,28},{20,24},{24,20},{28,16},{1,13},{... | collective-permute-start | bytes 393224 | tf_op jit(solution)/shard_map/ppermute | solution.py:368
  38.2 8.2 %collective-permute-start.13 = (f32[8,32,128]{2,1,0:T(8,128)S(1)}, f32[8,32,128]{2,1,0:T(8,128)S(1)}, u32[]{:S(2)}, u32[]{:S(2)}) collective-permute-start(f32[8,32,128]{2,1,0:T(8,128)S(1)} %get-tuple-element.91), channel_id=1, source_target_pairs={{0,8},{4,12},{8,0},{12,4},{16,24},{20,28},{24,16},{28,20},{1,9},{5... | collective-permute-start | bytes 393224 | tf_op jit(solution)/shard_map/ppermute | solution.py:368
  44.7 11.3 %collective-permute-start.25 = (f32[8,32,128]{2,1,0:T(8,128)S(1)}, f32[8,32,128]{2,1,0:T(8,128)S(1)}, u32[]{:S(2)}, u32[]{:S(2)}) collective-permute-start(f32[8,32,128]{2,1,0:T(8,128)S(1)} %get-tuple-element.102), channel_id=1, source_target_pairs={{0,12},{4,8},{8,4},{12,0},{16,28},{20,24},{24,20},{28,16},{1,13},{... | collective-permute-start | bytes 393224 | tf_op jit(solution)/shard_map/ppermute | solution.py:368
  46.5 9.5 %collective-permute-start.19 = (f32[8,32,128]{2,1,0:T(8,128)S(1)}, f32[8,32,128]{2,1,0:T(8,128)S(1)}, u32[]{:S(2)}, u32[]{:S(2)}) collective-permute-start(f32[8,32,128]{2,1,0:T(8,128)S(1)} %add.120.refs_0_), channel_id=1, source_target_pairs={{0,16},{4,20},{8,24},{12,28},{16,0},{20,4},{24,8},{28,12},{1,17},{... | collective-permute-start | bytes 393224 | tf_op jit(solution)/shard_map/ppermute | solution.py:368
  56.1 9.5 %collective-permute-start.26 = (f32[8,32,128]{2,1,0:T(8,128)S(1)}, f32[8,32,128]{2,1,0:T(8,128)S(1)}, u32[]{:S(2)}, u32[]{:S(2)}) collective-permute-start(f32[8,32,128]{2,1,0:T(8,128)S(1)} %add.122.refs_0_), channel_id=1, source_target_pairs={{0,16},{4,20},{8,24},{12,28},{16,0},{20,4},{24,8},{28,12},{1,17},{... | collective-permute-start | bytes 393224 | tf_op jit(solution)/shard_map/ppermute | solution.py:368
  57.1 8.4 %collective-permute-start.20 = (f32[8,32,128]{2,1,0:T(8,128)S(1)}, f32[8,32,128]{2,1,0:T(8,128)S(1)}, u32[]{:S(2)}, u32[]{:S(2)}) collective-permute-start(f32[8,32,128]{2,1,0:T(8,128)S(1)} %add.121.refs_0_), channel_id=1, source_target_pairs={{0,4},{4,0},{8,12},{12,8},{16,20},{20,16},{24,28},{28,24},{1,5},{5... | collective-permute-start | bytes 393224 | tf_op jit(solution)/shard_map/ppermute | solution.py:368
  58.6 10.5 %collective-permute-start.21 = (f32[8,32,128]{2,1,0:T(8,128)S(1)}, f32[8,32,128]{2,1,0:T(8,128)S(1)}, u32[]{:S(2)}, u32[]{:S(2)}) collective-permute-start(f32[8,32,128]{2,1,0:T(8,128)S(1)} %add.121.refs_0_), channel_id=1, source_target_pairs={{0,8},{4,12},{8,0},{12,4},{16,24},{20,28},{24,16},{28,20},{1,9},{5... | collective-permute-start | bytes 393224 | tf_op jit(solution)/shard_map/ppermute | solution.py:368
  78.9 8.2 %collective-permute-start.33 = (f32[8,32,128]{2,1,0:T(8,128)S(1)}, f32[8,32,128]{2,1,0:T(8,128)S(1)}, u32[]{:S(2)}, u32[]{:S(2)}) collective-permute-start(f32[8,32,128]{2,1,0:T(8,128)S(1)} %get-tuple-element.115), channel_id=1, source_target_pairs={{0,8},{4,12},{8,0},{12,4},{16,24},{20,28},{24,16},{28,20},{1,9},{5... | collective-permute-start | bytes 393224 | tf_op jit(solution)/shard_map/ppermute | solution.py:368
  79.3 8.8 %collective-permute-start.34 = (f32[8,32,128]{2,1,0:T(8,128)S(1)}, f32[8,32,128]{2,1,0:T(8,128)S(1)}, u32[]{:S(2)}, u32[]{:S(2)}) collective-permute-start(f32[8,32,128]{2,1,0:T(8,128)S(1)} %get-tuple-element.116), channel_id=1, source_target_pairs={{0,12},{4,8},{8,4},{12,0},{16,28},{20,24},{24,20},{28,16},{1,13},{... | collective-permute-start | bytes 393224 | tf_op jit(solution)/shard_map/ppermute | solution.py:368
  85.1 11.7 %collective-permute-start.43 = (f32[8,32,128]{2,1,0:T(8,128)S(1)}, f32[8,32,128]{2,1,0:T(8,128)S(1)}, u32[]{:S(2)}, u32[]{:S(2)}) collective-permute-start(f32[8,32,128]{2,1,0:T(8,128)S(1)} %get-tuple-element.124), channel_id=1, source_target_pairs={{0,12},{4,8},{8,4},{12,0},{16,28},{20,24},{24,20},{28,16},{1,13},{... | collective-permute-start | bytes 393224 | tf_op jit(solution)/shard_map/ppermute | solution.py:368
  88.1 8.7 %collective-permute-start.37 = (f32[8,32,128]{2,1,0:T(8,128)S(1)}, f32[8,32,128]{2,1,0:T(8,128)S(1)}, u32[]{:S(2)}, u32[]{:S(2)}) collective-permute-start(f32[8,32,128]{2,1,0:T(8,128)S(1)} %add.124.refs_0_), channel_id=1, source_target_pairs={{0,16},{4,20},{8,24},{12,28},{16,0},{20,4},{24,8},{28,12},{1,17},{... | collective-permute-start | bytes 393224 | tf_op jit(solution)/shard_map/ppermute | solution.py:368
  96.9 9.2 %collective-permute-start.44 = (f32[8,32,128]{2,1,0:T(8,128)S(1)}, f32[8,32,128]{2,1,0:T(8,128)S(1)}, u32[]{:S(2)}, u32[]{:S(2)}) collective-permute-start(f32[8,32,128]{2,1,0:T(8,128)S(1)} %add.126.refs_0_), channel_id=1, source_target_pairs={{0,16},{4,20},{8,24},{12,28},{16,0},{20,4},{24,8},{28,12},{1,17},{... | collective-permute-start | bytes 393224 | tf_op jit(solution)/shard_map/ppermute | solution.py:368
  98.0 8.1 %collective-permute-start.38 = (f32[8,32,128]{2,1,0:T(8,128)S(1)}, f32[8,32,128]{2,1,0:T(8,128)S(1)}, u32[]{:S(2)}, u32[]{:S(2)}) collective-permute-start(f32[8,32,128]{2,1,0:T(8,128)S(1)} %add.125.refs_0_), channel_id=1, source_target_pairs={{0,4},{4,0},{8,12},{12,8},{16,20},{20,16},{24,28},{28,24},{1,5},{5... | collective-permute-start | bytes 393224 | tf_op jit(solution)/shard_map/ppermute | solution.py:368
  99.0 10.6 %collective-permute-start.39 = (f32[8,32,128]{2,1,0:T(8,128)S(1)}, f32[8,32,128]{2,1,0:T(8,128)S(1)}, u32[]{:S(2)}, u32[]{:S(2)}) collective-permute-start(f32[8,32,128]{2,1,0:T(8,128)S(1)} %add.125.refs_0_), channel_id=1, source_target_pairs={{0,8},{4,12},{8,0},{12,4},{16,24},{20,28},{24,16},{28,20},{1,9},{5... | collective-permute-start | bytes 393224 | tf_op jit(solution)/shard_map/ppermute | solution.py:368
  102.9 8.6 %collective-permute-start.40 = (f32[8,32,128]{2,1,0:T(8,128)S(1)}, f32[8,32,128]{2,1,0:T(8,128)S(1)}, u32[]{:S(2)}, u32[]{:S(2)}) collective-permute-start(f32[8,32,128]{2,1,0:T(8,128)S(1)} %add.125.refs_0_), channel_id=1, source_target_pairs={{0,12},{4,8},{8,4},{12,0},{16,28},{20,24},{24,20},{28,16},{1,13},{... | collective-permute-start | bytes 393224 | tf_op jit(solution)/shard_map/ppermute | solution.py:368
  119.2 8.9 %collective-permute-start.50 = (f32[8,32,128]{2,1,0:T(8,128)S(1)}, f32[8,32,128]{2,1,0:T(8,128)S(1)}, u32[]{:S(2)}, u32[]{:S(2)}) collective-permute-start(f32[8,32,128]{2,1,0:T(8,128)S(1)} %get-tuple-element.136), channel_id=1, source_target_pairs={{0,4},{4,0},{8,12},{12,8},{16,20},{20,16},{24,28},{28,24},{1,5},{5... | collective-permute-start | bytes 393224 | tf_op jit(solution)/shard_map/ppermute | solution.py:368
  120.3 8.3 %collective-permute-start.51 = (f32[8,32,128]{2,1,0:T(8,128)S(1)}, f32[8,32,128]{2,1,0:T(8,128)S(1)}, u32[]{:S(2)}, u32[]{:S(2)}) collective-permute-start(f32[8,32,128]{2,1,0:T(8,128)S(1)} %get-tuple-element.137), channel_id=1, source_target_pairs={{0,8},{4,12},{8,0},{12,4},{16,24},{20,28},{24,16},{28,20},{1,9},{5... | collective-permute-start | bytes 393224 | tf_op jit(solution)/shard_map/ppermute | solution.py:368
  128.1 10.1 %collective-permute-start.58 = (f32[8,32,128]{2,1,0:T(8,128)S(1)}, f32[8,32,128]{2,1,0:T(8,128)S(1)}, u32[]{:S(2)}, u32[]{:S(2)}) collective-permute-start(f32[8,32,128]{2,1,0:T(8,128)S(1)} %get-tuple-element.147), channel_id=1, source_target_pairs={{0,12},{4,8},{8,4},{12,0},{16,28},{20,24},{24,20},{28,16},{1,13},{... | collective-permute-start | bytes 393224 | tf_op jit(solution)/shard_map/ppermute | solution.py:368
  128.8 9.9 %collective-permute-start.55 = (f32[8,32,128]{2,1,0:T(8,128)S(1)}, f32[8,32,128]{2,1,0:T(8,128)S(1)}, u32[]{:S(2)}, u32[]{:S(2)}) collective-permute-start(f32[8,32,128]{2,1,0:T(8,128)S(1)} %add.128.refs_0_), channel_id=1, source_target_pairs={{0,16},{4,20},{8,24},{12,28},{16,0},{20,4},{24,8},{28,12},{1,17},{... | collective-permute-start | bytes 393224 | tf_op jit(solution)/shard_map/ppermute | solution.py:368
  138.2 9.4 %collective-permute-start.59 = (f32[8,32,128]{2,1,0:T(8,128)S(1)}, f32[8,32,128]{2,1,0:T(8,128)S(1)}, u32[]{:S(2)}, u32[]{:S(2)}) collective-permute-start(f32[8,32,128]{2,1,0:T(8,128)S(1)} %add.129.refs_4_), channel_id=1, source_target_pairs={{0,16},{4,20},{8,24},{12,28},{16,0},{20,4},{24,8},{28,12},{1,17},{... | collective-permute-start | bytes 393224 | tf_op jit(solution)/shard_map/ppermute | solution.py:368
  (43 other events, 251.1 us)

commit v6 on v5

--- a/solution.py
+++ b/solution.py
@@ -406,10 +406,10 @@
 
     tiles, degree = prepare_tiles(tile_vals, table, group_blocks)
     others = [over_blk(chain, quad_count) for chain in chains]
-    others[0] = after(others[0], [degree, *others[1:]])
+    others[0] = after(others[0], degree)
     other = over_blk(degree, quad_count)
     gathered = [spread(join_halves(flags, x, y)) for x, y in zip(chains, others)]
-    other = after(other, [x[1] for x in gathered])
+    other = after(other, [gathered[0][1], gathered[1][1:3]])
     degrees = spread(add_all([degree[None], other[None]])[0])
     root, own_degree, inverse = call(
         functools.partial(roots, part=part),
@@ -436,7 +436,7 @@
             sums[c] = after(sums[c], parts[c + 1][0])
         totals, pieces = [], []
         for c in range(CHAINS):
-            mine = after(sums[c], other) if c else sums[c]
+            mine = sums[c]
             other = over_blk(mine, quad_count)
             arrived = after(other, pieces[c - 1][1]) if c else other
             totals.append(add_all([mine, arrived], inverse))
@@ -454,8 +454,6 @@
             states[c].append(state)
 
     sums = [gather_sum(parts[c]) for c in range(CHAINS)]
-    for c in range(CHAINS - 1):
-        sums[c] = after(sums[c], parts[c + 1][0])
     groups = [
         [sums[c], over_blk(sums[c], quad_count), states[c][-1], states[c][-2]]
         for c in range(CHAINS)

time: 162 us -> 158 us (0.975)
  starting transfers between devices: 77.6 us -> 69.9 us
  waiting for transfers between devices: 60 us -> 63.8 us
    ppermute x48, starting transfers between devices: 67.4 us -> 59.4 us  [over_blk(): return lax.ppermute(x, 'blk', [(i, i ^ k) for i in range(blk_count)])]
    ppermute x48, waiting for transfers between devices: 55.1 us -> 59 us  [over_blk(): return lax.ppermute(x, 'blk', [(i, i ^ k) for i in range(blk_count)])]
  transfers between devices with their start and end apart: 66 -> 66, of which waited for: 29 -> 31; matrix products, arithmetic and copies ran while one was open for 1% -> 1% of each run, Pallas kernels for 11% -> 11%
where the time goes in v6:
time: 158 us; the launch traced here: 157 us
  starting transfers between devices  69.9 us (44%)
  waiting for transfers between devices  63.8 us (40%)
  Pallas kernels  20.8 us (13%)
    ppermute x48, starting transfers between devices, over_blk(): return lax.ppermute(x, 'blk', [(i, i ^ k) for i in range(blk_count)])  59.4 us
    ppermute x48, waiting for transfers between devices, over_blk(): return lax.ppermute(x, 'blk', [(i, i ^ k) for i in range(blk_count)])  59 us
    pallas_call x29, Pallas kernels, call(): pl.pallas_call(kernel, in_specs=in_specs or [VMEM] * len(operands), out_s...  20.8 us
    ppermute x6, starting transfers between devices, over_all(): return lax.ppermute(x, ('blk', 'rows'), pairs)  5.48 us
    ppermute x6, waiting for transfers between devices, over_all(): return lax.ppermute(x, ('blk', 'rows'), pairs)  4.79 us
    ppermute x6, starting transfers between devices, with_far(): return lax.ppermute(x, 'rows', pairs + [(b, a) for a, b in pairs])  4.18 us
  transfers between devices with their start and end apart: 66, of which 31 were waited for; matrix products, arithmetic and copies ran while one was open for 1% of the time, Pallas kernels for 11%

profile of v6, /device:TPU:0, one launch (start us, length us, event | category | flops | bytes accessed | tf_op | source)
XLA Modules:
  0.0 157.4 jit_solution(6108031552954887703)
XLA Ops:
  0.9 4.1 %collective-permute-start.1 = (f32[4,32,128]{2,1,0:T(8,128)S(1)}, f32[4,32,128]{2,1,0:T(8,128)S(1)}, u32[]{:S(2)}, u32[]{:S(2)}) collective-permute-start(f32[4,32,128]{2,1,0:T(8,128)S(1)} %get-tuple-element.146.chain_ref), channel_id=1, source_target_pairs={{0,16},{4,20},{8,24},{12,28},{16,0},{20,4},{24,8},{28,12},{1,17},{... | collective-permute-start | bytes 196616 | tf_op jit(solution)/shard_map/ppermute | solution.py:368
  6.7 3.5 %prepare.1 = (bf16[64,128,256]{2,1,0:T(8,128)(2,1)S(1)}, f32[32,128]{1,0:T(8,128)S(1)}) custom-call(s32[129]{0:T(256)S(1)} %pad_add_fusion.table_ref.table_hbm, f32[64,128,128]{2,1,0:T(8,128)} %vals_hbm), custom_call_target="tpu_custom_call" | custom-call | flops 2000000000 | bytes 8388608 | tf_op jit(solution)/shard_map/prepare/pallas_call | solution.py:26
  14.3 2.8 %collective-permute-start = (f32[32,128]{1,0:T(8,128)S(1)}, f32[32,128]{1,0:T(8,128)S(1)}, u32[]{:S(2)}, u32[]{:S(2)}) collective-permute-start(f32[32,128]{1,0:T(8,128)S(1)} %get-tuple-element.78), channel_id=1, source_target_pairs={{0,16},{4,20},{8,24},{12,28},{16,0},{20,4},{24,8},{28,12},{1,17},{... | collective-permute-start | bytes 49160 | tf_op jit(solution)/shard_map/ppermute | solution.py:368
  19.1 2.9 %collective-permute-start.9 = (f32[8,32,128]{2,1,0:T(8,128)S(1)}, f32[8,32,128]{2,1,0:T(8,128)S(1)}, u32[]{:S(2)}, u32[]{:S(2)}) collective-permute-start(f32[8,32,128]{2,1,0:T(8,128)S(1)} %join.2.refs_0_), channel_id=1, source_target_pairs={{0,8},{4,12},{8,0},{12,4},{16,24},{20,28},{24,16},{28,20},{1,9},{5... | collective-permute-start | bytes 393224 | tf_op jit(solution)/shard_map/ppermute | solution.py:368
  29.0 2.8 %collective-permute-done.16.refs_3_ = f32[8,32,128]{2,1,0:T(8,128)S(1)} collective-permute-done((f32[8,32,128]{2,1,0:T(8,128)S(1)}, f32[8,32,128]{2,1,0:T(8,128)S(1)}, u32[]{:S(2)}, u32[]{:S(2)}) %collective-permute-start.16) | collective-permute-done | bytes 131104 | tf_op jit(solution)/shard_map/ppermute | solution.py:368
  32.7 2.2 %products.6 = (f32[48,32,128]{2,1,0:T(8,128)S(1)}, f32[8,32,128]{2,1,0:T(8,128)S(1)}, f32[8,32,128]{2,1,0:T(8,128)S(1)}, f32[8,32,128]{2,1,0:T(8,128)S(1)}, f32[8,32,128]{2,1,0:T(8,128)S(1)}) custom-call(s32[129]{0:T(256)S(1)} %pad_add_fusion.table_ref.table_hbm, f32[8,32,128]{2,1,0:T(8,128)S(1)} %join.2.refs_0_, ...), custom_call_target="tpu_custom_call" | custom-call | flops 3000000000 | bytes 4194304 | tf_op jit(solution)/shard_map/products/pallas_call | solution.py:26
  46.4 2.6 %collective-permute-done.23.refs_1_ = f32[8,32,128]{2,1,0:T(8,128)S(1)} collective-permute-done((f32[8,32,128]{2,1,0:T(8,128)S(1)}, f32[8,32,128]{2,1,0:T(8,128)S(1)}, u32[]{:S(2)}, u32[]{:S(2)}) %collective-permute-start.23) | collective-permute-done | bytes 131104 | tf_op jit(solution)/shard_map/ppermute | solution.py:368
  49.0 4.4 %collective-permute-done.25.refs_3_ = f32[8,32,128]{2,1,0:T(8,128)S(1)} collective-permute-done((f32[8,32,128]{2,1,0:T(8,128)S(1)}, f32[8,32,128]{2,1,0:T(8,128)S(1)}, u32[]{:S(2)}, u32[]{:S(2)}) %collective-permute-start.25) | collective-permute-done | bytes 131104 | tf_op jit(solution)/shard_map/ppermute | solution.py:368
  58.5 4.0 %collective-permute-done.26.refs_1_ = f32[8,32,128]{2,1,0:T(8,128)S(1)} collective-permute-done((f32[8,32,128]{2,1,0:T(8,128)S(1)}, f32[8,32,128]{2,1,0:T(8,128)S(1)}, u32[]{:S(2)}, u32[]{:S(2)}) %collective-permute-start.26) | collective-permute-done | bytes 131104 | tf_op jit(solution)/shard_map/ppermute | solution.py:368
  63.5 2.6 %collective-permute-start.30 = (f32[8,32,128]{2,1,0:T(8,128)S(1)}, f32[8,32,128]{2,1,0:T(8,128)S(1)}, u32[]{:S(2)}, u32[]{:S(2)}) collective-permute-start(f32[8,32,128]{2,1,0:T(8,128)S(1)} %add.123.refs_0_), channel_id=1, source_target_pairs={{0,12},{4,8},{8,4},{12,0},{16,28},{20,24},{24,20},{28,16},{1,13},{... | collective-permute-start | bytes 393224 | tf_op jit(solution)/shard_map/ppermute | solution.py:368
  73.5 2.2 %products.8 = (f32[48,32,128]{2,1,0:T(8,128)S(1)}, f32[8,32,128]{2,1,0:T(8,128)S(1)}, f32[8,32,128]{2,1,0:T(8,128)S(1)}, f32[8,32,128]{2,1,0:T(8,128)S(1)}, f32[8,32,128]{2,1,0:T(8,128)S(1)}) custom-call(s32[129]{0:T(256)S(1)} %pad_add_fusion.table_ref.table_hbm, f32[8,32,128]{2,1,0:T(8,128)S(1)} %add.121.refs_0_, ...), custom_call_target="tpu_custom_call" | custom-call | flops 3000000000 | bytes 4194304 | tf_op jit(solution)/shard_map/products/pallas_call | solution.py:26
  79.2 2.2 %products.9 = (f32[48,32,128]{2,1,0:T(8,128)S(1)}, f32[8,32,128]{2,1,0:T(8,128)S(1)}, f32[8,32,128]{2,1,0:T(8,128)S(1)}, f32[8,32,128]{2,1,0:T(8,128)S(1)}, f32[8,32,128]{2,1,0:T(8,128)S(1)}) custom-call(s32[129]{0:T(256)S(1)} %pad_add_fusion.table_ref.table_hbm, f32[8,32,128]{2,1,0:T(8,128)S(1)} %add.123.refs_0_, ...), custom_call_target="tpu_custom_call" | custom-call | flops 3000000000 | bytes 4194304 | tf_op jit(solution)/shard_map/products/pallas_call | solution.py:26
  86.8 2.6 %collective-permute-done.41.refs_1_ = f32[8,32,128]{2,1,0:T(8,128)S(1)} collective-permute-done((f32[8,32,128]{2,1,0:T(8,128)S(1)}, f32[8,32,128]{2,1,0:T(8,128)S(1)}, u32[]{:S(2)}, u32[]{:S(2)}) %collective-permute-start.41) | collective-permute-done | bytes 131104 | tf_op jit(solution)/shard_map/ppermute | solution.py:368
  89.5 3.7 %collective-permute-done.43.refs_3_ = f32[8,32,128]{2,1,0:T(8,128)S(1)} collective-permute-done((f32[8,32,128]{2,1,0:T(8,128)S(1)}, f32[8,32,128]{2,1,0:T(8,128)S(1)}, u32[]{:S(2)}, u32[]{:S(2)}) %collective-permute-start.43) | collective-permute-done | bytes 131104 | tf_op jit(solution)/shard_map/ppermute | solution.py:368
  99.1 3.1 %collective-permute-done.44.refs_1_ = f32[8,32,128]{2,1,0:T(8,128)S(1)} collective-permute-done((f32[8,32,128]{2,1,0:T(8,128)S(1)}, f32[8,32,128]{2,1,0:T(8,128)S(1)}, u32[]{:S(2)}, u32[]{:S(2)}) %collective-permute-start.44) | collective-permute-done | bytes 131104 | tf_op jit(solution)/shard_map/ppermute | solution.py:368
  105.9 2.4 %collective-permute-done.40.refs_3_ = f32[8,32,128]{2,1,0:T(8,128)S(1)} collective-permute-done((f32[8,32,128]{2,1,0:T(8,128)S(1)}, f32[8,32,128]{2,1,0:T(8,128)S(1)}, u32[]{:S(2)}, u32[]{:S(2)}) %collective-permute-start.40) | collective-permute-done | bytes 131104 | tf_op jit(solution)/shard_map/ppermute | solution.py:368
  117.6 2.4 %collective-permute-start.52 = (f32[8,32,128]{2,1,0:T(8,128)S(1)}, f32[8,32,128]{2,1,0:T(8,128)S(1)}, u32[]{:S(2)}, u32[]{:S(2)}) collective-permute-start(f32[8,32,128]{2,1,0:T(8,128)S(1)} %get-tuple-element.133), channel_id=1, source_target_pairs={{0,12},{4,8},{8,4},{12,0},{16,28},{20,24},{24,20},{28,16},{1,13},{... | collective-permute-start | bytes 393224 | tf_op jit(solution)/shard_map/ppermute | solution.py:368
  123.4 2.4 %collective-permute-start.58 = (f32[8,32,128]{2,1,0:T(8,128)S(1)}, f32[8,32,128]{2,1,0:T(8,128)S(1)}, u32[]{:S(2)}, u32[]{:S(2)}) collective-permute-start(f32[8,32,128]{2,1,0:T(8,128)S(1)} %get-tuple-element.141), channel_id=1, source_target_pairs={{0,12},{4,8},{8,4},{12,0},{16,28},{20,24},{24,20},{28,16},{1,13},{... | collective-permute-start | bytes 393224 | tf_op jit(solution)/shard_map/ppermute | solution.py:368
  126.9 3.7 %collective-permute-done.56.refs_1_ = f32[8,32,128]{2,1,0:T(8,128)S(1)} collective-permute-done((f32[8,32,128]{2,1,0:T(8,128)S(1)}, f32[8,32,128]{2,1,0:T(8,128)S(1)}, u32[]{:S(2)}, u32[]{:S(2)}) %collective-permute-start.56) | collective-permute-done | bytes 131104 | tf_op jit(solution)/shard_map/ppermute | solution.py:368
  130.6 3.6 %collective-permute-done.58.refs_3_ = f32[8,32,128]{2,1,0:T(8,128)S(1)} collective-permute-done((f32[8,32,128]{2,1,0:T(8,128)S(1)}, f32[8,32,128]{2,1,0:T(8,128)S(1)}, u32[]{:S(2)}, u32[]{:S(2)}) %collective-permute-start.58) | collective-permute-done | bytes 131104 | tf_op jit(solution)/shard_map/ppermute | solution.py:368
  134.3 9.4 %collective-permute-done.59.refs_5_ = f32[8,32,128]{2,1,0:T(8,128)S(1)} collective-permute-done((f32[8,32,128]{2,1,0:T(8,128)S(1)}, f32[8,32,128]{2,1,0:T(8,128)S(1)}, u32[]{:S(2)}, u32[]{:S(2)}) %collective-permute-start.59) | collective-permute-done | bytes 131104 | tf_op jit(solution)/shard_map/ppermute | solution.py:368
  146.2 2.3 %collective-permute-done.61 = f32[64,64]{1,0:T(8,128)S(1)} collective-permute-done((f32[64,64]{1,0:T(8,128)S(1)}, f32[64,64]{1,0:T(8,128)S(1)}, u32[]{:S(2)}, u32[]{:S(2)}) %collective-permute-start.61) | collective-permute-done | bytes 16416 | tf_op jit(solution)/shard_map/ppermute | solution.py:379
  149.8 2.3 %collective-permute-start.65 = (f32[64,64]{1,0:T(8,128)S(1)}, f32[64,64]{1,0:T(8,128)S(1)}, u32[]{:S(2)}, u32[]{:S(2)}) collective-permute-start(f32[64,64]{1,0:T(8,128)S(1)} %add_add_fusion.refs_0_), channel_id=1, source_target_pairs={{0,12},{1,13},{2,14},{3,15},{4,8},{5,9},{6,10},{7,11},{8,4},{9,5},... | collective-permute-start | bytes 49160 | tf_op jit(solution)/shard_map/ppermute | solution.py:379
  154.6 2.8 %solve.1 = f32[64,512]{1,0:T(8,128)} custom-call(f32[64,64]{1,0:T(8,128)S(1)} %add_add_fusion.refs_0_, f32[64,64]{1,0:T(8,128)S(1)} %collective-permute-done.63.refs_1_, f32[64,64]{1,0:T(8,128)S(1)} %collective-permute-done.64.refs_2_, f32[64,64]{1,0:T(8,128)S(1)} %collective-permute-done.65.refs_3_, f32[4,64,128]{2,1,0:T(8,128)S(1)} %get-tuple-element.144.refs_4_), custom_call_target="tpu_custom_call" | custom-call | tf_op jit(solution)/shard_map/solve/pallas_call | solution.py:26
  (146 shorter events, 79.3 us)
Async XLA Ops:
  0.9 9.3 %collective-permute-start.1 = (f32[4,32,128]{2,1,0:T(8,128)S(1)}, f32[4,32,128]{2,1,0:T(8,128)S(1)}, u32[]{:S(2)}, u32[]{:S(2)}) collective-permute-start(f32[4,32,128]{2,1,0:T(8,128)S(1)} %get-tuple-element.146.chain_ref), channel_id=1, source_target_pairs={{0,16},{4,20},{8,24},{12,28},{16,0},{20,4},{24,8},{28,12},{1,17},{... | collective-permute-start | bytes 196616 | tf_op jit(solution)/shard_map/ppermute | solution.py:368
  10.3 11.8 %collective-permute-start.2 = (f32[8,32,128]{2,1,0:T(8,128)S(1)}, f32[8,32,128]{2,1,0:T(8,128)S(1)}, u32[]{:S(2)}, u32[]{:S(2)}) collective-permute-start(f32[8,32,128]{2,1,0:T(8,128)S(1)} %join.2.refs_0_), channel_id=1, source_target_pairs={{0,4},{4,0},{8,12},{12,8},{16,20},{20,16},{24,28},{28,24},{1,5},{5... | collective-permute-start | bytes 393224 | tf_op jit(solution)/shard_map/ppermute | solution.py:368
  12.1 9.9 %collective-permute-start.4 = (f32[8,32,128]{2,1,0:T(8,128)S(1)}, f32[8,32,128]{2,1,0:T(8,128)S(1)}, u32[]{:S(2)}, u32[]{:S(2)}) collective-permute-start(f32[8,32,128]{2,1,0:T(8,128)S(1)} %join.3.refs_0_), channel_id=1, source_target_pairs={{0,4},{4,0},{8,12},{12,8},{16,20},{20,16},{24,28},{28,24},{1,5},{5... | collective-permute-start | bytes 393224 | tf_op jit(solution)/shard_map/ppermute | solution.py:368
  13.3 8.7 %collective-permute-start.5 = (f32[8,32,128]{2,1,0:T(8,128)S(1)}, f32[8,32,128]{2,1,0:T(8,128)S(1)}, u32[]{:S(2)}, u32[]{:S(2)}) collective-permute-start(f32[8,32,128]{2,1,0:T(8,128)S(1)} %join.3.refs_0_), channel_id=1, source_target_pairs={{0,8},{4,12},{8,0},{12,4},{16,24},{20,28},{24,16},{28,20},{1,9},{5... | collective-permute-start | bytes 393224 | tf_op jit(solution)/shard_map/ppermute | solution.py:368
  17.1 11.1 %collective-permute-start.10 = (f32[8,32,128]{2,1,0:T(8,128)S(1)}, f32[8,32,128]{2,1,0:T(8,128)S(1)}, u32[]{:S(2)}, u32[]{:S(2)}) collective-permute-start(f32[8,32,128]{2,1,0:T(8,128)S(1)} %join.2.refs_0_), channel_id=1, source_target_pairs={{0,12},{4,8},{8,4},{12,0},{16,28},{20,24},{24,20},{28,16},{1,13},{... | collective-permute-start | bytes 393224 | tf_op jit(solution)/shard_map/ppermute | solution.py:368
  19.1 9.0 %collective-permute-start.9 = (f32[8,32,128]{2,1,0:T(8,128)S(1)}, f32[8,32,128]{2,1,0:T(8,128)S(1)}, u32[]{:S(2)}, u32[]{:S(2)}) collective-permute-start(f32[8,32,128]{2,1,0:T(8,128)S(1)} %join.2.refs_0_), channel_id=1, source_target_pairs={{0,8},{4,12},{8,0},{12,4},{16,24},{20,28},{24,16},{28,20},{1,9},{5... | collective-permute-start | bytes 393224 | tf_op jit(solution)/shard_map/ppermute | solution.py:368
  34.9 8.6 %collective-permute-start.13 = (f32[8,32,128]{2,1,0:T(8,128)S(1)}, f32[8,32,128]{2,1,0:T(8,128)S(1)}, u32[]{:S(2)}, u32[]{:S(2)}) collective-permute-start(f32[8,32,128]{2,1,0:T(8,128)S(1)} %get-tuple-element.87), channel_id=1, source_target_pairs={{0,4},{4,0},{8,12},{12,8},{16,20},{20,16},{24,28},{28,24},{1,5},{5... | collective-permute-start | bytes 393224 | tf_op jit(solution)/shard_map/ppermute | solution.py:368
  43.5 10.0 %collective-permute-start.25 = (f32[8,32,128]{2,1,0:T(8,128)S(1)}, f32[8,32,128]{2,1,0:T(8,128)S(1)}, u32[]{:S(2)}, u32[]{:S(2)}) collective-permute-start(f32[8,32,128]{2,1,0:T(8,128)S(1)} %get-tuple-element.99), channel_id=1, source_target_pairs={{0,12},{4,8},{8,4},{12,0},{16,28},{20,24},{24,20},{28,16},{1,13},{... | collective-permute-start | bytes 393224 | tf_op jit(solution)/shard_map/ppermute | solution.py:368
  45.0 10.0 %collective-permute-start.19 = (f32[8,32,128]{2,1,0:T(8,128)S(1)}, f32[8,32,128]{2,1,0:T(8,128)S(1)}, u32[]{:S(2)}, u32[]{:S(2)}) collective-permute-start(f32[8,32,128]{2,1,0:T(8,128)S(1)} %add.120.refs_0_), channel_id=1, source_target_pairs={{0,16},{4,20},{8,24},{12,28},{16,0},{20,4},{24,8},{28,12},{1,17},{... | collective-permute-start | bytes 393224 | tf_op jit(solution)/shard_map/ppermute | solution.py:368
  53.5 9.1 %collective-permute-start.26 = (f32[8,32,128]{2,1,0:T(8,128)S(1)}, f32[8,32,128]{2,1,0:T(8,128)S(1)}, u32[]{:S(2)}, u32[]{:S(2)}) collective-permute-start(f32[8,32,128]{2,1,0:T(8,128)S(1)} %add.122.refs_0_), channel_id=1, source_target_pairs={{0,16},{4,20},{8,24},{12,28},{16,0},{20,4},{24,8},{28,12},{1,17},{... | collective-permute-start | bytes 393224 | tf_op jit(solution)/shard_map/ppermute | solution.py:368
  56.4 9.7 %collective-permute-start.21 = (f32[8,32,128]{2,1,0:T(8,128)S(1)}, f32[8,32,128]{2,1,0:T(8,128)S(1)}, u32[]{:S(2)}, u32[]{:S(2)}) collective-permute-start(f32[8,32,128]{2,1,0:T(8,128)S(1)} %add.121.refs_0_), channel_id=1, source_target_pairs={{0,8},{4,12},{8,0},{12,4},{16,24},{20,28},{24,16},{28,20},{1,9},{5... | collective-permute-start | bytes 393224 | tf_op jit(solution)/shard_map/ppermute | solution.py:368
  57.0 10.4 %collective-permute-start.22 = (f32[8,32,128]{2,1,0:T(8,128)S(1)}, f32[8,32,128]{2,1,0:T(8,128)S(1)}, u32[]{:S(2)}, u32[]{:S(2)}) collective-permute-start(f32[8,32,128]{2,1,0:T(8,128)S(1)} %add.121.refs_0_), channel_id=1, source_target_pairs={{0,12},{4,8},{8,4},{12,0},{16,28},{20,24},{24,20},{28,16},{1,13},{... | collective-permute-start | bytes 393224 | tf_op jit(solution)/shard_map/ppermute | solution.py:368
  63.5 9.1 %collective-permute-start.30 = (f32[8,32,128]{2,1,0:T(8,128)S(1)}, f32[8,32,128]{2,1,0:T(8,128)S(1)}, u32[]{:S(2)}, u32[]{:S(2)}) collective-permute-start(f32[8,32,128]{2,1,0:T(8,128)S(1)} %add.123.refs_0_), channel_id=1, source_target_pairs={{0,12},{4,8},{8,4},{12,0},{16,28},{20,24},{24,20},{28,16},{1,13},{... | collective-permute-start | bytes 393224 | tf_op jit(solution)/shard_map/ppermute | solution.py:368
  77.3 8.8 %collective-permute-start.34 = (f32[8,32,128]{2,1,0:T(8,128)S(1)}, f32[8,32,128]{2,1,0:T(8,128)S(1)}, u32[]{:S(2)}, u32[]{:S(2)}) collective-permute-start(f32[8,32,128]{2,1,0:T(8,128)S(1)} %get-tuple-element.112), channel_id=1, source_target_pairs={{0,12},{4,8},{8,4},{12,0},{16,28},{20,24},{24,20},{28,16},{1,13},{... | collective-permute-start | bytes 393224 | tf_op jit(solution)/shard_map/ppermute | solution.py:368
  83.1 10.1 %collective-permute-start.43 = (f32[8,32,128]{2,1,0:T(8,128)S(1)}, f32[8,32,128]{2,1,0:T(8,128)S(1)}, u32[]{:S(2)}, u32[]{:S(2)}) collective-permute-start(f32[8,32,128]{2,1,0:T(8,128)S(1)} %get-tuple-element.120), channel_id=1, source_target_pairs={{0,12},{4,8},{8,4},{12,0},{16,28},{20,24},{24,20},{28,16},{1,13},{... | collective-permute-start | bytes 393224 | tf_op jit(solution)/shard_map/ppermute | solution.py:368
  86.1 9.5 %collective-permute-start.37 = (f32[8,32,128]{2,1,0:T(8,128)S(1)}, f32[8,32,128]{2,1,0:T(8,128)S(1)}, u32[]{:S(2)}, u32[]{:S(2)}) collective-permute-start(f32[8,32,128]{2,1,0:T(8,128)S(1)} %add.124.refs_0_), channel_id=1, source_target_pairs={{0,16},{4,20},{8,24},{12,28},{16,0},{20,4},{24,8},{28,12},{1,17},{... | collective-permute-start | bytes 393224 | tf_op jit(solution)/shard_map/ppermute | solution.py:368
  93.2 9.1 %collective-permute-start.44 = (f32[8,32,128]{2,1,0:T(8,128)S(1)}, f32[8,32,128]{2,1,0:T(8,128)S(1)}, u32[]{:S(2)}, u32[]{:S(2)}) collective-permute-start(f32[8,32,128]{2,1,0:T(8,128)S(1)} %add.126.refs_0_), channel_id=1, source_target_pairs={{0,16},{4,20},{8,24},{12,28},{16,0},{20,4},{24,8},{28,12},{1,17},{... | collective-permute-start | bytes 393224 | tf_op jit(solution)/shard_map/ppermute | solution.py:368
  97.1 8.7 %collective-permute-start.39 = (f32[8,32,128]{2,1,0:T(8,128)S(1)}, f32[8,32,128]{2,1,0:T(8,128)S(1)}, u32[]{:S(2)}, u32[]{:S(2)}) collective-permute-start(f32[8,32,128]{2,1,0:T(8,128)S(1)} %add.125.refs_0_), channel_id=1, source_target_pairs={{0,8},{4,12},{8,0},{12,4},{16,24},{20,28},{24,16},{28,20},{1,9},{5... | collective-permute-start | bytes 393224 | tf_op jit(solution)/shard_map/ppermute | solution.py:368
  98.3 10.0 %collective-permute-start.40 = (f32[8,32,128]{2,1,0:T(8,128)S(1)}, f32[8,32,128]{2,1,0:T(8,128)S(1)}, u32[]{:S(2)}, u32[]{:S(2)}) collective-permute-start(f32[8,32,128]{2,1,0:T(8,128)S(1)} %add.125.refs_0_), channel_id=1, source_target_pairs={{0,12},{4,8},{8,4},{12,0},{16,28},{20,24},{24,20},{28,16},{1,13},{... | collective-permute-start | bytes 393224 | tf_op jit(solution)/shard_map/ppermute | solution.py:368
  104.2 8.7 %collective-permute-start.48 = (f32[8,32,128]{2,1,0:T(8,128)S(1)}, f32[8,32,128]{2,1,0:T(8,128)S(1)}, u32[]{:S(2)}, u32[]{:S(2)}) collective-permute-start(f32[8,32,128]{2,1,0:T(8,128)S(1)} %add.127.refs_0_), channel_id=1, source_target_pairs={{0,12},{4,8},{8,4},{12,0},{16,28},{20,24},{24,20},{28,16},{1,13},{... | collective-permute-start | bytes 393224 | tf_op jit(solution)/shard_map/ppermute | solution.py:368
  122.2 8.4 %collective-permute-start.56 = (f32[8,32,128]{2,1,0:T(8,128)S(1)}, f32[8,32,128]{2,1,0:T(8,128)S(1)}, u32[]{:S(2)}, u32[]{:S(2)}) collective-permute-start(f32[8,32,128]{2,1,0:T(8,128)S(1)} %get-tuple-element.139), channel_id=1, source_target_pairs={{0,4},{4,0},{8,12},{12,8},{16,20},{20,16},{24,28},{28,24},{1,5},{5... | collective-permute-start | bytes 393224 | tf_op jit(solution)/shard_map/ppermute | solution.py:368
  123.4 10.8 %collective-permute-start.58 = (f32[8,32,128]{2,1,0:T(8,128)S(1)}, f32[8,32,128]{2,1,0:T(8,128)S(1)}, u32[]{:S(2)}, u32[]{:S(2)}) collective-permute-start(f32[8,32,128]{2,1,0:T(8,128)S(1)} %get-tuple-element.141), channel_id=1, source_target_pairs={{0,12},{4,8},{8,4},{12,0},{16,28},{20,24},{24,20},{28,16},{1,13},{... | collective-permute-start | bytes 393224 | tf_op jit(solution)/shard_map/ppermute | solution.py:368
  125.8 8.5 %collective-permute-start.53 = (f32[8,32,128]{2,1,0:T(8,128)S(1)}, f32[8,32,128]{2,1,0:T(8,128)S(1)}, u32[]{:S(2)}, u32[]{:S(2)}) collective-permute-start(f32[8,32,128]{2,1,0:T(8,128)S(1)} %add.128.refs_0_), channel_id=1, source_target_pairs={{0,16},{4,20},{8,24},{12,28},{16,0},{20,4},{24,8},{28,12},{1,17},{... | collective-permute-start | bytes 393224 | tf_op jit(solution)/shard_map/ppermute | solution.py:368
  134.3 9.5 %collective-permute-start.59 = (f32[8,32,128]{2,1,0:T(8,128)S(1)}, f32[8,32,128]{2,1,0:T(8,128)S(1)}, u32[]{:S(2)}, u32[]{:S(2)}) collective-permute-start(f32[8,32,128]{2,1,0:T(8,128)S(1)} %add.129.refs_4_), channel_id=1, source_target_pairs={{0,16},{4,20},{8,24},{12,28},{16,0},{20,4},{24,8},{28,12},{1,17},{... | collective-permute-start | bytes 393224 | tf_op jit(solution)/shard_map/ppermute | solution.py:368
  (43 other events, 259.2 us)

commit v7 on v6

--- a/solution.py
+++ b/solution.py
@@ -438,7 +438,7 @@
         for c in range(CHAINS):
             mine = sums[c]
             other = over_blk(mine, quad_count)
-            arrived = after(other, pieces[c - 1][1]) if c else other
+            arrived = after(other, pieces[c - 1][1]) if c and index == 1 else other
             totals.append(add_all([mine, arrived], inverse))
             pieces.append(spread(totals[c]))
         for c in range(CHAINS):
@@ -454,6 +454,7 @@
             states[c].append(state)
 
     sums = [gather_sum(parts[c]) for c in range(CHAINS)]
+    sums[1] = after(sums[1], sums[0])
     groups = [
         [sums[c], over_blk(sums[c], quad_count), states[c][-1], states[c][-2]]
         for c in range(CHAINS)

time: 158 us -> 157 us (level)
  transfers between devices with their start and end apart: 66 -> 66, of which waited for: 31 -> 33; matrix products, arithmetic and copies ran while one was open for 1% -> 1% of each run, Pallas kernels for 11% -> 11%
where the time goes in v7:
time: 157 us
  starting transfers between devices  69.9 us (45%)
  waiting for transfers between devices  63.3 us (40%)
  Pallas kernels  20.8 us (13%)
    ppermute x48, starting transfers between devices, over_blk(): return lax.ppermute(x, 'blk', [(i, i ^ k) for i in range(blk_count)])  59.4 us
    ppermute x48, waiting for transfers between devices, over_blk(): return lax.ppermute(x, 'blk', [(i, i ^ k) for i in range(blk_count)])  57.9 us
    pallas_call x29, Pallas kernels, call(): pl.pallas_call(kernel, in_specs=in_specs or [VMEM] * len(operands), out_s...  20.8 us
    ppermute x6, starting transfers between devices, over_all(): return lax.ppermute(x, ('blk', 'rows'), pairs)  5.49 us
    ppermute x6, waiting for transfers between devices, over_all(): return lax.ppermute(x, ('blk', 'rows'), pairs)  5.43 us
    ppermute x6, starting transfers between devices, with_far(): return lax.ppermute(x, 'rows', pairs + [(b, a) for a, b in pairs])  4.18 us
  transfers between devices with their start and end apart: 66, of which 33 were waited for; matrix products, arithmetic and copies ran while one was open for 1% of the time, Pallas kernels for 11%

profile of v7, /device:TPU:0, one launch (start us, length us, event | category | flops | bytes accessed | tf_op | source)
XLA Modules:
  0.0 157.0 jit_solution(3662117632769454045)
XLA Ops:
  0.9 4.1 %collective-permute-start.1 = (f32[4,32,128]{2,1,0:T(8,128)S(1)}, f32[4,32,128]{2,1,0:T(8,128)S(1)}, u32[]{:S(2)}, u32[]{:S(2)}) collective-permute-start(f32[4,32,128]{2,1,0:T(8,128)S(1)} %get-tuple-element.146.chain_ref), channel_id=1, source_target_pairs={{0,16},{4,20},{8,24},{12,28},{16,0},{20,4},{24,8},{28,12},{1,17},{... | collective-permute-start | bytes 196616 | tf_op jit(solution)/shard_map/ppermute | solution.py:368
  6.7 3.5 %prepare.1 = (bf16[64,128,256]{2,1,0:T(8,128)(2,1)S(1)}, f32[32,128]{1,0:T(8,128)S(1)}) custom-call(s32[129]{0:T(256)S(1)} %pad_add_fusion.table_ref.table_hbm, f32[64,128,128]{2,1,0:T(8,128)} %vals_hbm), custom_call_target="tpu_custom_call" | custom-call | flops 2000000000 | bytes 8388608 | tf_op jit(solution)/shard_map/prepare/pallas_call | solution.py:26
  14.3 2.8 %collective-permute-start = (f32[32,128]{1,0:T(8,128)S(1)}, f32[32,128]{1,0:T(8,128)S(1)}, u32[]{:S(2)}, u32[]{:S(2)}) collective-permute-start(f32[32,128]{1,0:T(8,128)S(1)} %get-tuple-element.78), channel_id=1, source_target_pairs={{0,16},{4,20},{8,24},{12,28},{16,0},{20,4},{24,8},{28,12},{1,17},{... | collective-permute-start | bytes 49160 | tf_op jit(solution)/shard_map/ppermute | solution.py:368
  19.1 2.9 %collective-permute-start.9 = (f32[8,32,128]{2,1,0:T(8,128)S(1)}, f32[8,32,128]{2,1,0:T(8,128)S(1)}, u32[]{:S(2)}, u32[]{:S(2)}) collective-permute-start(f32[8,32,128]{2,1,0:T(8,128)S(1)} %join.2.refs_0_), channel_id=1, source_target_pairs={{0,8},{4,12},{8,0},{12,4},{16,24},{20,28},{24,16},{28,20},{1,9},{5... | collective-permute-start | bytes 393224 | tf_op jit(solution)/shard_map/ppermute | solution.py:368
  29.0 2.9 %collective-permute-done.16.refs_3_ = f32[8,32,128]{2,1,0:T(8,128)S(1)} collective-permute-done((f32[8,32,128]{2,1,0:T(8,128)S(1)}, f32[8,32,128]{2,1,0:T(8,128)S(1)}, u32[]{:S(2)}, u32[]{:S(2)}) %collective-permute-start.16) | collective-permute-done | bytes 131104 | tf_op jit(solution)/shard_map/ppermute | solution.py:368
  32.7 2.2 %products.6 = (f32[48,32,128]{2,1,0:T(8,128)S(1)}, f32[8,32,128]{2,1,0:T(8,128)S(1)}, f32[8,32,128]{2,1,0:T(8,128)S(1)}, f32[8,32,128]{2,1,0:T(8,128)S(1)}, f32[8,32,128]{2,1,0:T(8,128)S(1)}) custom-call(s32[129]{0:T(256)S(1)} %pad_add_fusion.table_ref.table_hbm, f32[8,32,128]{2,1,0:T(8,128)S(1)} %join.2.refs_0_, ...), custom_call_target="tpu_custom_call" | custom-call | flops 3000000000 | bytes 4194304 | tf_op jit(solution)/shard_map/products/pallas_call | solution.py:26
  38.5 2.2 %products.7 = (f32[48,32,128]{2,1,0:T(8,128)S(1)}, f32[8,32,128]{2,1,0:T(8,128)S(1)}, f32[8,32,128]{2,1,0:T(8,128)S(1)}, f32[8,32,128]{2,1,0:T(8,128)S(1)}, f32[8,32,128]{2,1,0:T(8,128)S(1)}) custom-call(s32[129]{0:T(256)S(1)} %pad_add_fusion.table_ref.table_hbm, f32[8,32,128]{2,1,0:T(8,128)S(1)} %join.3.refs_0_, ...), custom_call_target="tpu_custom_call" | custom-call | flops 3000000000 | bytes 4194304 | tf_op jit(solution)/shard_map/products/pallas_call | solution.py:26
  46.4 2.6 %collective-permute-done.23.refs_1_ = f32[8,32,128]{2,1,0:T(8,128)S(1)} collective-permute-done((f32[8,32,128]{2,1,0:T(8,128)S(1)}, f32[8,32,128]{2,1,0:T(8,128)S(1)}, u32[]{:S(2)}, u32[]{:S(2)}) %collective-permute-start.23) | collective-permute-done | bytes 131104 | tf_op jit(solution)/shard_map/ppermute | solution.py:368
  49.0 4.4 %collective-permute-done.25.refs_3_ = f32[8,32,128]{2,1,0:T(8,128)S(1)} collective-permute-done((f32[8,32,128]{2,1,0:T(8,128)S(1)}, f32[8,32,128]{2,1,0:T(8,128)S(1)}, u32[]{:S(2)}, u32[]{:S(2)}) %collective-permute-start.25) | collective-permute-done | bytes 131104 | tf_op jit(solution)/shard_map/ppermute | solution.py:368
  58.5 4.0 %collective-permute-done.26.refs_1_ = f32[8,32,128]{2,1,0:T(8,128)S(1)} collective-permute-done((f32[8,32,128]{2,1,0:T(8,128)S(1)}, f32[8,32,128]{2,1,0:T(8,128)S(1)}, u32[]{:S(2)}, u32[]{:S(2)}) %collective-permute-start.26) | collective-permute-done | bytes 131104 | tf_op jit(solution)/shard_map/ppermute | solution.py:368
  63.5 2.6 %collective-permute-start.30 = (f32[8,32,128]{2,1,0:T(8,128)S(1)}, f32[8,32,128]{2,1,0:T(8,128)S(1)}, u32[]{:S(2)}, u32[]{:S(2)}) collective-permute-start(f32[8,32,128]{2,1,0:T(8,128)S(1)} %add.123.refs_0_), channel_id=1, source_target_pairs={{0,12},{4,8},{8,4},{12,0},{16,28},{20,24},{24,20},{28,16},{1,13},{... | collective-permute-start | bytes 393224 | tf_op jit(solution)/shard_map/ppermute | solution.py:368
  73.5 2.2 %products.8 = (f32[48,32,128]{2,1,0:T(8,128)S(1)}, f32[8,32,128]{2,1,0:T(8,128)S(1)}, f32[8,32,128]{2,1,0:T(8,128)S(1)}, f32[8,32,128]{2,1,0:T(8,128)S(1)}, f32[8,32,128]{2,1,0:T(8,128)S(1)}) custom-call(s32[129]{0:T(256)S(1)} %pad_add_fusion.table_ref.table_hbm, f32[8,32,128]{2,1,0:T(8,128)S(1)} %add.121.refs_0_, ...), custom_call_target="tpu_custom_call" | custom-call | flops 3000000000 | bytes 4194304 | tf_op jit(solution)/shard_map/products/pallas_call | solution.py:26
  86.8 2.6 %collective-permute-done.41.refs_1_ = f32[8,32,128]{2,1,0:T(8,128)S(1)} collective-permute-done((f32[8,32,128]{2,1,0:T(8,128)S(1)}, f32[8,32,128]{2,1,0:T(8,128)S(1)}, u32[]{:S(2)}, u32[]{:S(2)}) %collective-permute-start.41) | collective-permute-done | bytes 131104 | tf_op jit(solution)/shard_map/ppermute | solution.py:368
  89.5 3.6 %collective-permute-done.43.refs_3_ = f32[8,32,128]{2,1,0:T(8,128)S(1)} collective-permute-done((f32[8,32,128]{2,1,0:T(8,128)S(1)}, f32[8,32,128]{2,1,0:T(8,128)S(1)}, u32[]{:S(2)}, u32[]{:S(2)}) %collective-permute-start.43) | collective-permute-done | bytes 131104 | tf_op jit(solution)/shard_map/ppermute | solution.py:368
  99.1 3.2 %collective-permute-done.44.refs_1_ = f32[8,32,128]{2,1,0:T(8,128)S(1)} collective-permute-done((f32[8,32,128]{2,1,0:T(8,128)S(1)}, f32[8,32,128]{2,1,0:T(8,128)S(1)}, u32[]{:S(2)}, u32[]{:S(2)}) %collective-permute-start.44) | collective-permute-done | bytes 131104 | tf_op jit(solution)/shard_map/ppermute | solution.py:368
  105.9 2.4 %collective-permute-done.40.refs_3_ = f32[8,32,128]{2,1,0:T(8,128)S(1)} collective-permute-done((f32[8,32,128]{2,1,0:T(8,128)S(1)}, f32[8,32,128]{2,1,0:T(8,128)S(1)}, u32[]{:S(2)}, u32[]{:S(2)}) %collective-permute-start.40) | collective-permute-done | bytes 131104 | tf_op jit(solution)/shard_map/ppermute | solution.py:368
  114.3 2.2 %products.10 = (f32[48,32,128]{2,1,0:T(8,128)S(1)}, f32[8,32,128]{2,1,0:T(8,128)S(1)}, f32[8,32,128]{2,1,0:T(8,128)S(1)}, f32[8,32,128]{2,1,0:T(8,128)S(1)}, f32[8,32,128]{2,1,0:T(8,128)S(1)}) custom-call(s32[129]{0:T(256)S(1)} %pad_add_fusion.table_ref.table_hbm, f32[8,32,128]{2,1,0:T(8,128)S(1)} %add.125.refs_0_, ...), custom_call_target="tpu_custom_call" | custom-call | flops 3000000000 | bytes 4194304 | tf_op jit(solution)/shard_map/products/pallas_call | solution.py:26
  117.6 2.5 %collective-permute-start.52 = (f32[8,32,128]{2,1,0:T(8,128)S(1)}, f32[8,32,128]{2,1,0:T(8,128)S(1)}, u32[]{:S(2)}, u32[]{:S(2)}) collective-permute-start(f32[8,32,128]{2,1,0:T(8,128)S(1)} %get-tuple-element.132), channel_id=1, source_target_pairs={{0,12},{4,8},{8,4},{12,0},{16,28},{20,24},{24,20},{28,16},{1,13},{... | collective-permute-start | bytes 393224 | tf_op jit(solution)/shard_map/ppermute | solution.py:368
  123.4 2.5 %collective-permute-start.58 = (f32[8,32,128]{2,1,0:T(8,128)S(1)}, f32[8,32,128]{2,1,0:T(8,128)S(1)}, u32[]{:S(2)}, u32[]{:S(2)}) collective-permute-start(f32[8,32,128]{2,1,0:T(8,128)S(1)} %get-tuple-element.140), channel_id=1, source_target_pairs={{0,12},{4,8},{8,4},{12,0},{16,28},{20,24},{24,20},{28,16},{1,13},{... | collective-permute-start | bytes 393224 | tf_op jit(solution)/shard_map/ppermute | solution.py:368
  127.7 2.5 %collective-permute-done.56.refs_1_ = f32[8,32,128]{2,1,0:T(8,128)S(1)} collective-permute-done((f32[8,32,128]{2,1,0:T(8,128)S(1)}, f32[8,32,128]{2,1,0:T(8,128)S(1)}, u32[]{:S(2)}, u32[]{:S(2)}) %collective-permute-start.56) | collective-permute-done | bytes 131104 | tf_op jit(solution)/shard_map/ppermute | solution.py:368
  130.3 4.5 %collective-permute-done.58.refs_3_ = f32[8,32,128]{2,1,0:T(8,128)S(1)} collective-permute-done((f32[8,32,128]{2,1,0:T(8,128)S(1)}, f32[8,32,128]{2,1,0:T(8,128)S(1)}, u32[]{:S(2)}, u32[]{:S(2)}) %collective-permute-start.58) | collective-permute-done | bytes 131104 | tf_op jit(solution)/shard_map/ppermute | solution.py:368
  136.4 6.2 %collective-permute-done.59.refs_5_ = f32[8,32,128]{2,1,0:T(8,128)S(1)} collective-permute-done((f32[8,32,128]{2,1,0:T(8,128)S(1)}, f32[8,32,128]{2,1,0:T(8,128)S(1)}, u32[]{:S(2)}, u32[]{:S(2)}) %collective-permute-start.59) | collective-permute-done | bytes 131104 | tf_op jit(solution)/shard_map/ppermute | solution.py:368
  145.2 2.5 %collective-permute-done.61 = f32[64,64]{1,0:T(8,128)S(1)} collective-permute-done((f32[64,64]{1,0:T(8,128)S(1)}, f32[64,64]{1,0:T(8,128)S(1)}, u32[]{:S(2)}, u32[]{:S(2)}) %collective-permute-start.61) | collective-permute-done | bytes 16416 | tf_op jit(solution)/shard_map/ppermute | solution.py:379
  154.2 2.8 %solve.1 = f32[64,512]{1,0:T(8,128)} custom-call(f32[64,64]{1,0:T(8,128)S(1)} %add_add_fusion.refs_0_, f32[64,64]{1,0:T(8,128)S(1)} %collective-permute-done.63.refs_1_, f32[64,64]{1,0:T(8,128)S(1)} %collective-permute-done.64.refs_2_, f32[64,64]{1,0:T(8,128)S(1)} %collective-permute-done.65.refs_3_, f32[4,64,128]{2,1,0:T(8,128)S(1)} %get-tuple-element.144.refs_4_), custom_call_target="tpu_custom_call" | custom-call | tf_op jit(solution)/shard_map/solve/pallas_call | solution.py:26
  (146 shorter events, 82.1 us)
Async XLA Ops:
  0.9 9.3 %collective-permute-start.1 = (f32[4,32,128]{2,1,0:T(8,128)S(1)}, f32[4,32,128]{2,1,0:T(8,128)S(1)}, u32[]{:S(2)}, u32[]{:S(2)}) collective-permute-start(f32[4,32,128]{2,1,0:T(8,128)S(1)} %get-tuple-element.146.chain_ref), channel_id=1, source_target_pairs={{0,16},{4,20},{8,24},{12,28},{16,0},{20,4},{24,8},{28,12},{1,17},{... | collective-permute-start | bytes 196616 | tf_op jit(solution)/shard_map/ppermute | solution.py:368
  10.3 11.8 %collective-permute-start.2 = (f32[8,32,128]{2,1,0:T(8,128)S(1)}, f32[8,32,128]{2,1,0:T(8,128)S(1)}, u32[]{:S(2)}, u32[]{:S(2)}) collective-permute-start(f32[8,32,128]{2,1,0:T(8,128)S(1)} %join.2.refs_0_), channel_id=1, source_target_pairs={{0,4},{4,0},{8,12},{12,8},{16,20},{20,16},{24,28},{28,24},{1,5},{5... | collective-permute-start | bytes 393224 | tf_op jit(solution)/shard_map/ppermute | solution.py:368
  12.1 9.9 %collective-permute-start.4 = (f32[8,32,128]{2,1,0:T(8,128)S(1)}, f32[8,32,128]{2,1,0:T(8,128)S(1)}, u32[]{:S(2)}, u32[]{:S(2)}) collective-permute-start(f32[8,32,128]{2,1,0:T(8,128)S(1)} %join.3.refs_0_), channel_id=1, source_target_pairs={{0,4},{4,0},{8,12},{12,8},{16,20},{20,16},{24,28},{28,24},{1,5},{5... | collective-permute-start | bytes 393224 | tf_op jit(solution)/shard_map/ppermute | solution.py:368
  13.3 8.8 %collective-permute-start.5 = (f32[8,32,128]{2,1,0:T(8,128)S(1)}, f32[8,32,128]{2,1,0:T(8,128)S(1)}, u32[]{:S(2)}, u32[]{:S(2)}) collective-permute-start(f32[8,32,128]{2,1,0:T(8,128)S(1)} %join.3.refs_0_), channel_id=1, source_target_pairs={{0,8},{4,12},{8,0},{12,4},{16,24},{20,28},{24,16},{28,20},{1,9},{5... | collective-permute-start | bytes 393224 | tf_op jit(solution)/shard_map/ppermute | solution.py:368
  17.1 11.1 %collective-permute-start.10 = (f32[8,32,128]{2,1,0:T(8,128)S(1)}, f32[8,32,128]{2,1,0:T(8,128)S(1)}, u32[]{:S(2)}, u32[]{:S(2)}) collective-permute-start(f32[8,32,128]{2,1,0:T(8,128)S(1)} %join.2.refs_0_), channel_id=1, source_target_pairs={{0,12},{4,8},{8,4},{12,0},{16,28},{20,24},{24,20},{28,16},{1,13},{... | collective-permute-start | bytes 393224 | tf_op jit(solution)/shard_map/ppermute | solution.py:368
  19.1 9.0 %collective-permute-start.9 = (f32[8,32,128]{2,1,0:T(8,128)S(1)}, f32[8,32,128]{2,1,0:T(8,128)S(1)}, u32[]{:S(2)}, u32[]{:S(2)}) collective-permute-start(f32[8,32,128]{2,1,0:T(8,128)S(1)} %join.2.refs_0_), channel_id=1, source_target_pairs={{0,8},{4,12},{8,0},{12,4},{16,24},{20,28},{24,16},{28,20},{1,9},{5... | collective-permute-start | bytes 393224 | tf_op jit(solution)/shard_map/ppermute | solution.py:368
  34.9 8.6 %collective-permute-start.13 = (f32[8,32,128]{2,1,0:T(8,128)S(1)}, f32[8,32,128]{2,1,0:T(8,128)S(1)}, u32[]{:S(2)}, u32[]{:S(2)}) collective-permute-start(f32[8,32,128]{2,1,0:T(8,128)S(1)} %get-tuple-element.87), channel_id=1, source_target_pairs={{0,4},{4,0},{8,12},{12,8},{16,20},{20,16},{24,28},{28,24},{1,5},{5... | collective-permute-start | bytes 393224 | tf_op jit(solution)/shard_map/ppermute | solution.py:368
  43.5 10.0 %collective-permute-start.25 = (f32[8,32,128]{2,1,0:T(8,128)S(1)}, f32[8,32,128]{2,1,0:T(8,128)S(1)}, u32[]{:S(2)}, u32[]{:S(2)}) collective-permute-start(f32[8,32,128]{2,1,0:T(8,128)S(1)} %get-tuple-element.99), channel_id=1, source_target_pairs={{0,12},{4,8},{8,4},{12,0},{16,28},{20,24},{24,20},{28,16},{1,13},{... | collective-permute-start | bytes 393224 | tf_op jit(solution)/shard_map/ppermute | solution.py:368
  45.0 10.0 %collective-permute-start.19 = (f32[8,32,128]{2,1,0:T(8,128)S(1)}, f32[8,32,128]{2,1,0:T(8,128)S(1)}, u32[]{:S(2)}, u32[]{:S(2)}) collective-permute-start(f32[8,32,128]{2,1,0:T(8,128)S(1)} %add.120.refs_0_), channel_id=1, source_target_pairs={{0,16},{4,20},{8,24},{12,28},{16,0},{20,4},{24,8},{28,12},{1,17},{... | collective-permute-start | bytes 393224 | tf_op jit(solution)/shard_map/ppermute | solution.py:368
  53.5 9.1 %collective-permute-start.26 = (f32[8,32,128]{2,1,0:T(8,128)S(1)}, f32[8,32,128]{2,1,0:T(8,128)S(1)}, u32[]{:S(2)}, u32[]{:S(2)}) collective-permute-start(f32[8,32,128]{2,1,0:T(8,128)S(1)} %add.122.refs_0_), channel_id=1, source_target_pairs={{0,16},{4,20},{8,24},{12,28},{16,0},{20,4},{24,8},{28,12},{1,17},{... | collective-permute-start | bytes 393224 | tf_op jit(solution)/shard_map/ppermute | solution.py:368
  56.4 9.7 %collective-permute-start.21 = (f32[8,32,128]{2,1,0:T(8,128)S(1)}, f32[8,32,128]{2,1,0:T(8,128)S(1)}, u32[]{:S(2)}, u32[]{:S(2)}) collective-permute-start(f32[8,32,128]{2,1,0:T(8,128)S(1)} %add.121.refs_0_), channel_id=1, source_target_pairs={{0,8},{4,12},{8,0},{12,4},{16,24},{20,28},{24,16},{28,20},{1,9},{5... | collective-permute-start | bytes 393224 | tf_op jit(solution)/shard_map/ppermute | solution.py:368
  57.0 10.5 %collective-permute-start.22 = (f32[8,32,128]{2,1,0:T(8,128)S(1)}, f32[8,32,128]{2,1,0:T(8,128)S(1)}, u32[]{:S(2)}, u32[]{:S(2)}) collective-permute-start(f32[8,32,128]{2,1,0:T(8,128)S(1)} %add.121.refs_0_), channel_id=1, source_target_pairs={{0,12},{4,8},{8,4},{12,0},{16,28},{20,24},{24,20},{28,16},{1,13},{... | collective-permute-start | bytes 393224 | tf_op jit(solution)/shard_map/ppermute | solution.py:368
  63.5 9.1 %collective-permute-start.30 = (f32[8,32,128]{2,1,0:T(8,128)S(1)}, f32[8,32,128]{2,1,0:T(8,128)S(1)}, u32[]{:S(2)}, u32[]{:S(2)}) collective-permute-start(f32[8,32,128]{2,1,0:T(8,128)S(1)} %add.123.refs_0_), channel_id=1, source_target_pairs={{0,12},{4,8},{8,4},{12,0},{16,28},{20,24},{24,20},{28,16},{1,13},{... | collective-permute-start | bytes 393224 | tf_op jit(solution)/shard_map/ppermute | solution.py:368
  77.3 8.8 %collective-permute-start.34 = (f32[8,32,128]{2,1,0:T(8,128)S(1)}, f32[8,32,128]{2,1,0:T(8,128)S(1)}, u32[]{:S(2)}, u32[]{:S(2)}) collective-permute-start(f32[8,32,128]{2,1,0:T(8,128)S(1)} %get-tuple-element.112), channel_id=1, source_target_pairs={{0,12},{4,8},{8,4},{12,0},{16,28},{20,24},{24,20},{28,16},{1,13},{... | collective-permute-start | bytes 393224 | tf_op jit(solution)/shard_map/ppermute | solution.py:368
  83.1 10.1 %collective-permute-start.43 = (f32[8,32,128]{2,1,0:T(8,128)S(1)}, f32[8,32,128]{2,1,0:T(8,128)S(1)}, u32[]{:S(2)}, u32[]{:S(2)}) collective-permute-start(f32[8,32,128]{2,1,0:T(8,128)S(1)} %get-tuple-element.120), channel_id=1, source_target_pairs={{0,12},{4,8},{8,4},{12,0},{16,28},{20,24},{24,20},{28,16},{1,13},{... | collective-permute-start | bytes 393224 | tf_op jit(solution)/shard_map/ppermute | solution.py:368
  86.1 9.5 %collective-permute-start.37 = (f32[8,32,128]{2,1,0:T(8,128)S(1)}, f32[8,32,128]{2,1,0:T(8,128)S(1)}, u32[]{:S(2)}, u32[]{:S(2)}) collective-permute-start(f32[8,32,128]{2,1,0:T(8,128)S(1)} %add.124.refs_0_), channel_id=1, source_target_pairs={{0,16},{4,20},{8,24},{12,28},{16,0},{20,4},{24,8},{28,12},{1,17},{... | collective-permute-start | bytes 393224 | tf_op jit(solution)/shard_map/ppermute | solution.py:368
  93.2 9.1 %collective-permute-start.44 = (f32[8,32,128]{2,1,0:T(8,128)S(1)}, f32[8,32,128]{2,1,0:T(8,128)S(1)}, u32[]{:S(2)}, u32[]{:S(2)}) collective-permute-start(f32[8,32,128]{2,1,0:T(8,128)S(1)} %add.126.refs_0_), channel_id=1, source_target_pairs={{0,16},{4,20},{8,24},{12,28},{16,0},{20,4},{24,8},{28,12},{1,17},{... | collective-permute-start | bytes 393224 | tf_op jit(solution)/shard_map/ppermute | solution.py:368
  95.6 8.6 %collective-permute-start.38 = (f32[8,32,128]{2,1,0:T(8,128)S(1)}, f32[8,32,128]{2,1,0:T(8,128)S(1)}, u32[]{:S(2)}, u32[]{:S(2)}) collective-permute-start(f32[8,32,128]{2,1,0:T(8,128)S(1)} %add.125.refs_0_), channel_id=1, source_target_pairs={{0,4},{4,0},{8,12},{12,8},{16,20},{20,16},{24,28},{28,24},{1,5},{5... | collective-permute-start | bytes 393224 | tf_op jit(solution)/shard_map/ppermute | solution.py:368
  97.1 8.7 %collective-permute-start.39 = (f32[8,32,128]{2,1,0:T(8,128)S(1)}, f32[8,32,128]{2,1,0:T(8,128)S(1)}, u32[]{:S(2)}, u32[]{:S(2)}) collective-permute-start(f32[8,32,128]{2,1,0:T(8,128)S(1)} %add.125.refs_0_), channel_id=1, source_target_pairs={{0,8},{4,12},{8,0},{12,4},{16,24},{20,28},{24,16},{28,20},{1,9},{5... | collective-permute-start | bytes 393224 | tf_op jit(solution)/shard_map/ppermute | solution.py:368
  98.3 10.0 %collective-permute-start.40 = (f32[8,32,128]{2,1,0:T(8,128)S(1)}, f32[8,32,128]{2,1,0:T(8,128)S(1)}, u32[]{:S(2)}, u32[]{:S(2)}) collective-permute-start(f32[8,32,128]{2,1,0:T(8,128)S(1)} %add.125.refs_0_), channel_id=1, source_target_pairs={{0,12},{4,8},{8,4},{12,0},{16,28},{20,24},{24,20},{28,16},{1,13},{... | collective-permute-start | bytes 393224 | tf_op jit(solution)/shard_map/ppermute | solution.py:368
  104.2 8.7 %collective-permute-start.48 = (f32[8,32,128]{2,1,0:T(8,128)S(1)}, f32[8,32,128]{2,1,0:T(8,128)S(1)}, u32[]{:S(2)}, u32[]{:S(2)}) collective-permute-start(f32[8,32,128]{2,1,0:T(8,128)S(1)} %add.127.refs_0_), channel_id=1, source_target_pairs={{0,12},{4,8},{8,4},{12,0},{16,28},{20,24},{24,20},{28,16},{1,13},{... | collective-permute-start | bytes 393224 | tf_op jit(solution)/shard_map/ppermute | solution.py:368
  117.6 9.1 %collective-permute-start.52 = (f32[8,32,128]{2,1,0:T(8,128)S(1)}, f32[8,32,128]{2,1,0:T(8,128)S(1)}, u32[]{:S(2)}, u32[]{:S(2)}) collective-permute-start(f32[8,32,128]{2,1,0:T(8,128)S(1)} %get-tuple-element.132), channel_id=1, source_target_pairs={{0,12},{4,8},{8,4},{12,0},{16,28},{20,24},{24,20},{28,16},{1,13},{... | collective-permute-start | bytes 393224 | tf_op jit(solution)/shard_map/ppermute | solution.py:368
  123.4 11.4 %collective-permute-start.58 = (f32[8,32,128]{2,1,0:T(8,128)S(1)}, f32[8,32,128]{2,1,0:T(8,128)S(1)}, u32[]{:S(2)}, u32[]{:S(2)}) collective-permute-start(f32[8,32,128]{2,1,0:T(8,128)S(1)} %get-tuple-element.140), channel_id=1, source_target_pairs={{0,12},{4,8},{8,4},{12,0},{16,28},{20,24},{24,20},{28,16},{1,13},{... | collective-permute-start | bytes 393224 | tf_op jit(solution)/shard_map/ppermute | solution.py:368
  126.7 9.7 %collective-permute-start.53 = (f32[8,32,128]{2,1,0:T(8,128)S(1)}, f32[8,32,128]{2,1,0:T(8,128)S(1)}, u32[]{:S(2)}, u32[]{:S(2)}) collective-permute-start(f32[8,32,128]{2,1,0:T(8,128)S(1)} %add.128.refs_0_), channel_id=1, source_target_pairs={{0,16},{4,20},{8,24},{12,28},{16,0},{20,4},{24,8},{28,12},{1,17},{... | collective-permute-start | bytes 393224 | tf_op jit(solution)/shard_map/ppermute | solution.py:368
  (43 other events, 260.0 us)
